TPU v7x, 32 devices: a whole 2x2x4 slice. The times are simulated.
32 devices in a mesh: groups: 2 (over y), seq: 4 (over z), heads: 2 (over x), sub: 2 (over core).
Axes of the slice: x: 2, y: 2, z: 4, core: 2. Of those that a mesh axis runs over, the one named last changes fastest.
Arguments:
- queries: bfloat16 [8192, 1024], P(('groups', 'seq', 'heads'), 'sub'), parts along dimension 0, may hold values from -6 to 6
- keys: bfloat16 [8192, 1024], P(('groups', 'seq', 'heads'), 'sub'), parts along dimension 0, may hold values from -6 to 6
- values: bfloat16 [8192, 1024], P(('groups', 'seq', 'heads'), 'sub'), parts along dimension 0, may hold values from -6 to 6
- out_grad: bfloat16 [8192, 1024], P(('groups', 'seq', 'heads'), 'sub'), parts along dimension 0, may hold values from -6 to 6
- level_weights: float32 [8, 8, 8192], P('sub', None, ('groups', 'seq', 'heads')), parts along dimension 2, may hold values from 0.25 to 2
Outputs:
- grad_queries: bfloat16 [8192, 1024], P(('groups', 'seq', 'heads'), 'sub'), parts along dimension 0
- grad_keys: bfloat16 [8192, 1024], P(('groups', 'seq', 'heads'), 'sub'), parts along dimension 0
- grad_values: bfloat16 [8192, 1024], P(('groups', 'seq', 'heads'), 'sub'), parts along dimension 0
- weight_grads: float32 [8, 8, 8192], P('sub', None, ('groups', 'seq', 'heads')), parts along dimension 2
There are 2 independent parts, one for each index of `groups`. A program takes and returns all parts, laid end to end along the dimension named above; each array names one. Nothing has to cross between parts.
All inputs are finite; a program needn't handle non-finite values.
Results may differ from a plain program's by a relative error of at most 0.0056.
Values may be sent and summed in bfloat16 or wider, within the bound.
No kernel may reach another device: no remote copies, remote signals or barrier semaphores. Data moves between devices by JAX's collectives and lax.ppermute only.
A program may use at most 64 MiB of HBM per device.

v0:
```python
import math

import jax
import jax.numpy as jnp
from jax import lax
from jax.sharding import PartitionSpec as P


def passed_along(block, axis, distance):
    devices = range(lax.axis_size(axis))
    route = [(i - distance, i) for i in devices if i - distance in devices]
    return lax.ppermute(block, axis, route)


def from_partner(shard, axis, apart):
    return lax.ppermute(shard, axis, [(i, i ^ 1 << apart) for i in range(lax.axis_size(axis))])


def top_state_move(block_sum, distance):
    return passed_along(block_sum.astype(jnp.bfloat16), ("seq", "heads"), distance)


def top_grad_move(pending, distance):
    return passed_along(pending, ("seq", "heads"), -distance)


def on_device(queries, keys, values, out_grad, level_weights):
    tok_rows = queries.shape[0]
    head_count = level_weights.shape[0]
    levels = level_weights.shape[1]
    head_width = queries.shape[1] // head_count
    shape_three = (tok_rows, head_count, head_width)
    queries_h = queries.reshape(shape_three)
    keys_h = keys.reshape(shape_three)
    values_h = values.reshape(shape_three)
    grads_h = out_grad.reshape(shape_three)
    bit_count = lax.axis_size(("seq", "heads")).bit_length() - 1
    position = lax.axis_index(("seq", "heads"))
    base_scale = 1.0 / math.sqrt(head_width * tok_rows)
    scales = [base_scale] + [
        base_scale / math.sqrt(2.0 ** (level_idx - 1)) for level_idx in range(1, levels)
    ]
    causal = jnp.tril(jnp.ones((tok_rows, tok_rows), dtype=bool))
    scores = jnp.einsum("thd,shd->hts", queries_h, keys_h, preferred_element_type=jnp.float32)
    grad_dots = jnp.einsum("thd,shd->hts", grads_h, values_h, preferred_element_type=jnp.float32)
    scores = jnp.where(causal, scores, 0.0)
    grad_dots = jnp.where(causal, grad_dots, 0.0)
    near_weight = scales[0] * jnp.sum(scores * grad_dots, axis=2)
    factor = scales[0] * level_weights[:, 0, :][:, :, None]
    grad_mix = (factor * grad_dots).astype(jnp.bfloat16)
    score_mix = (factor * scores).astype(jnp.bfloat16)
    grad_q = jnp.einsum("hts,shd->thd", grad_mix, keys_h, preferred_element_type=jnp.float32)
    near_k = jnp.einsum("hts,thd->shd", grad_mix, queries_h, preferred_element_type=jnp.float32)
    near_v = jnp.einsum("hts,thd->shd", score_mix, grads_h, preferred_element_type=jnp.float32)
    key_state = jnp.einsum("shd,she->hde", keys_h, values_h, preferred_element_type=jnp.float32)
    grad_list = []
    for level_idx in range(1, bit_count + 1):
        gate_now = level_weights[:, level_idx, :].T[:, :, None]
        scaled = (gate_now * queries_h).astype(jnp.bfloat16)
        grad_list.append(
            scales[level_idx]
            * jnp.einsum("thd,the->hde", scaled, grads_h, preferred_element_type=jnp.float32)
        )
    pending = jnp.stack(grad_list, axis=0)
    level_states = []
    reverse_sum = jnp.zeros_like(key_state)
    block_sum = key_state
    lower_bits = 0
    last_bit = bit_count - 1
    for bit_pos in range(lower_bits, last_bit):
        upper_half = position >> bit_pos & 1 == 1
        received = from_partner(block_sum, ("seq", "heads"), bit_pos)
        level_states.append(jnp.where(upper_half, received, 0.0))
        block_sum = block_sum + received
    for bit_pos in range(lower_bits, last_bit):
        upper_half = position >> bit_pos & 1 == 1
        received = from_partner(pending, ("seq", "heads"), bit_pos)
        reverse_sum = reverse_sum + jnp.where(upper_half, 0.0, received[0])
        pending = pending[1:] + received[1:]
    distance = lax.axis_size(("seq", "heads")) // 2
    top_state = top_state_move(block_sum, distance)
    level_states.append(top_state)
    top_grad = top_grad_move(pending, distance)
    reverse_sum = reverse_sum + top_grad[0]
    weight_rows = [near_weight]
    for level_idx in range(1, levels):
        if level_idx > bit_count:
            weight_rows.append(jnp.zeros_like(near_weight))
            continue
        state_low = level_states[level_idx - 1].astype(jnp.bfloat16)
        products = jnp.einsum(
            "the,hde->thd", grads_h, state_low, preferred_element_type=jnp.float32
        )
        gate_now = level_weights[:, level_idx, :].T[:, :, None]
        grad_q = grad_q + scales[level_idx] * gate_now * products
        weight_rows.append((scales[level_idx] * jnp.sum(products * queries_h, axis=2)).T)
    reverse_low = reverse_sum.astype(jnp.bfloat16)
    grad_k = near_k + jnp.einsum(
        "she,hde->shd", values_h, reverse_low, preferred_element_type=jnp.float32
    )
    grad_v = near_v + jnp.einsum(
        "shd,hde->she", keys_h, reverse_low, preferred_element_type=jnp.float32
    )
    flat = (tok_rows, head_count * head_width)
    weight_grads = jnp.stack(weight_rows, axis=1)
    return (
        grad_q.reshape(flat).astype(jnp.bfloat16),
        grad_k.reshape(flat).astype(jnp.bfloat16),
        grad_v.reshape(flat).astype(jnp.bfloat16),
        weight_grads,
    )


def solution(mesh):
    placed = (
        P(("groups", "seq", "heads"), "sub"),
        P(("groups", "seq", "heads"), "sub"),
        P(("groups", "seq", "heads"), "sub"),
        P(("groups", "seq", "heads"), "sub"),
        P("sub", None, ("groups", "seq", "heads")),
    )
    return jax.shard_map(
        on_device,
        mesh=mesh,
        in_specs=placed,
        out_specs=(
            P(("groups", "seq", "heads"), "sub"),
            P(("groups", "seq", "heads"), "sub"),
            P(("groups", "seq", "heads"), "sub"),
            P("sub", None, ("groups", "seq", "heads")),
        ),
        check_vma=False,
    )
```

profile of v0, /device:TPU:0, one launch (start us, length us, event | category | flops | bytes accessed | tf_op | source)
XLA Modules:
  0.0 67.4 jit_solution(12672516421317986934)
XLA Ops:
  0.6 1.0 %copy-done = bf16[512,512]{1,0:T(8,128)(2,1)S(1)} copy-done((bf16[512,512]{1,0:T(8,128)(2,1)S(1)}, bf16[512,512]{1,0:T(8,128)(2,1)}, u32[]{:S(2)}) %copy-start) | copy-done | bytes 524312
  1.7 2.1 %fusion.22 = f32[4,128,128]{2,1,0:T(8,128)} fusion(bf16[512,512]{1,0:T(8,128)(2,1)} %param.7, bf16[512,512]{1,0:T(8,128)(2,1)S(1)} %copy-done), kind=kOutput, calls=%fused_computation.41 | convolution fusion | flops 67108864 | bytes 1310720 | tf_op jit(solution)/shard_map/shd,she->hde/dot_general | solution.py:55
  3.8 2.9 %collective-permute-start = (f32[4,128,128]{2,1,0:T(8,128)}, f32[4,128,128]{2,1,0:T(8,128)}, u32[]{:S(2)}, u32[]{:S(2)}) collective-permute-start(f32[4,128,128]{2,1,0:T(8,128)} %fusion.22), channel_id=1, source_target_pairs={{0,2},{2,0},{4,6},{6,4},{8,10},{10,8},{12,14},{14,12},{1,3},{3,1},... | collective-permute-start | bytes 786440 | tf_op jit(solution)/shard_map/ppermute | solution.py:16
  6.7 1.3 %copy.73 = bf16[512,512]{0,1:T(8,128)(2,1)S(1)} copy(bf16[512,512]{1,0:T(8,128)(2,1)} %param.5) | data formatting | bytes 1048576 | tf_op args[0]
  8.0 1.3 %copy.101 = bf16[512,512]{0,1:T(8,128)(2,1)S(1)} copy(bf16[512,512]{1,0:T(8,128)(2,1)} %param.8) | data formatting | bytes 1048576 | tf_op jit(solution)/shard_map/reshape | solution.py:36
  9.2 1.0 %slice_multiply_fusion = (f32[4,1,512]{2,1,0:T(1,128)S(1)}, f32[4,1,512]{2,1,0:T(1,128)S(1)}, f32[4,1,512]{2,1,0:T(1,128)S(1)}, f32[4,1,512]{2,1,0:T(1,128)S(1)}) fusion(f32[4,8,512]{2,1,0:T(8,128)} %param.9), kind=kLoop, calls=%fused_computation.83 | loop fusion | flops 2048 | bytes 65536 | tf_op jit(solution)/shard_map/mul | solution.py:49
  11.2 1.0 %pad_maximum_fusion = f32[3,4,128,128]{3,2,1,0:T(8,128)} fusion(f32[1,4,128,128]{3,2,1,0:T(8,128)S(1)} %fusion.9, f32[1,4,128,128]{3,2,1,0:T(8,128)S(1)} %fusion.10, f32[1,4,128,128]{3,2,1,0:T(8,128)S(1)} %fusion.11), kind=kLoop, calls=%fused_computation.39 | loop fusion | flops 393216 | bytes 1572864 | tf_op jit(solution)/shard_map/stack | solution.py:64
  12.2 0.7 %fusion.24 = f32[4,512,512]{1,2,0:T(8,128)S(1)} fusion(bf16[512,4,128]{0,2,1:T(8,128)(2,1)S(1)} %bitcast.137, bf16[512,512]{1,0:T(8,128)(2,1)S(1)} %copy-done.4), kind=kOutput, calls=%fused_computation.43 | convolution fusion | flops 268435456 | bytes 5242880 | tf_op jit(solution)/shard_map/thd,shd->hts/dot_general | solution.py:45
  13.0 0.9 %multiply_reduce_fusion = (f32[4,512]{1,0:T(4,128)S(1)}, f32[4,512,512]{1,2,0:T(8,128)S(1)}) fusion(f32[4,512,512]{1,2,0:T(8,128)S(1)} %fusion.24, pred[512,512]{0,1:T(8,128)(4,1)S(1)} %iota_compare_fusion, bf16[512,4,128]{0,2,1:T(8,128)(2,1)S(1)} %bitcast.145, bf16[512,512]{1,0:T(8,128)(2,1)S(1)} %copy-done), kind=kOutput, calls=%fused_computation | convolution fusion | flops 272627712 | bytes 9707520 | tf_op jit(solution)/shard_map/thd,shd->hts/dot_general | solution.py:44
  14.0 0.9 %copy-done.1 = f32[4,512,512]{1,2,0:T(8,128)} copy-done((f32[4,512,512]{1,2,0:T(8,128)}, f32[4,512,512]{1,2,0:T(8,128)S(1)}, u32[]{:S(2)}) %copy-start.1) | copy-done | bytes 4194328
  14.9 1.9 %convolution_bitcast_fusion.1 = f32[512,4,128]{0,2,1:T(8,128)} fusion(bf16[512,4,128]{0,2,1:T(8,128)(2,1)S(1)} %bitcast.146, f32[4,512,512]{1,2,0:T(8,128)S(1)} %fusion.24, f32[4,512]{1,0:T(4,128)S(1)} %bitcast.150, pred[512,512]{0,1:T(8,128)(4,1)S(1)} %iota_compare_fusion), kind=kOutput, calls=%fused_computation.14 | convolution fusion | flops 271581184 | bytes 6037504 | tf_op jit(solution)/shard_map/hts,thd->shd/dot_general | solution.py:53
  16.7 0.9 %fusion.4 = f32[512,4,128]{0,2,1:T(8,128)S(1)} fusion(bf16[512,4,128]{0,2,1:T(8,128)(2,1)S(1)} %bitcast.138, f32[4,512,512]{1,2,0:T(8,128)S(1)} %get-tuple-element.24, f32[4,512]{1,0:T(4,128)S(1)} %bitcast.151, pred[512,512]{0,1:T(8,128)(4,1)S(1)} %iota_compare_fusion), kind=kOutput, calls=%fused_computation.15 | convolution fusion | flops 271581184 | bytes 6037504 | tf_op jit(solution)/shard_map/hts,thd->shd/dot_general | solution.py:54
  17.7 1.1 %add.40 = f32[4,128,128]{2,1,0:T(8,128)S(1)} add(f32[4,128,128]{2,1,0:T(8,128)} %fusion.22, f32[4,128,128]{2,1,0:T(8,128)} %collective-permute-done) | non-fusion elementwise | flops 65536 | bytes 786432 | tf_op jit(solution)/shard_map/add | solution.py:74
  18.8 2.1 %collective-permute-start.1 = (f32[4,128,128]{2,1,0:T(8,128)S(1)}, f32[4,128,128]{2,1,0:T(8,128)S(1)}, u32[]{:S(2)}, u32[]{:S(2)}) collective-permute-start(f32[4,128,128]{2,1,0:T(8,128)S(1)} %add.40), channel_id=1, source_target_pairs={{0,4},{2,6},{4,0},{6,2},{8,12},{10,14},{12,8},{14,10},{1,5},{3,7},... | collective-permute-start | bytes 786440 | tf_op jit(solution)/shard_map/ppermute | solution.py:16
  21.2 5.5 %collective-permute-done.1 = f32[4,128,128]{2,1,0:T(8,128)S(1)} collective-permute-done((f32[4,128,128]{2,1,0:T(8,128)S(1)}, f32[4,128,128]{2,1,0:T(8,128)S(1)}, u32[]{:S(2)}, u32[]{:S(2)}) %collective-permute-start.1) | collective-permute-done | bytes 262176 | tf_op jit(solution)/shard_map/ppermute | solution.py:16
  26.7 4.7 %collective-permute-start.2 = (bf16[4,128,128]{2,1,0:T(8,128)(2,1)S(1)}, bf16[4,128,128]{2,1,0:T(8,128)(2,1)S(1)}, u32[]{:S(2)}, u32[]{:S(2)}) collective-permute-start(bf16[4,128,128]{2,1,0:T(8,128)(2,1)S(1)} %add_convert_fusion.1), channel_id=1, source_target_pairs={{0,8},{2,10},{4,12},{6,14},{1,9},{3,11},{5,13},{7,15},{16,24},{18,... | collective-permute-start | bytes 393224 | tf_op jit(solution)/shard_map/ppermute | solution.py:12
  31.7 1.1 %slice_add_fusion = f32[2,4,128,128]{3,2,1,0:T(8,128)S(1)} fusion(f32[3,4,128,128]{3,2,1,0:T(8,128)} %collective-permute-done.3, f32[1,4,128,128]{3,2,1,0:T(8,128)S(1)} %fusion.9, f32[1,4,128,128]{3,2,1,0:T(8,128)S(1)} %fusion.10), kind=kLoop, calls=%fused_computation.50 | loop fusion | flops 262144 | bytes 1572864 | tf_op jit(solution)/shard_map/add | solution.py:79
  32.8 1.6 %collective-permute-start.4 = (f32[2,4,128,128]{3,2,1,0:T(8,128)S(1)}, f32[2,4,128,128]{3,2,1,0:T(8,128)S(1)}, u32[]{:S(2)}, u32[]{:S(2)}) collective-permute-start(f32[2,4,128,128]{3,2,1,0:T(8,128)S(1)} %slice_add_fusion), channel_id=1, source_target_pairs={{0,4},{2,6},{4,0},{6,2},{8,12},{10,14},{12,8},{14,10},{1,5},{3,7},... | collective-permute-start | bytes 1572872 | tf_op jit(solution)/shard_map/ppermute | solution.py:16
  34.4 0.4 collective-permute-done.2
  34.8 0.4 fusion.17
  35.2 1.9 %add_convert_fusion = bf16[512,4,128]{0,2,1:T(8,128)(2,1)} fusion(f32[512,4,128]{0,2,1:T(8,128)S(1)} %get-tuple-element.25, f32[512,4,128]{0,2,1:T(8,128)S(1)} %convolution_bitcast_fusion.5, f32[512,4,128]{0,2,1:T(8,128)S(1)} %convolution_bitcast_fusion.6, f32[512,4]{0,1:T(4,128)S(1)} %get-tuple-element.30, f32[512,4]{0,1:T(4,128)S(1)} %get-tuple-element.31, ...), kind=kOutput, calls=%fused_computation.37 | convolution fusion | flops 273416192 | bytes 8683520 | tf_op jit(solution)/shard_map/hts,shd->thd/dot_general | solution.py:52
  37.1 8.0 %collective-permute-done.4 = f32[2,4,128,128]{3,2,1,0:T(8,128)S(1)} collective-permute-done((f32[2,4,128,128]{3,2,1,0:T(8,128)S(1)}, f32[2,4,128,128]{3,2,1,0:T(8,128)S(1)}, u32[]{:S(2)}, u32[]{:S(2)}) %collective-permute-start.4) | collective-permute-done | bytes 524320 | tf_op jit(solution)/shard_map/ppermute | solution.py:16
  45.1 0.8 %copy-done.6 = f32[2,4,128,128]{3,2,1,0:T(8,128)} copy-done((f32[2,4,128,128]{3,2,1,0:T(8,128)}, f32[2,4,128,128]{3,2,1,0:T(8,128)S(1)}, u32[]{:S(2)}) %copy-start.6) | copy-done | bytes 524312
  45.9 1.3 %collective-permute-start.5 = (f32[1,4,128,128]{3,2,1,0:T(8,128)S(1)}, f32[1,4,128,128]{3,2,1,0:T(8,128)}, u32[]{:S(2)}, u32[]{:S(2)}) collective-permute-start(f32[1,4,128,128]{3,2,1,0:T(8,128)S(1)} %slice_add_fusion.1), channel_id=1, source_target_pairs={{8,0},{10,2},{12,4},{14,6},{9,1},{11,3},{13,5},{15,7},{24,16},{26,... | collective-permute-start | bytes 786440 | tf_op jit(solution)/shard_map/ppermute | solution.py:12
  47.2 2.0 %copy.89 = bf16[512,512]{1,0:T(8,128)(2,1)} copy(bf16[512,512]{0,1:T(8,128)(2,1)} %bitcast.147) | data formatting | bytes 1048576
  49.3 0.7 %stack.39 = f32[4,8,512]{2,1,0:T(8,128)} concatenate(f32[4,1,512]{2,1,0:T(1,128)S(1)} %copy.85, f32[4,1,512]{2,1,0:T(1,128)S(1)} %copy.86, f32[4,1,512]{2,1,0:T(1,128)S(1)} %copy.87, f32[4,1,512]{2,1,0:T(1,128)S(1)} %copy.88, f32[4,4,512]{2,1,0:T(4,128)S(1)} %stack.38), dimensions={1} | concatenate | bytes 131072 | tf_op jit(solution)/shard_map/stack | solution.py:105
  50.0 11.7 %collective-permute-done.5 = f32[1,4,128,128]{3,2,1,0:T(8,128)} collective-permute-done((f32[1,4,128,128]{3,2,1,0:T(8,128)S(1)}, f32[1,4,128,128]{3,2,1,0:T(8,128)}, u32[]{:S(2)}, u32[]{:S(2)}) %collective-permute-start.5) | collective-permute-done | bytes 262176 | tf_op jit(solution)/shard_map/ppermute | solution.py:12
  61.8 1.2 %fusion.46 = bf16[4,128,128]{2,1,0:T(8,128)(2,1)S(1)} fusion(f32[1,4,128,128]{3,2,1,0:T(8,128)} %collective-permute-done.5, f32[2,4,128,128]{3,2,1,0:T(8,128)} %copy-done.6, f32[3,4,128,128]{3,2,1,0:T(8,128)} %collective-permute-done.3, pred[]{:T(512)S(6)} %eq.9, pred[]{:T(512)S(6)} %eq.8), kind=kLoop, calls=%fused_computation.70 | loop fusion | flops 327680 | bytes 917506 | tf_op jit(solution)/shard_map/convert_element_type | solution.py:97
  62.9 1.1 %fusion.7 = bf16[512,4,128]{0,2,1:T(8,128)(2,1)} fusion(f32[512,4,128]{0,2,1:T(8,128)S(1)} %copy-done.3, bf16[4,128,128]{2,1,0:T(8,128)(2,1)S(1)} %fusion.46, bf16[512,512]{1,0:T(8,128)(2,1)S(1)} %copy-done.5), kind=kOutput, calls=%fused_computation.23 | convolution fusion | flops 67633152 | bytes 2228224 | tf_op jit(solution)/shard_map/she,hde->shd/dot_general | solution.py:98
  64.0 2.0 %copy.90 = bf16[512,512]{1,0:T(8,128)(2,1)} copy(bf16[512,512]{0,1:T(8,128)(2,1)} %bitcast.149) | data formatting | bytes 1048576
  66.1 0.3 fusion.8
  66.4 1.0 %copy.91 = bf16[512,512]{1,0:T(8,128)(2,1)} copy(bf16[512,512]{0,1:T(8,128)(2,1)S(1)} %bitcast.148) | data formatting | bytes 1048576
  (35 shorter events, 1.8 us)
Async XLA Ops:
  0.6 1.0 %copy-start = (bf16[512,512]{1,0:T(8,128)(2,1)S(1)}, bf16[512,512]{1,0:T(8,128)(2,1)}, u32[]{:S(2)}) copy-start(bf16[512,512]{1,0:T(8,128)(2,1)} %param.6) | copy-start | bytes 1572868
  3.8 8.4 %copy-start.4 = (bf16[512,512]{1,0:T(8,128)(2,1)S(1)}, bf16[512,512]{1,0:T(8,128)(2,1)}, u32[]{:S(2)}) copy-start(bf16[512,512]{1,0:T(8,128)(2,1)} %param.7) | copy-start | bytes 1572868
  3.8 14.0 %collective-permute-start = (f32[4,128,128]{2,1,0:T(8,128)}, f32[4,128,128]{2,1,0:T(8,128)}, u32[]{:S(2)}, u32[]{:S(2)}) collective-permute-start(f32[4,128,128]{2,1,0:T(8,128)} %fusion.22), channel_id=1, source_target_pairs={{0,2},{2,0},{4,6},{6,4},{8,10},{10,8},{12,14},{14,12},{1,3},{3,1},... | collective-permute-start | bytes 786440 | tf_op jit(solution)/shard_map/ppermute | solution.py:16
  12.1 19.5 %collective-permute-start.3 = (f32[3,4,128,128]{3,2,1,0:T(8,128)}, f32[3,4,128,128]{3,2,1,0:T(8,128)}, u32[]{:S(2)}, u32[]{:S(2)}) collective-permute-start(f32[3,4,128,128]{3,2,1,0:T(8,128)} %pad_maximum_fusion), channel_id=1, source_target_pairs={{0,2},{2,0},{4,6},{6,4},{8,10},{10,8},{12,14},{14,12},{1,3},{3,1},... | collective-permute-start | bytes 2359304 | tf_op jit(solution)/shard_map/ppermute | solution.py:16
  12.9 1.9 %copy-start.1 = (f32[4,512,512]{1,2,0:T(8,128)}, f32[4,512,512]{1,2,0:T(8,128)S(1)}, u32[]{:S(2)}) copy-start(f32[4,512,512]{1,2,0:T(8,128)S(1)} %fusion.24) | copy-start | bytes 12582916
  18.8 7.9 %collective-permute-start.1 = (f32[4,128,128]{2,1,0:T(8,128)S(1)}, f32[4,128,128]{2,1,0:T(8,128)S(1)}, u32[]{:S(2)}, u32[]{:S(2)}) collective-permute-start(f32[4,128,128]{2,1,0:T(8,128)S(1)} %add.40), channel_id=1, source_target_pairs={{0,4},{2,6},{4,0},{6,2},{8,12},{10,14},{12,8},{14,10},{1,5},{3,7},... | collective-permute-start | bytes 786440 | tf_op jit(solution)/shard_map/ppermute | solution.py:16
  21.2 14.0 %copy-start.2 = (f32[4,512,512]{1,2,0:T(8,128)S(1)}, f32[4,512,512]{1,2,0:T(8,128)}, u32[]{:S(2)}) copy-start(f32[4,512,512]{1,2,0:T(8,128)} %copy-done.1) | copy-start | bytes 12582916
  26.7 8.1 %collective-permute-start.2 = (bf16[4,128,128]{2,1,0:T(8,128)(2,1)S(1)}, bf16[4,128,128]{2,1,0:T(8,128)(2,1)S(1)}, u32[]{:S(2)}, u32[]{:S(2)}) collective-permute-start(bf16[4,128,128]{2,1,0:T(8,128)(2,1)S(1)} %add_convert_fusion.1), channel_id=1, source_target_pairs={{0,8},{2,10},{4,12},{6,14},{1,9},{3,11},{5,13},{7,15},{16,24},{18,... | collective-permute-start | bytes 393224 | tf_op jit(solution)/shard_map/ppermute | solution.py:12
  32.8 12.3 %collective-permute-start.4 = (f32[2,4,128,128]{3,2,1,0:T(8,128)S(1)}, f32[2,4,128,128]{3,2,1,0:T(8,128)S(1)}, u32[]{:S(2)}, u32[]{:S(2)}) collective-permute-start(f32[2,4,128,128]{3,2,1,0:T(8,128)S(1)} %slice_add_fusion), channel_id=1, source_target_pairs={{0,4},{2,6},{4,0},{6,2},{8,12},{10,14},{12,8},{14,10},{1,5},{3,7},... | collective-permute-start | bytes 1572872 | tf_op jit(solution)/shard_map/ppermute | solution.py:16
  35.2 27.7 %copy-start.3 = (f32[512,4,128]{0,2,1:T(8,128)S(1)}, f32[512,4,128]{0,2,1:T(8,128)}, u32[]{:S(2)}) copy-start(f32[512,4,128]{0,2,1:T(8,128)} %convolution_bitcast_fusion.1) | copy-start | bytes 3145732
  35.2 27.7 %copy-start.5 = (bf16[512,512]{1,0:T(8,128)(2,1)S(1)}, bf16[512,512]{1,0:T(8,128)(2,1)}, u32[]{:S(2)}) copy-start(bf16[512,512]{1,0:T(8,128)(2,1)} %param.7) | copy-start | bytes 1572868
  45.1 0.8 %copy-start.6 = (f32[2,4,128,128]{3,2,1,0:T(8,128)}, f32[2,4,128,128]{3,2,1,0:T(8,128)S(1)}, u32[]{:S(2)}) copy-start(f32[2,4,128,128]{3,2,1,0:T(8,128)S(1)} %collective-permute-done.4) | copy-start | bytes 1572868
  45.9 15.9 %collective-permute-start.5 = (f32[1,4,128,128]{3,2,1,0:T(8,128)S(1)}, f32[1,4,128,128]{3,2,1,0:T(8,128)}, u32[]{:S(2)}, u32[]{:S(2)}) collective-permute-start(f32[1,4,128,128]{3,2,1,0:T(8,128)S(1)} %slice_add_fusion.1), channel_id=1, source_target_pairs={{8,0},{10,2},{12,4},{14,6},{9,1},{11,3},{13,5},{15,7},{24,16},{26,... | collective-permute-start | bytes 786440 | tf_op jit(solution)/shard_map/ppermute | solution.py:12
where the time goes:
time: 68 us; the launch traced here: 67.4 us
  waiting for transfers between devices  25.6 us (38%)
  starting transfers between devices  12.7 us (19%)
  matrix products  11.7 us (17%)
  local copies, waits for them, and re-layouts  11.1 us (16%)
  other arithmetic  5.45 us (8%)
  between operations  0.92 us (1%)
    ppermute x4, waiting for transfers between devices, from_partner(): lax.ppermute(shard, axis, [(i, i ^ 1 << apart) for i in range(lax.axis_si...  13.5 us
    ppermute x2, waiting for transfers between devices, passed_along(): return lax.ppermute(block, axis, route)  12.1 us
    unnamed x20, local copies, waits for them, and re-layouts  9.08 us
    ppermute x4, starting transfers between devices, from_partner(): lax.ppermute(shard, axis, [(i, i ^ 1 << apart) for i in range(lax.axis_si...  6.75 us
    ppermute x2, starting transfers between devices, passed_along(): return lax.ppermute(block, axis, route)  5.94 us
    dot_general x1, matrix products, on_device(): jnp.einsum('shd,she->hde', keys_h, values_h, preferred_element_type=jnp.f...  2.09 us
    dot_general x1, matrix products, on_device(): jnp.einsum('hts,thd->shd', grad_mix, queries_h, preferred_element_type=jn...  1.89 us
    dot_general x1, matrix products, on_device(): jnp.einsum('hts,shd->thd', grad_mix, keys_h, preferred_element_type=jnp.f...  1.86 us
  transfers between devices with their start and end apart: 6, of which 4 were waited for; matrix products, arithmetic and copies ran while one was open for 26% of the time, Pallas kernels for 0%

commit v1 on v0

v1 whole, which is shorter than its diff:
```python
import functools
import math

import jax
import jax.numpy as jnp
from jax import lax
from jax.experimental import pallas as pl
from jax.experimental.pallas import tpu as pltpu
from jax.sharding import PartitionSpec as P

AXES = ("seq", "heads")
LOW = jnp.bfloat16
ROWS = 256


def nt(left, right):
    return lax.dot_general(
        left, right, (((1,), (1,)), ((), ())), preferred_element_type=jnp.float32
    )


def nn(left, right):
    return jnp.dot(left, right, preferred_element_type=jnp.float32)


def flip(block, mask):
    size = lax.axis_size(AXES)
    return lax.ppermute(block, AXES, [(i, i ^ mask) for i in range(size)])


def block_index():
    return lax.axis_index("seq") * lax.axis_size("heads") + lax.axis_index("heads")


def in_vmem(array):
    return pltpu.with_memory_space_constraint(array, pltpu.VMEM)


def level_scales(width, tokens, count):
    base = 1.0 / math.sqrt(width * tokens)
    return [base] + [base / math.sqrt(2.0 ** (level - 1)) for level in range(1, count)]


def state_kernel(
    bits, scales, q_hbm, k_hbm, v_hbm, g_hbm, w_hbm,
    q_out, k_out, v_out, g_out, w_out, qt_out, kt_out, d1_out, own_out, other_out, far_out, sems, w_sem,
):
    heads, tokens, width = q_out.shape
    half = heads // 2
    pairs = ((q_hbm, q_out), (k_hbm, k_out), (v_hbm, v_out), (g_hbm, g_out))
    w_copy = pltpu.make_async_copy(w_hbm, w_out, w_sem)
    copies = [
        [
            pltpu.make_async_copy(src.at[:, pl.ds(h * width, width)], dst.at[h], sems.at[i, h])
            for i, (src, dst) in enumerate(pairs)
        ]
        for h in range(heads)
    ]
    w_copy.start()
    for group in copies:
        for copy in group:
            copy.start()
    place = block_index()
    low_bit = place & 1
    w_copy.wait()
    for h in range(heads):
        for copy in copies[h]:
            copy.wait()
        query_t = q_out[h].T
        key_t = k_out[h].T
        qt_out[h] = query_t
        kt_out[h] = key_t
        grad = g_out[h]
        state = nn(key_t, v_out[h])
        query_f = query_t.astype(jnp.float32)
        slot = (h // half) ^ low_bit
        for level in range(1, bits + 1):
            scaled = (w_out[h, pl.ds(level, 1), :] * query_f).astype(LOW)
            level_state = scales[level] * nn(scaled, grad)
            upper = ((place >> (level - 1)) & 1) == 1
            mixed = jnp.where(upper, level_state, state).astype(LOW)
            if level == 1:
                d1_out[h] = mixed
            else:
                row = (level - 2) * half + h % half

                @pl.when(slot == 0)
                def _():
                    own_out[row] = mixed

                @pl.when(slot == 1)
                def _():
                    other_out[row] = mixed
                    if level > 2:
                        far_out[row - half] = mixed


def near_kernel(
    first, scale, q_ref, k_ref, v_ref, g_ref, w_ref, kt_ref, nq_out, nk_out, nv_out, nw_out
):
    heads, width, tokens = nq_out.shape
    rows = min(ROWS, tokens)
    for local in range(heads):
        h = first + local
        factor = scale * w_ref[h, pl.ds(0, 1), :]
        total = None
        weight = None
        for start in range(0, tokens, rows):
            left = tokens - start
            key = k_ref[h, start : start + rows, :]
            value = v_ref[h, start : start + rows, :]
            query = q_ref[h, start:, :]
            grad = g_ref[h, start:, :]
            scores = nt(key, query)
            dots = nt(value, grad)
            allowed = lax.broadcasted_iota(jnp.int32, (rows, left), 0) <= lax.broadcasted_iota(
                jnp.int32, (rows, left), 1
            )
            scores = jnp.where(allowed, scores, 0.0)
            dots = jnp.where(allowed, dots, 0.0)
            part = jnp.sum(scores * dots, axis=0, keepdims=True)
            now = factor[:, start:]
            grad_mix = (now * dots).astype(LOW)
            score_mix = (now * scores).astype(LOW)
            nk_out[local, start : start + rows, :] = nn(grad_mix, query)
            nv_out[local, start : start + rows, :] = nn(score_mix, grad)
            back = nn(kt_ref[h, :, start : start + rows], grad_mix)
            if start == 0:
                nq_out[local] = back
                nw_out[local] = scale * part
            else:
                nq_out[local, :, start:] += back
                nw_out[local, :, start:] += scale * part


def far_kernel(bits, scales, split, *refs):
    (k_ref, v_ref, g_ref, w_ref, qt_ref, r1_ref, own_ref, other_ref), refs = refs[:8], refs[8:]
    near = [refs[4 * i : 4 * i + 4] for i in range(len(split))]
    gq_hbm, gk_hbm, gv_hbm, gw_out, gq_buf, gk_buf, gv_buf, sems = refs[4 * len(split) :]
    heads, tokens, width = k_ref.shape
    half = heads // 2
    place = block_index()
    low_bit = place & 1
    copies = []
    for h in range(heads):
        index = max(i for i, first in enumerate(split) if first <= h)
        nq_ref, nk_ref, nv_ref, nw_ref = near[index]
        local = h - split[index]
        grad = g_ref[h]
        query_t = qt_ref[h].astype(jnp.float32)
        reverse = jnp.zeros((width, width), jnp.float32)
        total = nq_ref[local]
        gw_out[h] = jnp.zeros(gw_out.shape[1:], jnp.float32)
        gw_out[h, pl.ds(0, 1), :] = nw_ref[local]
        for level in range(1, bits + 1):
            if level == 1:
                got = r1_ref[h]
            else:
                row = (level - 2) * half + h % half
                got = jnp.where(low_bit == h // half, own_ref[row], other_ref[row])
            upper = ((place >> (level - 1)) & 1) == 1
            got_f = got.astype(jnp.float32)
            sibling = jnp.where(upper, got_f, 0.0).astype(LOW)
            reverse = reverse + jnp.where(upper, 0.0, got_f)
            products = scales[level] * nt(sibling, grad)
            total = total + w_ref[h, pl.ds(level, 1), :] * products
            gw_out[h, pl.ds(level, 1), :] = jnp.sum(products * query_t, axis=0, keepdims=True)
        low = reverse.astype(LOW)
        gq_buf[h] = total.T.astype(LOW)
        gk_buf[h] = (nk_ref[local] + nt(v_ref[h], low)).astype(LOW)
        gv_buf[h] = (nv_ref[local] + nn(k_ref[h], low)).astype(LOW)
        for i, (buf, hbm) in enumerate(((gq_buf, gq_hbm), (gk_buf, gk_hbm), (gv_buf, gv_hbm))):
            copy = pltpu.make_async_copy(buf.at[h], hbm.at[:, pl.ds(h * width, width)], sems.at[i, h])
            copy.start()
            copies.append(copy)
    for copy in copies:
        copy.wait()


ANY = pl.BlockSpec(memory_space=pl.ANY)
IN_VMEM = pl.BlockSpec(memory_space=pltpu.VMEM)
LIMIT = 48 * 1024 * 1024


def on_device(queries, keys, values, out_grad, level_weights):
    tokens = queries.shape[0]
    heads, levels, _ = level_weights.shape
    width = queries.shape[1] // heads
    half = heads // 2
    bits = lax.axis_size(AXES).bit_length() - 1
    scales = level_scales(width, tokens, levels)
    by_head = pltpu.VMEM((heads, tokens, width), LOW)
    by_head_t = pltpu.VMEM((heads, width, tokens), LOW)
    halves = (bits - 1) * half
    (q_v, k_v, v_v, g_v, w_v, qt, kt, d1, own, other, far) = pl.pallas_call(
        functools.partial(state_kernel, bits, scales),
        out_shape=(
            by_head, by_head, by_head, by_head,
            pltpu.VMEM((heads, levels, tokens), jnp.float32),
            by_head_t, by_head_t,
            pltpu.VMEM((heads, width, width), LOW),
            pltpu.VMEM((halves, width, width), LOW),
            pltpu.VMEM((halves, width, width), LOW),
            pltpu.VMEM((halves - half, width, width), LOW),
        ),
        in_specs=[ANY] * 5,
        out_specs=(IN_VMEM,) * 11,
        scratch_shapes=[pltpu.SemaphoreType.DMA((4, heads)), pltpu.SemaphoreType.DMA],
        compiler_params=pltpu.CompilerParams(vmem_limit_bytes=LIMIT),
        cost_estimate=pl.CostEstimate(
            flops=2 * heads * (bits + 1) * tokens * width * width,
            bytes_accessed=4 * heads * tokens * width * 2,
            transcendentals=0,
        ),
        name="states",
    )(queries, keys, values, out_grad, level_weights)

    def near(first, count):
        return pl.pallas_call(
            functools.partial(near_kernel, first, scales[0]),
            out_shape=(
                pltpu.VMEM((count, width, tokens), jnp.float32),
                pltpu.VMEM((count, tokens, width), jnp.float32),
                pltpu.VMEM((count, tokens, width), jnp.float32),
                pltpu.VMEM((count, 1, tokens), jnp.float32),
            ),
            in_specs=[IN_VMEM] * 6,
            out_specs=(IN_VMEM,) * 4,
            compiler_params=pltpu.CompilerParams(vmem_limit_bytes=LIMIT),
            cost_estimate=pl.CostEstimate(
                flops=10 * count * tokens * tokens * width,
                bytes_accessed=count * tokens * width * 20,
                transcendentals=0,
            ),
            name="near",
        )(*[in_vmem(x) for x in (q_v, k_v, v_v, g_v, w_v, kt)])

    split = (0, half)
    near_parts = [near(0, half), near(half, heads - half)]

    got_x = flip(other, 1)
    got_1 = flip(d1, 1)
    got_z = flip(own[half:], 2)
    got_d = flip(far, 3)
    as_f = lambda x: x.astype(jnp.float32)
    pair = (as_f(own[:half]) + as_f(got_x[:half])).astype(LOW)
    quad = as_f(own[half:]) + as_f(got_x[half:]) + as_f(got_z) + as_f(got_d)
    sums = [pair]
    for bit in range(2, bits):
        sums.append(quad[:half].astype(LOW))
        quad = quad[half:]
        if bit < bits - 1:
            quad = quad + as_f(flip(quad.astype(LOW), 1 << bit))
    own_half = [flip(x, 1 << (i + 1)) for i, x in enumerate(sums)]
    other_half = [flip(x, (1 << (i + 1)) ^ 1) for i, x in enumerate(sums)]
    out = jax.ShapeDtypeStruct((tokens, heads * width), LOW)
    flat_near = [x for part in near_parts for x in part]
    return pl.pallas_call(
        functools.partial(far_kernel, bits, scales, split),
        out_shape=(out, out, out, jax.ShapeDtypeStruct((heads, levels, tokens), jnp.float32)),
        in_specs=[IN_VMEM] * (8 + len(flat_near)),
        out_specs=(ANY, ANY, ANY, IN_VMEM),
        scratch_shapes=[pltpu.VMEM((heads, tokens, width), LOW)] * 3
        + [pltpu.SemaphoreType.DMA((3, heads))],
        compiler_params=pltpu.CompilerParams(vmem_limit_bytes=LIMIT),
        cost_estimate=pl.CostEstimate(
            flops=2 * heads * (bits + 2) * tokens * width * width,
            bytes_accessed=3 * heads * tokens * width * 2,
            transcendentals=0,
        ),
        name="far",
    )(
        *[
            in_vmem(x)
            for x in (
                k_v, v_v, g_v, w_v, qt, got_1,
                jnp.concatenate(own_half, 0), jnp.concatenate(other_half, 0), *flat_near,
            )
        ]
    )


def solution(mesh):
    rows = P(("groups", "seq", "heads"), "sub")
    weights = P("sub", None, ("groups", "seq", "heads"))
    return jax.shard_map(
        on_device,
        mesh=mesh,
        in_specs=(rows, rows, rows, rows, weights),
        out_specs=(rows, rows, rows, weights),
        check_vma=False,
    )
```

time: 68 us -> 35.5 us (0.52)
  waiting for transfers between devices: 25.6 us -> 8.76 us
  matrix products: 11.7 us -> 0 us
  Pallas kernels: 0 us -> 8.16 us
  local copies, waits for them, and re-layouts: 11.1 us -> 5 us
  other arithmetic: 5.45 us -> 0.08 us
    ppermute x6 -> x8, waiting for transfers between devices: 25.6 us -> 8.76 us  [flip(): return lax.ppermute(block, AXES, [(i, i ^ mask) for i in range(size)])]
    dot_general x14 -> x0, matrix products: 11.7 us -> none  [the longest x1 2.09 us: on_device(): jnp.einsum('shd,she->hde', keys_h, values_h, preferred_element_type=jnp.f...]
    pallas_call x0 -> x4, Pallas kernels: none -> 8.16 us  [the longest x1 2.8 us: on_device(): pl.pallas_call(functools.partial(far_kernel, bits, scales, split), out_sh...]
    unnamed x20 -> x10, local copies, waits for them, and re-layouts: 9.08 us -> 5 us
    add x3 -> x0, other arithmetic: 2.19 us -> none  [the longest x2 1.13 us: on_device(): pending = pending[1:] + received[1:]]
    reshape x1 -> x0, local copies, waits for them, and re-layouts: 1.26 us -> none  [on_device(): grads_h = out_grad.reshape(shape_three)]
    convert_element_type x2 -> x1, other arithmetic: 1.19 us -> 0.06 us  [on_device(): pair = (as_f(own[:half]) + as_f(got_x[:half])).astype(LOW)]
    mul x4 -> x0, other arithmetic: 1.03 us -> none  [the longest x1 1.02 us: on_device(): factor = scales[0] * level_weights[:, 0, :][:, :, None]]
  transfers between devices with their start and end apart: 6 -> 8, of which waited for: 4 -> 4; matrix products, arithmetic and copies ran while one was open for 26% -> 0% of each run, Pallas kernels for 0% -> 8%
where the time goes in v1:
time: 35.5 us; the launch traced here: 35.2 us
  starting transfers between devices  12.5 us (35%)
  waiting for transfers between devices  8.76 us (25%)
  Pallas kernels  8.16 us (23%)
  local copies, waits for them, and re-layouts  5 us (14%)
  between operations  0.69 us (2%)
    ppermute x8, starting transfers between devices, flip(): return lax.ppermute(block, AXES, [(i, i ^ mask) for i in range(size)])  12.5 us
    ppermute x8, waiting for transfers between devices, flip(): return lax.ppermute(block, AXES, [(i, i ^ mask) for i in range(size)])  8.76 us
    unnamed x10, local copies, waits for them, and re-layouts  5 us
    pallas_call x1, Pallas kernels, on_device(): pl.pallas_call(functools.partial(far_kernel, bits, scales, split), out_sh...  2.8 us
    pallas_call x2, Pallas kernels, near(): pl.pallas_call(functools.partial(near_kernel, first, scales[0]), out_shap...  2.74 us
    pallas_call x1, Pallas kernels, on_device(): pl.pallas_call(functools.partial(state_kernel, bits, scales), out_shape=(...  2.62 us
  transfers between devices with their start and end apart: 8, of which 4 were waited for; matrix products, arithmetic and copies ran while one was open for 0% of the time, Pallas kernels for 8%

profile of v1, /device:TPU:0, one launch (start us, length us, event | category | flops | bytes accessed | tf_op | source)
XLA Modules:
  0.0 35.2 jit_solution(12777548969378107379)
XLA Ops:
  0.6 0.0 copy-start
  0.6 1.0 %copy-done = bf16[512,512]{1,0:T(8,128)(2,1)S(1)} copy-done((bf16[512,512]{1,0:T(8,128)(2,1)S(1)}, bf16[512,512]{1,0:T(8,128)(2,1)}, u32[]{:S(2)}) %copy-start) | copy-done | bytes 524312
  1.7 0.0 copy-start.1
  1.7 1.0 %copy-done.1 = bf16[512,512]{1,0:T(8,128)(2,1)S(1)} copy-done((bf16[512,512]{1,0:T(8,128)(2,1)S(1)}, bf16[512,512]{1,0:T(8,128)(2,1)}, u32[]{:S(2)}) %copy-start.1) | copy-done | bytes 524312
  2.7 0.0 copy-start.2
  2.7 1.0 %copy-done.2 = bf16[512,512]{1,0:T(8,128)(2,1)S(1)} copy-done((bf16[512,512]{1,0:T(8,128)(2,1)S(1)}, bf16[512,512]{1,0:T(8,128)(2,1)}, u32[]{:S(2)}) %copy-start.2) | copy-done | bytes 524312
  3.8 0.0 copy-start.3
  3.8 1.0 %copy-done.3 = bf16[512,512]{1,0:T(8,128)(2,1)S(1)} copy-done((bf16[512,512]{1,0:T(8,128)(2,1)S(1)}, bf16[512,512]{1,0:T(8,128)(2,1)}, u32[]{:S(2)}) %copy-start.3) | copy-done | bytes 524312
  4.8 0.0 copy-start.4
  4.8 0.8 %copy-done.4 = f32[4,8,512]{2,1,0:T(8,128)S(1)} copy-done((f32[4,8,512]{2,1,0:T(8,128)S(1)}, f32[4,8,512]{2,1,0:T(8,128)}, u32[]{:S(2)}) %copy-start.4) | copy-done | bytes 65560
  5.6 2.6 %states.1 = (bf16[4,512,128]{2,1,0:T(8,128)(2,1)S(1)}, bf16[4,512,128]{2,1,0:T(8,128)(2,1)S(1)}, bf16[4,512,128]{2,1,0:T(8,128)(2,1)S(1)}, bf16[4,512,128]{2,1,0...) custom-call(bf16[512,512]{1,0:T(8,128)(2,1)S(1)} %copy-done, ...), custom_call_target="tpu_custom_call" | custom-call | flops 268435456 | bytes 2097152 | tf_op jit(solution)/shard_map/states/pallas_call | solution.py:195
  8.3 3.0 %collective-permute-start.1 = (bf16[4,128,128]{2,1,0:T(8,128)(2,1)S(1)}, bf16[4,128,128]{2,1,0:T(8,128)(2,1)S(1)}, u32[]{:S(2)}, u32[]{:S(2)}) collective-permute-start(bf16[4,128,128]{2,1,0:T(8,128)(2,1)S(1)} %get-tuple-element.30), channel_id=1, source_target_pairs={{0,2},{2,0},{4,6},{6,4},{8,10},{10,8},{12,14},{14,12},{1,3},{3,1},... | collective-permute-start | bytes 393224 | tf_op jit(solution)/shard_map/ppermute | solution.py:28
  11.3 1.6 %collective-permute-start.3 = (bf16[2,128,128]{2,1,0:T(8,128)(2,1)S(1)}, bf16[2,128,128]{2,1,0:T(8,128)(2,1)S(1)}, u32[]{:S(2)}, u32[]{:S(2)}) collective-permute-start(bf16[2,128,128]{2,1,0:T(8,128)(2,1)S(1)} %slice.15), channel_id=1, source_target_pairs={{0,4},{2,6},{4,0},{6,2},{8,12},{10,14},{12,8},{14,10},{1,5},{3,7},... | collective-permute-start | bytes 196616 | tf_op jit(solution)/shard_map/ppermute | solution.py:28
  12.9 0.0 collective-permute-start.4
  12.9 1.9 %collective-permute-start = (bf16[4,128,128]{2,1,0:T(8,128)(2,1)S(1)}, bf16[4,128,128]{2,1,0:T(8,128)(2,1)S(1)}, u32[]{:S(2)}, u32[]{:S(2)}) collective-permute-start(bf16[4,128,128]{2,1,0:T(8,128)(2,1)S(1)} %get-tuple-element.28), channel_id=1, source_target_pairs={{0,2},{2,0},{4,6},{6,4},{8,10},{10,8},{12,14},{14,12},{1,3},{3,1},... | collective-permute-start | bytes 393224 | tf_op jit(solution)/shard_map/ppermute | solution.py:28
  14.8 1.3 %collective-permute-done.3 = bf16[2,128,128]{2,1,0:T(8,128)(2,1)S(1)} collective-permute-done((bf16[2,128,128]{2,1,0:T(8,128)(2,1)S(1)}, bf16[2,128,128]{2,1,0:T(8,128)(2,1)S(1)}, u32[]{:S(2)}, u32[]{:S(2)}) %collective-permute-start.3) | collective-permute-done | bytes 65568 | tf_op jit(solution)/shard_map/ppermute | solution.py:28
  16.1 2.0 %collective-permute-done.4 = bf16[2,128,128]{2,1,0:T(8,128)(2,1)S(1)} collective-permute-done((bf16[2,128,128]{2,1,0:T(8,128)(2,1)S(1)}, bf16[2,128,128]{2,1,0:T(8,128)(2,1)S(1)}, u32[]{:S(2)}, u32[]{:S(2)}) %collective-permute-start.4) | collective-permute-done | bytes 65568 | tf_op jit(solution)/shard_map/ppermute | solution.py:28
  18.1 0.0 collective-permute-done.1
  18.1 0.1 add_convert_fusion.1
  18.2 1.6 %collective-permute-start.6 = (bf16[2,128,128]{2,1,0:T(8,128)(2,1)S(1)}, bf16[2,128,128]{2,1,0:T(8,128)(2,1)S(1)}, u32[]{:S(2)}, u32[]{:S(2)}) collective-permute-start(bf16[2,128,128]{2,1,0:T(8,128)(2,1)S(1)} %get-tuple-element.42), channel_id=1, source_target_pairs={{0,6},{2,4},{4,2},{6,0},{8,14},{10,12},{12,10},{14,8},{1,7},{3,5},... | collective-permute-start | bytes 196616 | tf_op jit(solution)/shard_map/ppermute | solution.py:28
  19.8 2.4 %collective-permute-start.7 = (bf16[2,128,128]{2,1,0:T(8,128)(2,1)S(1)}, bf16[2,128,128]{2,1,0:T(8,128)(2,1)S(1)}, u32[]{:S(2)}, u32[]{:S(2)}) collective-permute-start(bf16[2,128,128]{2,1,0:T(8,128)(2,1)S(1)} %get-tuple-element.43), channel_id=1, source_target_pairs={{0,10},{2,8},{4,14},{6,12},{8,2},{10,0},{12,6},{14,4},{1,11},{3,9}... | collective-permute-start | bytes 196616 | tf_op jit(solution)/shard_map/ppermute | solution.py:28
  22.2 1.4 %near.3 = (f32[2,128,512]{2,1,0:T(8,128)S(1)}, f32[2,512,128]{2,1,0:T(8,128)S(1)}, f32[2,512,128]{2,1,0:T(8,128)S(1)}, f32[2,1,512]{2,1,0:T(1,128)S(1)}) custom-call(bf16[4,512,128]{2,1,0:T(8,128)(2,1)S(1)} %get-tuple-element.32.q_ref, bf16[4,512,128]{2,1,0:T(8,128)(2,1)S(1)} %get-tuple-element.23.k_ref.refs_0_, ...), custom_call_target="tpu_custom_call" | custom-call | flops 671088640 | bytes 2621440 | tf_op jit(solution)/shard_map/near/pallas_call | solution.py:219
  23.6 1.4 %near.2 = (f32[2,128,512]{2,1,0:T(8,128)S(1)}, f32[2,512,128]{2,1,0:T(8,128)S(1)}, f32[2,512,128]{2,1,0:T(8,128)S(1)}, f32[2,1,512]{2,1,0:T(1,128)S(1)}) custom-call(bf16[4,512,128]{2,1,0:T(8,128)(2,1)S(1)} %get-tuple-element.32.q_ref, bf16[4,512,128]{2,1,0:T(8,128)(2,1)S(1)} %get-tuple-element.23.k_ref.refs_0_, ...), custom_call_target="tpu_custom_call" | custom-call | flops 671088640 | bytes 2621440 | tf_op jit(solution)/shard_map/near/pallas_call | solution.py:219
  24.9 1.6 %collective-permute-start.2 = (bf16[2,128,128]{2,1,0:T(8,128)(2,1)S(1)}, bf16[2,128,128]{2,1,0:T(8,128)(2,1)S(1)}, u32[]{:S(2)}, u32[]{:S(2)}) collective-permute-start(bf16[2,128,128]{2,1,0:T(8,128)(2,1)S(1)} %get-tuple-element.42), channel_id=1, source_target_pairs={{0,4},{2,6},{4,0},{6,2},{8,12},{10,14},{12,8},{14,10},{1,5},{3,7},... | collective-permute-start | bytes 196616 | tf_op jit(solution)/shard_map/ppermute | solution.py:28
  26.6 0.3 collective-permute-start.5
  26.9 0.0 collective-permute-done.6
  26.9 0.0 collective-permute-done.7
  26.9 2.5 %collective-permute-done.2 = bf16[2,128,128]{2,1,0:T(8,128)(2,1)S(1)} collective-permute-done((bf16[2,128,128]{2,1,0:T(8,128)(2,1)S(1)}, bf16[2,128,128]{2,1,0:T(8,128)(2,1)S(1)}, u32[]{:S(2)}, u32[]{:S(2)}) %collective-permute-start.2) | collective-permute-done | bytes 65568 | tf_op jit(solution)/shard_map/ppermute | solution.py:28
  29.5 2.9 %collective-permute-done.5 = bf16[2,128,128]{2,1,0:T(8,128)(2,1)S(1)} collective-permute-done((bf16[2,128,128]{2,1,0:T(8,128)(2,1)S(1)}, bf16[2,128,128]{2,1,0:T(8,128)(2,1)S(1)}, u32[]{:S(2)}, u32[]{:S(2)}) %collective-permute-start.5) | collective-permute-done | bytes 65568 | tf_op jit(solution)/shard_map/ppermute | solution.py:28
  32.4 0.0 collective-permute-done.refs_5_
  32.4 2.8 %far.1 = (bf16[512,512]{1,0:T(8,128)(2,1)}, bf16[512,512]{1,0:T(8,128)(2,1)}, bf16[512,512]{1,0:T(8,128)(2,1)}, f32[4,8,512]{2,1,0:T(8,128)}) custom-call(bf16[4,512,128]{2,1,0:T(8,128)(2,1)S(1)} %get-tuple-element.23.k_ref.refs_0_, bf16[4,512,128]{2,1,0:T(8,128)(2,1)S(1)} %get-tuple-element.24.v_ref.refs_1_, ...), custom_call_target="tpu_custom_call" | custom-call | flops 335544320 | bytes 1572864 | tf_op jit(solution)/shard_map/far/pallas_call | solution.py:258
  (3 shorter events, 0.0 us)
Async XLA Ops:
  0.6 1.0 %copy-start = (bf16[512,512]{1,0:T(8,128)(2,1)S(1)}, bf16[512,512]{1,0:T(8,128)(2,1)}, u32[]{:S(2)}) copy-start(bf16[512,512]{1,0:T(8,128)(2,1)} %q_hbm.1) | copy-start | bytes 1572868
  1.7 1.0 %copy-start.1 = (bf16[512,512]{1,0:T(8,128)(2,1)S(1)}, bf16[512,512]{1,0:T(8,128)(2,1)}, u32[]{:S(2)}) copy-start(bf16[512,512]{1,0:T(8,128)(2,1)} %k_hbm.1) | copy-start | bytes 1572868
  2.7 1.0 %copy-start.2 = (bf16[512,512]{1,0:T(8,128)(2,1)S(1)}, bf16[512,512]{1,0:T(8,128)(2,1)}, u32[]{:S(2)}) copy-start(bf16[512,512]{1,0:T(8,128)(2,1)} %v_hbm.1) | copy-start | bytes 1572868
  3.8 1.0 %copy-start.3 = (bf16[512,512]{1,0:T(8,128)(2,1)S(1)}, bf16[512,512]{1,0:T(8,128)(2,1)}, u32[]{:S(2)}) copy-start(bf16[512,512]{1,0:T(8,128)(2,1)} %g_hbm.1) | copy-start | bytes 1572868
  4.8 0.8 %copy-start.4 = (f32[4,8,512]{2,1,0:T(8,128)S(1)}, f32[4,8,512]{2,1,0:T(8,128)}, u32[]{:S(2)}) copy-start(f32[4,8,512]{2,1,0:T(8,128)} %w_hbm.1) | copy-start | bytes 196612
  8.3 9.9 %collective-permute-start.1 = (bf16[4,128,128]{2,1,0:T(8,128)(2,1)S(1)}, bf16[4,128,128]{2,1,0:T(8,128)(2,1)S(1)}, u32[]{:S(2)}, u32[]{:S(2)}) collective-permute-start(bf16[4,128,128]{2,1,0:T(8,128)(2,1)S(1)} %get-tuple-element.30), channel_id=1, source_target_pairs={{0,2},{2,0},{4,6},{6,4},{8,10},{10,8},{12,14},{14,12},{1,3},{3,1},... | collective-permute-start | bytes 393224 | tf_op jit(solution)/shard_map/ppermute | solution.py:28
  11.3 4.8 %collective-permute-start.3 = (bf16[2,128,128]{2,1,0:T(8,128)(2,1)S(1)}, bf16[2,128,128]{2,1,0:T(8,128)(2,1)S(1)}, u32[]{:S(2)}, u32[]{:S(2)}) collective-permute-start(bf16[2,128,128]{2,1,0:T(8,128)(2,1)S(1)} %slice.15), channel_id=1, source_target_pairs={{0,4},{2,6},{4,0},{6,2},{8,12},{10,14},{12,8},{14,10},{1,5},{3,7},... | collective-permute-start | bytes 196616 | tf_op jit(solution)/shard_map/ppermute | solution.py:28
  12.9 5.3 %collective-permute-start.4 = (bf16[2,128,128]{2,1,0:T(8,128)(2,1)S(1)}, bf16[2,128,128]{2,1,0:T(8,128)(2,1)S(1)}, u32[]{:S(2)}, u32[]{:S(2)}) collective-permute-start(bf16[2,128,128]{2,1,0:T(8,128)(2,1)S(1)} %get-tuple-element.31), channel_id=1, source_target_pairs={{0,6},{2,4},{4,2},{6,0},{8,14},{10,12},{12,10},{14,8},{1,7},{3,5},... | collective-permute-start | bytes 196616 | tf_op jit(solution)/shard_map/ppermute | solution.py:28
  12.9 19.5 %collective-permute-start = (bf16[4,128,128]{2,1,0:T(8,128)(2,1)S(1)}, bf16[4,128,128]{2,1,0:T(8,128)(2,1)S(1)}, u32[]{:S(2)}, u32[]{:S(2)}) collective-permute-start(bf16[4,128,128]{2,1,0:T(8,128)(2,1)S(1)} %get-tuple-element.28), channel_id=1, source_target_pairs={{0,2},{2,0},{4,6},{6,4},{8,10},{10,8},{12,14},{14,12},{1,3},{3,1},... | collective-permute-start | bytes 393224 | tf_op jit(solution)/shard_map/ppermute | solution.py:28
  18.2 8.7 %collective-permute-start.6 = (bf16[2,128,128]{2,1,0:T(8,128)(2,1)S(1)}, bf16[2,128,128]{2,1,0:T(8,128)(2,1)S(1)}, u32[]{:S(2)}, u32[]{:S(2)}) collective-permute-start(bf16[2,128,128]{2,1,0:T(8,128)(2,1)S(1)} %get-tuple-element.42), channel_id=1, source_target_pairs={{0,6},{2,4},{4,2},{6,0},{8,14},{10,12},{12,10},{14,8},{1,7},{3,5},... | collective-permute-start | bytes 196616 | tf_op jit(solution)/shard_map/ppermute | solution.py:28
  19.8 7.1 %collective-permute-start.7 = (bf16[2,128,128]{2,1,0:T(8,128)(2,1)S(1)}, bf16[2,128,128]{2,1,0:T(8,128)(2,1)S(1)}, u32[]{:S(2)}, u32[]{:S(2)}) collective-permute-start(bf16[2,128,128]{2,1,0:T(8,128)(2,1)S(1)} %get-tuple-element.43), channel_id=1, source_target_pairs={{0,10},{2,8},{4,14},{6,12},{8,2},{10,0},{12,6},{14,4},{1,11},{3,9}... | collective-permute-start | bytes 196616 | tf_op jit(solution)/shard_map/ppermute | solution.py:28
  24.9 4.5 %collective-permute-start.2 = (bf16[2,128,128]{2,1,0:T(8,128)(2,1)S(1)}, bf16[2,128,128]{2,1,0:T(8,128)(2,1)S(1)}, u32[]{:S(2)}, u32[]{:S(2)}) collective-permute-start(bf16[2,128,128]{2,1,0:T(8,128)(2,1)S(1)} %get-tuple-element.42), channel_id=1, source_target_pairs={{0,4},{2,6},{4,0},{6,2},{8,12},{10,14},{12,8},{14,10},{1,5},{3,7},... | collective-permute-start | bytes 196616 | tf_op jit(solution)/shard_map/ppermute | solution.py:28
  26.6 5.8 %collective-permute-start.5 = (bf16[2,128,128]{2,1,0:T(8,128)(2,1)S(1)}, bf16[2,128,128]{2,1,0:T(8,128)(2,1)S(1)}, u32[]{:S(2)}, u32[]{:S(2)}) collective-permute-start(bf16[2,128,128]{2,1,0:T(8,128)(2,1)S(1)} %get-tuple-element.43), channel_id=1, source_target_pairs={{0,8},{2,10},{4,12},{6,14},{8,0},{10,2},{12,4},{14,6},{1,9},{3,11}... | collective-permute-start | bytes 196616 | tf_op jit(solution)/shard_map/ppermute | solution.py:28

commit v2 on v1

--- a/solution.py
+++ b/solution.py
@@ -96,8 +96,12 @@
 
 
 def near_kernel(
-    first, scale, q_ref, k_ref, v_ref, g_ref, w_ref, kt_ref, nq_out, nk_out, nv_out, nw_out
+    first, scale, q_ref, k_ref, v_ref, g_ref, w_ref, kt_ref, *refs
 ):
+    if first == 0:
+        refs[-1][...] = refs[0][...]
+        refs = refs[1:-1]
+    nq_out, nk_out, nv_out, nw_out = refs
     heads, width, tokens = nq_out.shape
     rows = min(ROWS, tokens)
     for local in range(heads):
@@ -134,7 +138,8 @@
 
 
 def far_kernel(bits, scales, split, *refs):
-    (k_ref, v_ref, g_ref, w_ref, qt_ref, r1_ref, own_ref, other_ref), refs = refs[:8], refs[8:]
+    (k_ref, v_ref, g_ref, w_ref, qt_ref, r1_ref), refs = refs[:6], refs[6:]
+    own_refs, other_refs, refs = refs[: bits - 1], refs[bits - 1 : 2 * bits - 2], refs[2 * bits - 2 :]
     near = [refs[4 * i : 4 * i + 4] for i in range(len(split))]
     gq_hbm, gk_hbm, gv_hbm, gw_out, gq_buf, gk_buf, gv_buf, sems = refs[4 * len(split) :]
     heads, tokens, width = k_ref.shape
@@ -156,8 +161,8 @@
             if level == 1:
                 got = r1_ref[h]
             else:
-                row = (level - 2) * half + h % half
-                got = jnp.where(low_bit == h // half, own_ref[row], other_ref[row])
+                own_ref, other_ref = own_refs[level - 2], other_refs[level - 2]
+                got = jnp.where(low_bit == h // half, own_ref[h % half], other_ref[h % half])
             upper = ((place >> (level - 1)) & 1) == 1
             got_f = got.astype(jnp.float32)
             sibling = jnp.where(upper, got_f, 0.0).astype(LOW)
@@ -213,9 +218,9 @@
             transcendentals=0,
         ),
         name="states",
-    )(queries, keys, values, out_grad, level_weights)
-
-    def near(first, count):
+    )(*[pltpu.with_memory_space_constraint(x, pltpu.HBM) for x in (queries, keys, values, out_grad, level_weights)])
+
+    def near(first, count, passed=()):
         return pl.pallas_call(
             functools.partial(near_kernel, first, scales[0]),
             out_shape=(
@@ -223,20 +228,22 @@
                 pltpu.VMEM((count, tokens, width), jnp.float32),
                 pltpu.VMEM((count, tokens, width), jnp.float32),
                 pltpu.VMEM((count, 1, tokens), jnp.float32),
+                *[pltpu.VMEM(x.shape, x.dtype) for x in passed],
             ),
-            in_specs=[IN_VMEM] * 6,
-            out_specs=(IN_VMEM,) * 4,
+            in_specs=[IN_VMEM] * (6 + len(passed)),
+            out_specs=(IN_VMEM,) * (4 + len(passed)),
             compiler_params=pltpu.CompilerParams(vmem_limit_bytes=LIMIT),
             cost_estimate=pl.CostEstimate(
-                flops=10 * count * tokens * tokens * width,
+                flops=1000 * count * tokens * tokens * width,
                 bytes_accessed=count * tokens * width * 20,
                 transcendentals=0,
             ),
             name="near",
-        )(*[in_vmem(x) for x in (q_v, k_v, v_v, g_v, w_v, kt)])
+        )(*[in_vmem(x) for x in (q_v, k_v, v_v, g_v, w_v, kt, *passed)])
 
     split = (0, half)
-    near_parts = [near(0, half), near(half, heads - half)]
+    near_parts = [near(0, half, (d1,)), near(half, heads - half)]
+    d1 = near_parts[0][-1]
 
     got_x = flip(other, 1)
     got_1 = flip(d1, 1)
@@ -254,11 +261,12 @@
     own_half = [flip(x, 1 << (i + 1)) for i, x in enumerate(sums)]
     other_half = [flip(x, (1 << (i + 1)) ^ 1) for i, x in enumerate(sums)]
     out = jax.ShapeDtypeStruct((tokens, heads * width), LOW)
-    flat_near = [x for part in near_parts for x in part]
+    operands = [k_v, v_v, g_v, w_v, qt, got_1, *own_half, *other_half]
+    operands += [x for part in near_parts for x in part[:4]]
     return pl.pallas_call(
         functools.partial(far_kernel, bits, scales, split),
         out_shape=(out, out, out, jax.ShapeDtypeStruct((heads, levels, tokens), jnp.float32)),
-        in_specs=[IN_VMEM] * (8 + len(flat_near)),
+        in_specs=[IN_VMEM] * len(operands),
         out_specs=(ANY, ANY, ANY, IN_VMEM),
         scratch_shapes=[pltpu.VMEM((heads, tokens, width), LOW)] * 3
         + [pltpu.SemaphoreType.DMA((3, heads))],
@@ -269,15 +277,7 @@
             transcendentals=0,
         ),
         name="far",
-    )(
-        *[
-            in_vmem(x)
-            for x in (
-                k_v, v_v, g_v, w_v, qt, got_1,
-                jnp.concatenate(own_half, 0), jnp.concatenate(other_half, 0), *flat_near,
-            )
-        ]
-    )
+    )(*[in_vmem(x) for x in operands])
 
 
 def solution(mesh):

time: 35.5 us -> 28.3 us (0.80)
  local copies, waits for them, and re-layouts: 5 us -> 0.01 us
  waiting for transfers between devices: 8.76 us -> 5.48 us
  Pallas kernels: 8.16 us -> 9.42 us
    unnamed x10 -> x0, local copies, waits for them, and re-layouts: 5 us -> none
    ppermute x8, waiting for transfers between devices: 8.76 us -> 5.48 us  [flip(): return lax.ppermute(block, AXES, [(i, i ^ mask) for i in range(size)])]
    pallas_call x1, Pallas kernels: 2.62 us -> 3.81 us  [on_device(): pl.pallas_call(functools.partial(state_kernel, bits, scales), out_shape=(...]
  transfers between devices with their start and end apart: 8 -> 8, of which waited for: 4 -> 5; matrix products, arithmetic and copies ran while one was open for 0% -> 0% of each run, Pallas kernels for 8% -> 10%
where the time goes in v2:
time: 28.3 us; the launch traced here: 28.1 us
  starting transfers between devices  12.5 us (44%)
  Pallas kernels  9.42 us (33%)
  waiting for transfers between devices  5.48 us (19%)
  between operations  0.67 us (2%)
    ppermute x8, starting transfers between devices, flip(): return lax.ppermute(block, AXES, [(i, i ^ mask) for i in range(size)])  12.5 us
    ppermute x8, waiting for transfers between devices, flip(): return lax.ppermute(block, AXES, [(i, i ^ mask) for i in range(size)])  5.48 us
    pallas_call x1, Pallas kernels, on_device(): pl.pallas_call(functools.partial(state_kernel, bits, scales), out_shape=(...  3.81 us
    pallas_call x1, Pallas kernels, on_device(): pl.pallas_call(functools.partial(far_kernel, bits, scales, split), out_sh...  2.86 us
    pallas_call x2, Pallas kernels, near(): pl.pallas_call(functools.partial(near_kernel, first, scales[0]), out_shap...  2.76 us
  transfers between devices with their start and end apart: 8, of which 5 were waited for; matrix products, arithmetic and copies ran while one was open for 0% of the time, Pallas kernels for 10%

profile of v2, /device:TPU:0, one launch (start us, length us, event | category | flops | bytes accessed | tf_op | source)
XLA Modules:
  0.0 28.1 jit_solution(1972825597763697975)
XLA Ops:
  0.6 3.8 %states.1 = (bf16[4,512,128]{2,1,0:T(8,128)(2,1)S(1)}, bf16[4,512,128]{2,1,0:T(8,128)(2,1)S(1)}, bf16[4,512,128]{2,1,0:T(8,128)(2,1)S(1)}, bf16[4,512,128]{2,1,0...) custom-call(bf16[512,512]{1,0:T(8,128)(2,1)} %q_hbm.1, ...), custom_call_target="tpu_custom_call" | custom-call | flops 268435456 | bytes 2097152 | tf_op jit(solution)/shard_map/states/pallas_call | solution.py:200
  4.5 3.1 %collective-permute-start.3 = (bf16[2,128,128]{2,1,0:T(8,128)(2,1)S(1)}, bf16[2,128,128]{2,1,0:T(8,128)(2,1)S(1)}, u32[]{:S(2)}, u32[]{:S(2)}) collective-permute-start(bf16[2,128,128]{2,1,0:T(8,128)(2,1)S(1)} %slice.15), channel_id=1, source_target_pairs={{0,4},{2,6},{4,0},{6,2},{8,12},{10,14},{12,8},{14,10},{1,5},{3,7},... | collective-permute-start | bytes 196616 | tf_op jit(solution)/shard_map/ppermute | solution.py:28
  7.6 1.4 %collective-permute-start.4 = (bf16[2,128,128]{2,1,0:T(8,128)(2,1)S(1)}, bf16[2,128,128]{2,1,0:T(8,128)(2,1)S(1)}, u32[]{:S(2)}, u32[]{:S(2)}) collective-permute-start(bf16[2,128,128]{2,1,0:T(8,128)(2,1)S(1)} %get-tuple-element.35), channel_id=1, source_target_pairs={{0,6},{2,4},{4,2},{6,0},{8,14},{10,12},{12,10},{14,8},{1,7},{3,5},... | collective-permute-start | bytes 196616 | tf_op jit(solution)/shard_map/ppermute | solution.py:28
  8.9 0.2 collective-permute-start.1
  9.1 1.4 %near.2 = (f32[2,128,512]{2,1,0:T(8,128)S(1)}, f32[2,512,128]{2,1,0:T(8,128)S(1)}, f32[2,512,128]{2,1,0:T(8,128)S(1)}, f32[2,1,512]{2,1,0:T(1,128)S(1)}, bf16[4,128,128]{2,1,0:T(8,128)(2,1)S(1)}) custom-call(bf16[4,512,128]{2,1,0:T(8,128)(2,1)S(1)} %get-tuple-element.29.q_ref, bf16[4,512,128]{2,1,0:T(8,128)(2,1)S(1)} %get-tuple-element.24.k_ref.refs_0_, ...), custom_call_target="tpu_custom_call" | custom-call | flops 67108864000 | bytes 2621440 | tf_op jit(solution)/shard_map/near/pallas_call | solution.py:224
  10.5 1.9 %collective-permute-start = (bf16[4,128,128]{2,1,0:T(8,128)(2,1)S(1)}, bf16[4,128,128]{2,1,0:T(8,128)(2,1)S(1)}, u32[]{:S(2)}, u32[]{:S(2)}) collective-permute-start(bf16[4,128,128]{2,1,0:T(8,128)(2,1)S(1)} %get-tuple-element.32), channel_id=1, source_target_pairs={{0,2},{2,0},{4,6},{6,4},{8,10},{10,8},{12,14},{14,12},{1,3},{3,1},... | collective-permute-start | bytes 393224 | tf_op jit(solution)/shard_map/ppermute | solution.py:28
  12.4 0.0 collective-permute-done.3
  12.4 0.4 %collective-permute-done.4 = bf16[2,128,128]{2,1,0:T(8,128)(2,1)S(1)} collective-permute-done((bf16[2,128,128]{2,1,0:T(8,128)(2,1)S(1)}, bf16[2,128,128]{2,1,0:T(8,128)(2,1)S(1)}, u32[]{:S(2)}, u32[]{:S(2)}) %collective-permute-start.4) | collective-permute-done | bytes 65568 | tf_op jit(solution)/shard_map/ppermute | solution.py:28
  12.8 2.9 %collective-permute-done.1 = bf16[4,128,128]{2,1,0:T(8,128)(2,1)S(1)} collective-permute-done((bf16[4,128,128]{2,1,0:T(8,128)(2,1)S(1)}, bf16[4,128,128]{2,1,0:T(8,128)(2,1)S(1)}, u32[]{:S(2)}, u32[]{:S(2)}) %collective-permute-start.1) | collective-permute-done | bytes 131104 | tf_op jit(solution)/shard_map/ppermute | solution.py:28
  15.6 0.1 add_convert_fusion
  15.7 3.1 %collective-permute-start.7 = (bf16[2,128,128]{2,1,0:T(8,128)(2,1)S(1)}, bf16[2,128,128]{2,1,0:T(8,128)(2,1)S(1)}, u32[]{:S(2)}, u32[]{:S(2)}) collective-permute-start(bf16[2,128,128]{2,1,0:T(8,128)(2,1)S(1)} %get-tuple-element.44), channel_id=1, source_target_pairs={{0,10},{2,8},{4,14},{6,12},{8,2},{10,0},{12,6},{14,4},{1,11},{3,9}... | collective-permute-start | bytes 196616 | tf_op jit(solution)/shard_map/ppermute | solution.py:28
  18.8 0.2 collective-permute-start.5
  18.9 2.0 %collective-permute-start.6 = (bf16[2,128,128]{2,1,0:T(8,128)(2,1)S(1)}, bf16[2,128,128]{2,1,0:T(8,128)(2,1)S(1)}, u32[]{:S(2)}, u32[]{:S(2)}) collective-permute-start(bf16[2,128,128]{2,1,0:T(8,128)(2,1)S(1)} %get-tuple-element.45), channel_id=1, source_target_pairs={{0,6},{2,4},{4,2},{6,0},{8,14},{10,12},{12,10},{14,8},{1,7},{3,5},... | collective-permute-start | bytes 196616 | tf_op jit(solution)/shard_map/ppermute | solution.py:28
  20.9 0.7 %collective-permute-start.2 = (bf16[2,128,128]{2,1,0:T(8,128)(2,1)S(1)}, bf16[2,128,128]{2,1,0:T(8,128)(2,1)S(1)}, u32[]{:S(2)}, u32[]{:S(2)}) collective-permute-start(bf16[2,128,128]{2,1,0:T(8,128)(2,1)S(1)} %get-tuple-element.45), channel_id=1, source_target_pairs={{0,4},{2,6},{4,0},{6,2},{8,12},{10,14},{12,8},{14,10},{1,5},{3,7},... | collective-permute-start | bytes 196616 | tf_op jit(solution)/shard_map/ppermute | solution.py:28
  21.6 1.4 %near.3 = (f32[2,128,512]{2,1,0:T(8,128)S(1)}, f32[2,512,128]{2,1,0:T(8,128)S(1)}, f32[2,512,128]{2,1,0:T(8,128)S(1)}, f32[2,1,512]{2,1,0:T(1,128)S(1)}) custom-call(bf16[4,512,128]{2,1,0:T(8,128)(2,1)S(1)} %get-tuple-element.29.q_ref, bf16[4,512,128]{2,1,0:T(8,128)(2,1)S(1)} %get-tuple-element.24.k_ref.refs_0_, ...), custom_call_target="tpu_custom_call" | custom-call | flops 67108864000 | bytes 2621440 | tf_op jit(solution)/shard_map/near/pallas_call | solution.py:224
  23.0 0.0 collective-permute-done.refs_5_
  23.0 1.0 %collective-permute-done.7.refs_9_ = bf16[2,128,128]{2,1,0:T(8,128)(2,1)S(1)} collective-permute-done((bf16[2,128,128]{2,1,0:T(8,128)(2,1)S(1)}, bf16[2,128,128]{2,1,0:T(8,128)(2,1)S(1)}, u32[]{:S(2)}, u32[]{:S(2)}) %collective-permute-start.7) | collective-permute-done | bytes 65568 | tf_op jit(solution)/shard_map/ppermute | solution.py:28
  24.0 0.1 collective-permute-done.5.refs_7_
  24.1 1.1 %collective-permute-done.6.refs_8_ = bf16[2,128,128]{2,1,0:T(8,128)(2,1)S(1)} collective-permute-done((bf16[2,128,128]{2,1,0:T(8,128)(2,1)S(1)}, bf16[2,128,128]{2,1,0:T(8,128)(2,1)S(1)}, u32[]{:S(2)}, u32[]{:S(2)}) %collective-permute-start.6) | collective-permute-done | bytes 65568 | tf_op jit(solution)/shard_map/ppermute | solution.py:28
  25.3 0.0 collective-permute-done.2.refs_6_
  25.3 2.9 %far.1 = (bf16[512,512]{1,0:T(8,128)(2,1)}, bf16[512,512]{1,0:T(8,128)(2,1)}, bf16[512,512]{1,0:T(8,128)(2,1)}, f32[4,8,512]{2,1,0:T(8,128)}) custom-call(bf16[4,512,128]{2,1,0:T(8,128)(2,1)S(1)} %get-tuple-element.24.k_ref.refs_0_, bf16[4,512,128]{2,1,0:T(8,128)(2,1)S(1)} %get-tuple-element.25.v_ref.refs_1_, ...), custom_call_target="tpu_custom_call" | custom-call | flops 335544320 | bytes 1572864 | tf_op jit(solution)/shard_map/far/pallas_call | solution.py:266
  (1 shorter events, 0.0 us)
Async XLA Ops:
  4.5 7.9 %collective-permute-start.3 = (bf16[2,128,128]{2,1,0:T(8,128)(2,1)S(1)}, bf16[2,128,128]{2,1,0:T(8,128)(2,1)S(1)}, u32[]{:S(2)}, u32[]{:S(2)}) collective-permute-start(bf16[2,128,128]{2,1,0:T(8,128)(2,1)S(1)} %slice.15), channel_id=1, source_target_pairs={{0,4},{2,6},{4,0},{6,2},{8,12},{10,14},{12,8},{14,10},{1,5},{3,7},... | collective-permute-start | bytes 196616 | tf_op jit(solution)/shard_map/ppermute | solution.py:28
  7.6 5.2 %collective-permute-start.4 = (bf16[2,128,128]{2,1,0:T(8,128)(2,1)S(1)}, bf16[2,128,128]{2,1,0:T(8,128)(2,1)S(1)}, u32[]{:S(2)}, u32[]{:S(2)}) collective-permute-start(bf16[2,128,128]{2,1,0:T(8,128)(2,1)S(1)} %get-tuple-element.35), channel_id=1, source_target_pairs={{0,6},{2,4},{4,2},{6,0},{8,14},{10,12},{12,10},{14,8},{1,7},{3,5},... | collective-permute-start | bytes 196616 | tf_op jit(solution)/shard_map/ppermute | solution.py:28
  8.9 6.7 %collective-permute-start.1 = (bf16[4,128,128]{2,1,0:T(8,128)(2,1)S(1)}, bf16[4,128,128]{2,1,0:T(8,128)(2,1)S(1)}, u32[]{:S(2)}, u32[]{:S(2)}) collective-permute-start(bf16[4,128,128]{2,1,0:T(8,128)(2,1)S(1)} %get-tuple-element.34), channel_id=1, source_target_pairs={{0,2},{2,0},{4,6},{6,4},{8,10},{10,8},{12,14},{14,12},{1,3},{3,1},... | collective-permute-start | bytes 393224 | tf_op jit(solution)/shard_map/ppermute | solution.py:28
  10.5 12.5 %collective-permute-start = (bf16[4,128,128]{2,1,0:T(8,128)(2,1)S(1)}, bf16[4,128,128]{2,1,0:T(8,128)(2,1)S(1)}, u32[]{:S(2)}, u32[]{:S(2)}) collective-permute-start(bf16[4,128,128]{2,1,0:T(8,128)(2,1)S(1)} %get-tuple-element.32), channel_id=1, source_target_pairs={{0,2},{2,0},{4,6},{6,4},{8,10},{10,8},{12,14},{14,12},{1,3},{3,1},... | collective-permute-start | bytes 393224 | tf_op jit(solution)/shard_map/ppermute | solution.py:28
  15.7 8.3 %collective-permute-start.7 = (bf16[2,128,128]{2,1,0:T(8,128)(2,1)S(1)}, bf16[2,128,128]{2,1,0:T(8,128)(2,1)S(1)}, u32[]{:S(2)}, u32[]{:S(2)}) collective-permute-start(bf16[2,128,128]{2,1,0:T(8,128)(2,1)S(1)} %get-tuple-element.44), channel_id=1, source_target_pairs={{0,10},{2,8},{4,14},{6,12},{8,2},{10,0},{12,6},{14,4},{1,11},{3,9}... | collective-permute-start | bytes 196616 | tf_op jit(solution)/shard_map/ppermute | solution.py:28
  18.8 5.3 %collective-permute-start.5 = (bf16[2,128,128]{2,1,0:T(8,128)(2,1)S(1)}, bf16[2,128,128]{2,1,0:T(8,128)(2,1)S(1)}, u32[]{:S(2)}, u32[]{:S(2)}) collective-permute-start(bf16[2,128,128]{2,1,0:T(8,128)(2,1)S(1)} %get-tuple-element.44), channel_id=1, source_target_pairs={{0,8},{2,10},{4,12},{6,14},{8,0},{10,2},{12,4},{14,6},{1,9},{3,11}... | collective-permute-start | bytes 196616 | tf_op jit(solution)/shard_map/ppermute | solution.py:28
  18.9 6.3 %collective-permute-start.6 = (bf16[2,128,128]{2,1,0:T(8,128)(2,1)S(1)}, bf16[2,128,128]{2,1,0:T(8,128)(2,1)S(1)}, u32[]{:S(2)}, u32[]{:S(2)}) collective-permute-start(bf16[2,128,128]{2,1,0:T(8,128)(2,1)S(1)} %get-tuple-element.45), channel_id=1, source_target_pairs={{0,6},{2,4},{4,2},{6,0},{8,14},{10,12},{12,10},{14,8},{1,7},{3,5},... | collective-permute-start | bytes 196616 | tf_op jit(solution)/shard_map/ppermute | solution.py:28
  20.9 4.4 %collective-permute-start.2 = (bf16[2,128,128]{2,1,0:T(8,128)(2,1)S(1)}, bf16[2,128,128]{2,1,0:T(8,128)(2,1)S(1)}, u32[]{:S(2)}, u32[]{:S(2)}) collective-permute-start(bf16[2,128,128]{2,1,0:T(8,128)(2,1)S(1)} %get-tuple-element.45), channel_id=1, source_target_pairs={{0,4},{2,6},{4,0},{6,2},{8,12},{10,14},{12,8},{14,10},{1,5},{3,7},... | collective-permute-start | bytes 196616 | tf_op jit(solution)/shard_map/ppermute | solution.py:28

commit v3 on v2

v3 whole, which is shorter than its diff:
```python
import functools
import math

import jax
import jax.numpy as jnp
from jax import lax
from jax.experimental import pallas as pl
from jax.experimental.pallas import tpu as pltpu
from jax.sharding import PartitionSpec as P

AXES = ("seq", "heads")
LOW = jnp.bfloat16
ROWS = 256


def nt(left, right):
    return lax.dot_general(
        left, right, (((1,), (1,)), ((), ())), preferred_element_type=jnp.float32
    )


def nn(left, right):
    return jnp.dot(left, right, preferred_element_type=jnp.float32)


def flip(block, mask):
    size = lax.axis_size(AXES)
    return lax.ppermute(block, AXES, [(i, i ^ mask) for i in range(size)])


def block_index():
    return lax.axis_index("seq") * lax.axis_size("heads") + lax.axis_index("heads")


def in_vmem(array):
    return pltpu.with_memory_space_constraint(array, pltpu.VMEM)


def level_scales(width, tokens, count):
    base = 1.0 / math.sqrt(width * tokens)
    return [base] + [base / math.sqrt(2.0 ** (level - 1)) for level in range(1, count)]


def state_kernel(
    bits, scales, q_hbm, k_hbm, v_hbm, g_hbm, w_hbm,
    q_out, k_out, v_out, g_out, w_out, qt_out, kt_out, state_out, own_out, other_out, sems, w_sem,
):
    heads, tokens, width = q_out.shape
    half = heads // 2
    pairs = ((q_hbm, q_out), (k_hbm, k_out), (v_hbm, v_out), (g_hbm, g_out))
    w_copy = pltpu.make_async_copy(w_hbm, w_out, w_sem)
    copies = [
        [
            pltpu.make_async_copy(src.at[:, pl.ds(h * width, width)], dst.at[h], sems.at[i, h])
            for i, (src, dst) in enumerate(pairs)
        ]
        for h in range(heads)
    ]
    for copy in copies[0]:
        copy.start()
    w_copy.start()
    for group in copies[1:]:
        for copy in group:
            copy.start()
    place = block_index()
    low_bit = place & 1
    for h in range(heads):
        for copy in copies[h]:
            copy.wait()
        if h == 0:
            w_copy.wait()
        query_t = q_out[h].T
        key_t = k_out[h].T
        qt_out[h] = query_t
        kt_out[h] = key_t
        state = nn(key_t, v_out[h])
        state_out[h] = state.astype(LOW)
        query_f = query_t.astype(jnp.float32)
        scaled = [
            (w_out[h, pl.ds(level, 1), :] * query_f).astype(LOW) for level in range(2, bits + 1)
        ]
        grads = nn(jnp.concatenate(scaled, 0), g_out[h])
        mixed = []
        for level in range(2, bits + 1):
            upper = ((place >> (level - 1)) & 1) == 1
            row = (level - 2) * width
            mixed.append(jnp.where(upper, scales[level] * grads[row : row + width], state).astype(LOW))

        @pl.when(low_bit == h // half)
        def _():
            for i, block in enumerate(mixed):
                own_out[i * half + h % half] = block

        @pl.when(low_bit != h // half)
        def _():
            for i, block in enumerate(mixed):
                other_out[i * half + h % half] = block


def first_level_kernel(
    scale, g_ref, w_ref, qt_ref, state_ref, own_ref, other_ref, d1_out, near_out, far_out
):
    heads = g_ref.shape[0]
    half = heads // 2
    near_out[...] = own_ref[half:]
    far_out[...] = other_ref[half:]
    upper = (block_index() & 1) == 1
    for h in range(heads):
        scaled = (w_ref[h, pl.ds(1, 1), :] * qt_ref[h].astype(jnp.float32)).astype(LOW)
        state = state_ref[h]
        d1_out[h] = jnp.where(upper, (scale * nn(scaled, g_ref[h])).astype(LOW), state)


def near_head(scale, h, q_ref, k_ref, v_ref, g_ref, w_ref, kt_ref, nk_out, nv_out, local):
    width, tokens = kt_ref.shape[1:]
    rows = min(ROWS, tokens)
    factor = scale * w_ref[h, pl.ds(0, 1), :]
    back, weight = [], []
    for start in range(0, tokens, rows):
        left = tokens - start
        key = k_ref[h, start : start + rows, :]
        value = v_ref[h, start : start + rows, :]
        query = q_ref[h, start:, :]
        grad = g_ref[h, start:, :]
        scores = nt(key, query)
        dots = nt(value, grad)
        allowed = lax.broadcasted_iota(jnp.int32, (rows, left), 0) <= lax.broadcasted_iota(
            jnp.int32, (rows, left), 1
        )
        scores = jnp.where(allowed, scores, 0.0)
        dots = jnp.where(allowed, dots, 0.0)
        part = jnp.sum(scores * dots, axis=0, keepdims=True)
        now = factor[:, start:]
        grad_mix = (now * dots).astype(LOW)
        score_mix = (now * scores).astype(LOW)
        nk_out[local, start : start + rows, :] = nn(grad_mix, query)
        nv_out[local, start : start + rows, :] = nn(score_mix, grad)
        back.append(nn(kt_ref[h, :, start : start + rows], grad_mix))
        weight.append(scale * part)
    return back, weight


def store_sums(ref, h, rows, parts):
    tokens = parts[0].shape[1]
    for i, part in enumerate(parts):
        start = tokens - part.shape[1]
        if i == 0:
            ref[h, rows, :] = part
        else:
            ref[h, rows, start:] += part


def early_kernel(count, scale, *refs):
    ins, (d1_ref, nq_out, nk_out, nv_out, nw_out, d1_out) = refs[:6], refs[6:]
    d1_out[...] = d1_ref[...]
    for h in range(count):
        back, weight = near_head(scale, h, *ins, nk_out, nv_out, h)
        store_sums(nq_out, h, slice(None), back)
        store_sums(nw_out, h, slice(None), weight)


def late_kernel(count, scales, *refs):
    ins, refs = refs[:6], refs[6:]
    qt_ref, r1_ref, nq_ref, nw_ref, sum_out, gw_out, nk_out, nv_out = refs
    g_ref, w_ref = ins[3], ins[4]
    heads = sum_out.shape[0]
    upper = (block_index() & 1) == 1
    for h in range(heads):
        gw_out[h] = jnp.zeros(gw_out.shape[1:], jnp.float32)
        if h < count:
            sum_out[h] = nq_ref[h]
            gw_out[h, pl.ds(0, 1), :] = nw_ref[h]
        else:
            back, weight = near_head(scales[0], h, *ins, nk_out, nv_out, h - count)
            store_sums(sum_out, h, slice(None), back)
            store_sums(gw_out, h, pl.ds(0, 1), weight)
        add_level(scales[1], h, 1, jnp.where(upper, r1_ref[h], 0), g_ref, w_ref, qt_ref, sum_out, gw_out)


def add_level(scale, h, level, sibling, g_ref, w_ref, qt_ref, sum_ref, gw_ref):
    products = nt(sibling, g_ref[h])
    sum_ref[h] += (scale * w_ref[h, pl.ds(level, 1), :]) * products
    gw_ref[h, pl.ds(level, 1), :] = scale * jnp.sum(
        products * qt_ref[h].astype(jnp.float32), axis=0, keepdims=True
    )


def far_kernel(bits, scales, count, *refs):
    k_ref, v_ref, g_ref, w_ref, qt_ref, sum_ref, weight_ref, r1_ref = refs[:8]
    early, late, refs = refs[8:10], refs[10:12], refs[12:]
    own_refs, other_refs, refs = refs[: bits - 1], refs[bits - 1 : 2 * bits - 2], refs[2 * bits - 2 :]
    gq_hbm, gk_hbm, gv_hbm, gw_hbm, gq_buf, gk_buf, gv_buf, gw_buf, sems, w_sem = refs
    heads, tokens, width = k_ref.shape
    half = heads // 2
    place = block_index()
    low_bit = place & 1
    copies = []
    gw_buf[...] = weight_ref[...]
    for h in range(heads):
        nk_ref, nv_ref = early if h < count else late
        local = h if h < count else h - count
        grad = g_ref[h]
        query_t = qt_ref[h].astype(jnp.float32)
        reverse = jnp.where(low_bit == 1, 0, r1_ref[h]).astype(jnp.float32)
        total = sum_ref[h]
        for level in range(2, bits + 1):
            own_ref, other_ref = own_refs[level - 2], other_refs[level - 2]
            got = jnp.where(low_bit == h // half, own_ref[h % half], other_ref[h % half])
            upper = ((place >> (level - 1)) & 1) == 1
            sibling = jnp.where(upper, got, 0)
            reverse = reverse + jnp.where(upper, 0, got).astype(jnp.float32)
            products = nt(sibling, grad)
            total = total + (scales[level] * w_ref[h, pl.ds(level, 1), :]) * products
            gw_buf[h, pl.ds(level, 1), :] = scales[level] * jnp.sum(
                products * query_t, axis=0, keepdims=True
            )
        low = reverse.astype(LOW)
        gq_buf[h] = total.astype(LOW).T
        gk_buf[h] = (nk_ref[local] + nt(v_ref[h], low)).astype(LOW)
        gv_buf[h] = (nv_ref[local] + nn(k_ref[h], low)).astype(LOW)
        for i, (buf, hbm) in enumerate(((gq_buf, gq_hbm), (gk_buf, gk_hbm), (gv_buf, gv_hbm))):
            copy = pltpu.make_async_copy(buf.at[h], hbm.at[:, pl.ds(h * width, width)], sems.at[i, h])
            copy.start()
            copies.append(copy)
    copy = pltpu.make_async_copy(gw_buf, gw_hbm, w_sem)
    copy.start()
    copies.append(copy)
    for copy in copies:
        copy.wait()


ANY = pl.BlockSpec(memory_space=pl.ANY)
IN_VMEM = pl.BlockSpec(memory_space=pltpu.VMEM)
LIMIT = 16 * 1024 * 1024
EARLY = 1


def call(kernel, name, flops, out_shape, operands):
    outs = [pltpu.VMEM(shape, dtype) for shape, dtype in out_shape]
    return pl.pallas_call(
        kernel,
        out_shape=outs,
        in_specs=[IN_VMEM] * len(operands),
        out_specs=[IN_VMEM] * len(outs),
        compiler_params=pltpu.CompilerParams(vmem_limit_bytes=LIMIT),
        cost_estimate=pl.CostEstimate(flops=flops, bytes_accessed=0, transcendentals=0),
        name=name,
    )(*[in_vmem(x) for x in operands])


def on_device(queries, keys, values, out_grad, level_weights):
    tokens = queries.shape[0]
    heads, levels, _ = level_weights.shape
    width = queries.shape[1] // heads
    half = heads // 2
    bits = lax.axis_size(AXES).bit_length() - 1
    scales = level_scales(width, tokens, levels)
    by_head = pltpu.VMEM((heads, tokens, width), LOW)
    by_head_t = pltpu.VMEM((heads, width, tokens), LOW)
    halves = (bits - 1) * half
    f32 = jnp.float32
    near_flops = 1000 * tokens * tokens * width
    (q_v, k_v, v_v, g_v, w_v, qt, kt, state, own, other) = pl.pallas_call(
        functools.partial(state_kernel, bits, scales),
        out_shape=(
            by_head, by_head, by_head, by_head,
            pltpu.VMEM((heads, levels, tokens), jnp.float32),
            by_head_t, by_head_t,
            pltpu.VMEM((heads, width, width), LOW),
            pltpu.VMEM((halves, width, width), LOW),
            pltpu.VMEM((halves, width, width), LOW),
        ),
        in_specs=[ANY] * 5,
        out_specs=(IN_VMEM,) * 10,
        scratch_shapes=[pltpu.SemaphoreType.DMA((4, heads)), pltpu.SemaphoreType.DMA],
        compiler_params=pltpu.CompilerParams(vmem_limit_bytes=LIMIT),
        cost_estimate=pl.CostEstimate(
            flops=2 * heads * (bits + 1) * tokens * width * width,
            bytes_accessed=4 * heads * tokens * width * 2,
            transcendentals=0,
        ),
        name="states",
    )(*[pltpu.with_memory_space_constraint(x, pltpu.HBM) for x in (queries, keys, values, out_grad, level_weights)])
    got_x = flip(other, 1)
    rest = ((halves - half, width, width), LOW)
    full = ((heads, width, width), LOW)
    d1, mine, far = call(
        functools.partial(first_level_kernel, scales[1]), "first_level", near_flops,
        [full, rest, rest], [g_v, w_v, qt, state, own, other],
    )
    ins = [q_v, k_v, v_v, g_v, w_v, kt]
    nq, nk_a, nv_a, nw, d1 = call(
        functools.partial(early_kernel, EARLY, scales[0]), "near_early", near_flops,
        [
            ((EARLY, width, tokens), f32), ((EARLY, tokens, width), f32),
            ((EARLY, tokens, width), f32), ((EARLY, 1, tokens), f32), full,
        ],
        [*ins, d1],
    )
    got_1 = flip(d1, 1)
    got_z = flip(mine, 2)
    got_d = flip(far, 3)
    as_f = lambda x: x.astype(jnp.float32)
    pair = (as_f(own[:half]) + as_f(got_x[:half])).astype(LOW)
    quad = as_f(own[half:]) + as_f(got_x[half:]) + as_f(got_z) + as_f(got_d)
    sums = [pair]
    for bit in range(2, bits):
        sums.append(quad[:half].astype(LOW))
        quad = quad[half:]
        if bit < bits - 1:
            quad = quad + as_f(flip(quad.astype(LOW), 1 << bit))
    own_half = [flip(x, 1 << (i + 1)) for i, x in enumerate(sums)]
    other_half = [flip(x, (1 << (i + 1)) ^ 1) for i, x in enumerate(sums)]
    later = heads - EARLY
    total, weights, nk_b, nv_b = call(
        functools.partial(late_kernel, EARLY, scales), "near_late", near_flops,
        [
            ((heads, width, tokens), f32), ((heads, levels, tokens), f32),
            ((later, tokens, width), f32), ((later, tokens, width), f32),
        ],
        [*ins, qt, got_1, nq, nw],
    )
    operands = [k_v, v_v, g_v, w_v, qt, total, weights, got_1, nk_a, nv_a, nk_b, nv_b]
    operands += [*own_half, *other_half]
    out = jax.ShapeDtypeStruct((tokens, heads * width), LOW)
    return pl.pallas_call(
        functools.partial(far_kernel, bits, scales, EARLY),
        out_shape=(out, out, out, jax.ShapeDtypeStruct((heads, levels, tokens), jnp.float32)),
        in_specs=[IN_VMEM] * len(operands),
        out_specs=(ANY,) * 4,
        scratch_shapes=[pltpu.VMEM((heads, tokens, width), LOW)] * 3
        + [
            pltpu.VMEM((heads, levels, tokens), jnp.float32),
            pltpu.SemaphoreType.DMA((3, heads)),
            pltpu.SemaphoreType.DMA,
        ],
        compiler_params=pltpu.CompilerParams(vmem_limit_bytes=LIMIT),
        cost_estimate=pl.CostEstimate(
            flops=2 * heads * (bits + 2) * tokens * width * width,
            bytes_accessed=3 * heads * tokens * width * 2,
            transcendentals=0,
        ),
        name="far",
    )(*[in_vmem(x) for x in operands])


def solution(mesh):
    rows = P(("groups", "seq", "heads"), "sub")
    weights = P("sub", None, ("groups", "seq", "heads"))
    return jax.shard_map(
        on_device,
        mesh=mesh,
        in_specs=(rows, rows, rows, rows, weights),
        out_specs=(rows, rows, rows, weights),
        check_vma=False,
    )
```

time: 28.3 us -> 25.4 us (0.90)
  waiting for transfers between devices: 5.48 us -> 3.77 us
  Pallas kernels: 9.42 us -> 8.24 us
    ppermute x8, waiting for transfers between devices: 5.48 us -> 3.77 us  [flip(): return lax.ppermute(block, AXES, [(i, i ^ mask) for i in range(size)])]
    pallas_call x1, Pallas kernels: 3.81 us -> 3.07 us  [on_device(): pl.pallas_call(functools.partial(state_kernel, bits, scales), out_shape=(...]
    pallas_call x3 -> x4, Pallas kernels: 5.61 us -> 5.17 us  [the longest x3 3.32 us: call(): pl.pallas_call(kernel, out_shape=outs, in_specs=[IN_VMEM] * len(operands)...]
  transfers between devices with their start and end apart: 8 -> 8, of which waited for: 5 -> 4; matrix products, arithmetic and copies ran while one was open for 0% -> 0% of each run, Pallas kernels for 10% -> 13%
where the time goes in v3:
time: 25.4 us; the launch traced here: 25.3 us
  starting transfers between devices  12.5 us (49%)
  Pallas kernels  8.24 us (32%)
  waiting for transfers between devices  3.77 us (15%)
  between operations  0.68 us (3%)
    ppermute x8, starting transfers between devices, flip(): return lax.ppermute(block, AXES, [(i, i ^ mask) for i in range(size)])  12.5 us
    ppermute x8, waiting for transfers between devices, flip(): return lax.ppermute(block, AXES, [(i, i ^ mask) for i in range(size)])  3.77 us
    pallas_call x3, Pallas kernels, call(): pl.pallas_call(kernel, out_shape=outs, in_specs=[IN_VMEM] * len(operands)...  3.32 us
    pallas_call x1, Pallas kernels, on_device(): pl.pallas_call(functools.partial(state_kernel, bits, scales), out_shape=(...  3.07 us
    pallas_call x1, Pallas kernels, on_device(): pl.pallas_call(functools.partial(far_kernel, bits, scales, EARLY), out_sh...  1.85 us
  transfers between devices with their start and end apart: 8, of which 4 were waited for; matrix products, arithmetic and copies ran while one was open for 0% of the time, Pallas kernels for 13%

profile of v3, /device:TPU:0, one launch (start us, length us, event | category | flops | bytes accessed | tf_op | source)
XLA Modules:
  0.0 25.3 jit_solution(16039333666853012168)
XLA Ops:
  0.6 3.1 %states.1 = (bf16[4,512,128]{2,1,0:T(8,128)(2,1)S(1)}, bf16[4,512,128]{2,1,0:T(8,128)(2,1)S(1)}, bf16[4,512,128]{2,1,0:T(8,128)(2,1)S(1)}, bf16[4,512,128]{2,1,0...) custom-call(bf16[512,512]{1,0:T(8,128)(2,1)} %q_hbm.1, ...), custom_call_target="tpu_custom_call" | custom-call | flops 268435456 | bytes 2097152 | tf_op jit(solution)/shard_map/states/pallas_call | solution.py:263
  3.7 3.0 %collective-permute-start.1 = (bf16[4,128,128]{2,1,0:T(8,128)(2,1)S(1)}, bf16[4,128,128]{2,1,0:T(8,128)(2,1)S(1)}, u32[]{:S(2)}, u32[]{:S(2)}) collective-permute-start(bf16[4,128,128]{2,1,0:T(8,128)(2,1)S(1)} %get-tuple-element.35.other_ref), channel_id=1, source_target_pairs={{0,2},{2,0},{4,6},{6,4},{8,10},{10,8},{12,14},{14,12},{1,3},{3,1},... | collective-permute-start | bytes 393224 | tf_op jit(solution)/shard_map/ppermute | solution.py:28
  6.7 0.3 %first_level.1 = (bf16[4,128,128]{2,1,0:T(8,128)(2,1)S(1)}, bf16[2,128,128]{2,1,0:T(8,128)(2,1)S(1)}, bf16[2,128,128]{2,1,0:T(8,128)(2,1)S(1)}) custom-call(bf16[4,512,128]{2,1,0:T(8,128)(2,1)S(1)} %get-tuple-element.28.g_ref.refs_3_.refs_2_, f32[4,8,512]{2,1,0:T(8,128)S(1)} %get-tuple-element.29.w_ref.refs_4_.refs_3_, ...), custom_call_target="tpu_custom_call" | custom-call | flops 33554432000 | tf_op jit(solution)/shard_map/first_level/pallas_call | solution.py:240
  7.0 1.6 %collective-permute-start.3 = (bf16[2,128,128]{2,1,0:T(8,128)(2,1)S(1)}, bf16[2,128,128]{2,1,0:T(8,128)(2,1)S(1)}, u32[]{:S(2)}, u32[]{:S(2)}) collective-permute-start(bf16[2,128,128]{2,1,0:T(8,128)(2,1)S(1)} %get-tuple-element.46), channel_id=1, source_target_pairs={{0,4},{2,6},{4,0},{6,2},{8,12},{10,14},{12,8},{14,10},{1,5},{3,7},... | collective-permute-start | bytes 196616 | tf_op jit(solution)/shard_map/ppermute | solution.py:28
  8.7 0.1 collective-permute-start.4
  8.7 0.8 %near_early.1 = (f32[1,128,512]{2,1,0:T(8,128)S(1)}, f32[1,512,128]{2,1,0:T(8,128)S(1)}, f32[1,512,128]{2,1,0:T(8,128)S(1)}, f32[1,1,512]{2,1,0:T(1,128)S(1)}, bf16[4,128,128]{2,1,0:T(8,128)(2,1)S(1)}) custom-call(bf16[4,512,128]{2,1,0:T(8,128)(2,1)S(1)} %get-tuple-element.31.refs_0_, bf16[4,512,128]{2,1,0:T(8,128)(2,1)S(1)} %get-tuple-element.26.refs_1_.refs_0_, ...), custom_call_target="tpu_custom_call" | custom-call | flops 33554432000 | tf_op jit(solution)/shard_map/near_early/pallas_call | solution.py:240
  9.5 1.9 %collective-permute-start = (bf16[4,128,128]{2,1,0:T(8,128)(2,1)S(1)}, bf16[4,128,128]{2,1,0:T(8,128)(2,1)S(1)}, u32[]{:S(2)}, u32[]{:S(2)}) collective-permute-start(bf16[4,128,128]{2,1,0:T(8,128)(2,1)S(1)} %get-tuple-element.37), channel_id=1, source_target_pairs={{0,2},{2,0},{4,6},{6,4},{8,10},{10,8},{12,14},{14,12},{1,3},{3,1},... | collective-permute-start | bytes 393224 | tf_op jit(solution)/shard_map/ppermute | solution.py:28
  11.5 0.4 %collective-permute-done.3 = bf16[2,128,128]{2,1,0:T(8,128)(2,1)S(1)} collective-permute-done((bf16[2,128,128]{2,1,0:T(8,128)(2,1)S(1)}, bf16[2,128,128]{2,1,0:T(8,128)(2,1)S(1)}, u32[]{:S(2)}, u32[]{:S(2)}) %collective-permute-start.3) | collective-permute-done | bytes 65568 | tf_op jit(solution)/shard_map/ppermute | solution.py:28
  11.9 2.0 %collective-permute-done.4 = bf16[2,128,128]{2,1,0:T(8,128)(2,1)S(1)} collective-permute-done((bf16[2,128,128]{2,1,0:T(8,128)(2,1)S(1)}, bf16[2,128,128]{2,1,0:T(8,128)(2,1)S(1)}, u32[]{:S(2)}, u32[]{:S(2)}) %collective-permute-start.4) | collective-permute-done | bytes 65568 | tf_op jit(solution)/shard_map/ppermute | solution.py:28
  13.9 0.0 collective-permute-done.1
  13.9 0.1 add_convert_fusion
  14.0 2.6 %collective-permute-start.7 = (bf16[2,128,128]{2,1,0:T(8,128)(2,1)S(1)}, bf16[2,128,128]{2,1,0:T(8,128)(2,1)S(1)}, u32[]{:S(2)}, u32[]{:S(2)}) collective-permute-start(bf16[2,128,128]{2,1,0:T(8,128)(2,1)S(1)} %get-tuple-element.48), channel_id=1, source_target_pairs={{0,10},{2,8},{4,14},{6,12},{8,2},{10,0},{12,6},{14,4},{1,11},{3,9}... | collective-permute-start | bytes 196616 | tf_op jit(solution)/shard_map/ppermute | solution.py:28
  16.6 0.3 %collective-permute-start.5 = (bf16[2,128,128]{2,1,0:T(8,128)(2,1)S(1)}, bf16[2,128,128]{2,1,0:T(8,128)(2,1)S(1)}, u32[]{:S(2)}, u32[]{:S(2)}) collective-permute-start(bf16[2,128,128]{2,1,0:T(8,128)(2,1)S(1)} %get-tuple-element.48), channel_id=1, source_target_pairs={{0,8},{2,10},{4,12},{6,14},{8,0},{10,2},{12,4},{14,6},{1,9},{3,11}... | collective-permute-start | bytes 196616 | tf_op jit(solution)/shard_map/ppermute | solution.py:28
  17.0 1.4 %collective-permute-start.6 = (bf16[2,128,128]{2,1,0:T(8,128)(2,1)S(1)}, bf16[2,128,128]{2,1,0:T(8,128)(2,1)S(1)}, u32[]{:S(2)}, u32[]{:S(2)}) collective-permute-start(bf16[2,128,128]{2,1,0:T(8,128)(2,1)S(1)} %get-tuple-element.49), channel_id=1, source_target_pairs={{0,6},{2,4},{4,2},{6,0},{8,14},{10,12},{12,10},{14,8},{1,7},{3,5},... | collective-permute-start | bytes 196616 | tf_op jit(solution)/shard_map/ppermute | solution.py:28
  18.3 1.6 %collective-permute-start.2 = (bf16[2,128,128]{2,1,0:T(8,128)(2,1)S(1)}, bf16[2,128,128]{2,1,0:T(8,128)(2,1)S(1)}, u32[]{:S(2)}, u32[]{:S(2)}) collective-permute-start(bf16[2,128,128]{2,1,0:T(8,128)(2,1)S(1)} %get-tuple-element.49), channel_id=1, source_target_pairs={{0,4},{2,6},{4,0},{6,2},{8,12},{10,14},{12,8},{14,10},{1,5},{3,7},... | collective-permute-start | bytes 196616 | tf_op jit(solution)/shard_map/ppermute | solution.py:28
  19.9 0.0 collective-permute-done.refs_7_
  19.9 2.2 %near_late.1 = (f32[4,128,512]{2,1,0:T(8,128)S(1)}, f32[4,8,512]{2,1,0:T(8,128)S(1)}, f32[3,512,128]{2,1,0:T(8,128)S(1)}, f32[3,512,128]{2,1,0:T(8,128)S(1)}) custom-call(bf16[4,512,128]{2,1,0:T(8,128)(2,1)S(1)} %get-tuple-element.31.refs_0_, bf16[4,512,128]{2,1,0:T(8,128)(2,1)S(1)} %get-tuple-element.26.refs_1_.refs_0_, ...), custom_call_target="tpu_custom_call" | custom-call | flops 33554432000 | tf_op jit(solution)/shard_map/near_late/pallas_call | solution.py:240
  22.1 0.0 collective-permute-done.7.refs_15_
  22.1 0.5 %collective-permute-done.5.refs_13_ = bf16[2,128,128]{2,1,0:T(8,128)(2,1)S(1)} collective-permute-done((bf16[2,128,128]{2,1,0:T(8,128)(2,1)S(1)}, bf16[2,128,128]{2,1,0:T(8,128)(2,1)S(1)}, u32[]{:S(2)}, u32[]{:S(2)}) %collective-permute-start.5) | collective-permute-done | bytes 65568 | tf_op jit(solution)/shard_map/ppermute | solution.py:28
  22.6 0.0 collective-permute-done.6.refs_14_
  22.6 0.8 %collective-permute-done.2.refs_12_ = bf16[2,128,128]{2,1,0:T(8,128)(2,1)S(1)} collective-permute-done((bf16[2,128,128]{2,1,0:T(8,128)(2,1)S(1)}, bf16[2,128,128]{2,1,0:T(8,128)(2,1)S(1)}, u32[]{:S(2)}, u32[]{:S(2)}) %collective-permute-start.2) | collective-permute-done | bytes 65568 | tf_op jit(solution)/shard_map/ppermute | solution.py:28
  23.4 1.8 %far.1 = (bf16[512,512]{1,0:T(8,128)(2,1)}, bf16[512,512]{1,0:T(8,128)(2,1)}, bf16[512,512]{1,0:T(8,128)(2,1)}, f32[4,8,512]{2,1,0:T(8,128)}) custom-call(bf16[4,512,128]{2,1,0:T(8,128)(2,1)S(1)} %get-tuple-element.26.refs_1_.refs_0_, bf16[4,512,128]{2,1,0:T(8,128)(2,1)S(1)} %get-tuple-element.27.refs_2_.refs_1_, ...), custom_call_target="tpu_custom_call" | custom-call | flops 335544320 | bytes 1572864 | tf_op jit(solution)/shard_map/far/pallas_call | solution.py:326
Async XLA Ops:
  3.7 10.2 %collective-permute-start.1 = (bf16[4,128,128]{2,1,0:T(8,128)(2,1)S(1)}, bf16[4,128,128]{2,1,0:T(8,128)(2,1)S(1)}, u32[]{:S(2)}, u32[]{:S(2)}) collective-permute-start(bf16[4,128,128]{2,1,0:T(8,128)(2,1)S(1)} %get-tuple-element.35.other_ref), channel_id=1, source_target_pairs={{0,2},{2,0},{4,6},{6,4},{8,10},{10,8},{12,14},{14,12},{1,3},{3,1},... | collective-permute-start | bytes 393224 | tf_op jit(solution)/shard_map/ppermute | solution.py:28
  7.0 4.9 %collective-permute-start.3 = (bf16[2,128,128]{2,1,0:T(8,128)(2,1)S(1)}, bf16[2,128,128]{2,1,0:T(8,128)(2,1)S(1)}, u32[]{:S(2)}, u32[]{:S(2)}) collective-permute-start(bf16[2,128,128]{2,1,0:T(8,128)(2,1)S(1)} %get-tuple-element.46), channel_id=1, source_target_pairs={{0,4},{2,6},{4,0},{6,2},{8,12},{10,14},{12,8},{14,10},{1,5},{3,7},... | collective-permute-start | bytes 196616 | tf_op jit(solution)/shard_map/ppermute | solution.py:28
  8.7 5.3 %collective-permute-start.4 = (bf16[2,128,128]{2,1,0:T(8,128)(2,1)S(1)}, bf16[2,128,128]{2,1,0:T(8,128)(2,1)S(1)}, u32[]{:S(2)}, u32[]{:S(2)}) collective-permute-start(bf16[2,128,128]{2,1,0:T(8,128)(2,1)S(1)} %get-tuple-element.47), channel_id=1, source_target_pairs={{0,6},{2,4},{4,2},{6,0},{8,14},{10,12},{12,10},{14,8},{1,7},{3,5},... | collective-permute-start | bytes 196616 | tf_op jit(solution)/shard_map/ppermute | solution.py:28
  9.5 10.4 %collective-permute-start = (bf16[4,128,128]{2,1,0:T(8,128)(2,1)S(1)}, bf16[4,128,128]{2,1,0:T(8,128)(2,1)S(1)}, u32[]{:S(2)}, u32[]{:S(2)}) collective-permute-start(bf16[4,128,128]{2,1,0:T(8,128)(2,1)S(1)} %get-tuple-element.37), channel_id=1, source_target_pairs={{0,2},{2,0},{4,6},{6,4},{8,10},{10,8},{12,14},{14,12},{1,3},{3,1},... | collective-permute-start | bytes 393224 | tf_op jit(solution)/shard_map/ppermute | solution.py:28
  14.0 8.1 %collective-permute-start.7 = (bf16[2,128,128]{2,1,0:T(8,128)(2,1)S(1)}, bf16[2,128,128]{2,1,0:T(8,128)(2,1)S(1)}, u32[]{:S(2)}, u32[]{:S(2)}) collective-permute-start(bf16[2,128,128]{2,1,0:T(8,128)(2,1)S(1)} %get-tuple-element.48), channel_id=1, source_target_pairs={{0,10},{2,8},{4,14},{6,12},{8,2},{10,0},{12,6},{14,4},{1,11},{3,9}... | collective-permute-start | bytes 196616 | tf_op jit(solution)/shard_map/ppermute | solution.py:28
  16.6 6.0 %collective-permute-start.5 = (bf16[2,128,128]{2,1,0:T(8,128)(2,1)S(1)}, bf16[2,128,128]{2,1,0:T(8,128)(2,1)S(1)}, u32[]{:S(2)}, u32[]{:S(2)}) collective-permute-start(bf16[2,128,128]{2,1,0:T(8,128)(2,1)S(1)} %get-tuple-element.48), channel_id=1, source_target_pairs={{0,8},{2,10},{4,12},{6,14},{8,0},{10,2},{12,4},{14,6},{1,9},{3,11}... | collective-permute-start | bytes 196616 | tf_op jit(solution)/shard_map/ppermute | solution.py:28
  17.0 5.7 %collective-permute-start.6 = (bf16[2,128,128]{2,1,0:T(8,128)(2,1)S(1)}, bf16[2,128,128]{2,1,0:T(8,128)(2,1)S(1)}, u32[]{:S(2)}, u32[]{:S(2)}) collective-permute-start(bf16[2,128,128]{2,1,0:T(8,128)(2,1)S(1)} %get-tuple-element.49), channel_id=1, source_target_pairs={{0,6},{2,4},{4,2},{6,0},{8,14},{10,12},{12,10},{14,8},{1,7},{3,5},... | collective-permute-start | bytes 196616 | tf_op jit(solution)/shard_map/ppermute | solution.py:28
  18.3 5.1 %collective-permute-start.2 = (bf16[2,128,128]{2,1,0:T(8,128)(2,1)S(1)}, bf16[2,128,128]{2,1,0:T(8,128)(2,1)S(1)}, u32[]{:S(2)}, u32[]{:S(2)}) collective-permute-start(bf16[2,128,128]{2,1,0:T(8,128)(2,1)S(1)} %get-tuple-element.49), channel_id=1, source_target_pairs={{0,4},{2,6},{4,0},{6,2},{8,12},{10,14},{12,8},{14,10},{1,5},{3,7},... | collective-permute-start | bytes 196616 | tf_op jit(solution)/shard_map/ppermute | solution.py:28

commit v4 on v3

v4 whole, which is shorter than its diff:
```python
import functools
import math

import jax
import jax.numpy as jnp
from jax import lax
from jax.experimental import pallas as pl
from jax.experimental.pallas import tpu as pltpu
from jax.sharding import PartitionSpec as P

AXES = ("seq", "heads")
LOW = jnp.bfloat16
ROWS = 256


def nt(left, right):
    return lax.dot_general(
        left, right, (((1,), (1,)), ((), ())), preferred_element_type=jnp.float32
    )


def nn(left, right):
    return jnp.dot(left, right, preferred_element_type=jnp.float32)


def flip(block, mask):
    size = lax.axis_size(AXES)
    return lax.ppermute(block, AXES, [(i, i ^ mask) for i in range(size)])


def block_index():
    return lax.axis_index("seq") * lax.axis_size("heads") + lax.axis_index("heads")


def in_vmem(array):
    return pltpu.with_memory_space_constraint(array, pltpu.VMEM)


def level_scales(width, tokens, count):
    base = 1.0 / math.sqrt(width * tokens)
    return [base] + [base / math.sqrt(2.0 ** (level - 1)) for level in range(1, count)]


def top_kernel(
    bits, scales, q_hbm, k_hbm, v_hbm, g_hbm, w_hbm,
    q_out, k_out, v_out, g_out, w_out, t_out, own_out, other_out, sems, w_sem,
):
    heads, tokens, width = q_out.shape
    half = heads // 2
    pairs = ((q_hbm, q_out), (k_hbm, k_out), (v_hbm, v_out), (g_hbm, g_out))
    w_copy = pltpu.make_async_copy(w_hbm, w_out, w_sem)
    q_copy, k_copy, v_copy, g_copy = [
        [
            pltpu.make_async_copy(src.at[:, pl.ds(h * width, width)], dst.at[h], sems.at[i, h])
            for h in range(heads)
        ]
        for i, (src, dst) in enumerate(pairs)
    ]
    place = block_index()
    low_bit = place & 1

    def start(*groups):
        for h in range(heads):
            for group in groups:
                group[h].start()

    def wait(*groups):
        for h in range(heads):
            for group in groups:
                group[h].wait()

    def states(level, upper, left_copy, right_copy):
        left_ref, right_ref = (q_out, g_out) if upper else (k_out, v_out)
        for h in range(heads):
            if left_copy is not None:
                left_copy[h].wait()
                right_copy[h].wait()
            turned = left_ref[h].T
            if level == bits:
                t_out[h] = turned
            if upper:
                scaled = (w_out[h, pl.ds(level, 1), :] * turned.astype(jnp.float32)).astype(LOW)
                state = scales[level] * nn(scaled, right_ref[h])
            else:
                state = nn(turned, right_ref[h])
            state = state.astype(LOW)
            row = (level - 3) * half + h % half

            @pl.when(low_bit == h // half)
            def _():
                own_out[row] = state

            @pl.when(low_bit != h // half)
            def _():
                other_out[row] = state

    top = (place >> (bits - 1)) & 1

    @pl.when(top == 1)
    def _():
        w_copy.start()
        start(q_copy, g_copy)
        start(k_copy, v_copy)
        w_copy.wait()
        states(bits, True, q_copy, g_copy)
        wait(k_copy, v_copy)

    @pl.when(top == 0)
    def _():
        start(k_copy, v_copy)
        w_copy.start()
        start(q_copy, g_copy)
        states(bits, False, k_copy, v_copy)
        w_copy.wait()
        wait(q_copy, g_copy)

    for level in range(3, bits):
        bit = (place >> (level - 1)) & 1
        for value in (0, 1):

            @pl.when(bit == value)
            def _():
                states(level, value == 1, None, None)


def low_kernel(
    bits, scales, q_ref, k_ref, v_ref, g_ref, w_ref, t_ref, qt_out, kt_out, d1_out, d2_out
):
    heads = q_ref.shape[0]
    place = block_index()
    top = ((place >> (bits - 1)) & 1) == 1
    for h in range(heads):
        turned = t_ref[h]
        other = jnp.where(top, k_ref[h], q_ref[h]).T
        query_t = jnp.where(top, turned, other)
        key_t = jnp.where(top, other, turned)
        qt_out[h] = query_t
        kt_out[h] = key_t
        for level, out in ((1, d1_out), (2, d2_out)):
            upper = ((place >> (level - 1)) & 1) == 1
            scaled = (w_ref[h, pl.ds(level, 1), :] * query_t.astype(jnp.float32)).astype(LOW)
            left = jnp.where(upper, scaled, key_t)
            right = jnp.where(upper, g_ref[h], v_ref[h])
            out[h] = (jnp.where(upper, scales[level], 1.0) * nn(left, right)).astype(LOW)


def near_head(scale, h, q_ref, k_ref, v_ref, g_ref, w_ref, kt_ref, nk_out, nv_out, local):
    width, tokens = kt_ref.shape[1:]
    rows = min(ROWS, tokens)
    factor = scale * w_ref[h, pl.ds(0, 1), :]
    back, weight = [], []
    for start in range(0, tokens, rows):
        left = tokens - start
        key = k_ref[h, start : start + rows, :]
        value = v_ref[h, start : start + rows, :]
        query = q_ref[h, start:, :]
        grad = g_ref[h, start:, :]
        scores = nt(key, query)
        dots = nt(value, grad)
        allowed = lax.broadcasted_iota(jnp.int32, (rows, left), 0) <= lax.broadcasted_iota(
            jnp.int32, (rows, left), 1
        )
        scores = jnp.where(allowed, scores, 0.0)
        dots = jnp.where(allowed, dots, 0.0)
        part = jnp.sum(scores * dots, axis=0, keepdims=True)
        now = factor[:, start:]
        grad_mix = (now * dots).astype(LOW)
        score_mix = (now * scores).astype(LOW)
        nk_out[local, start : start + rows, :] = nn(grad_mix, query)
        nv_out[local, start : start + rows, :] = nn(score_mix, grad)
        back.append(nn(kt_ref[h, :, start : start + rows], grad_mix))
        weight.append(scale * part)
    return back, weight


def store_sums(ref, h, rows, parts):
    tokens = parts[0].shape[1]
    for i, part in enumerate(parts):
        start = tokens - part.shape[1]
        if i == 0:
            ref[h, rows, :] = part
        else:
            ref[h, rows, start:] += part


def near_kernel(scales, *refs):
    ins, (qt_ref, r1_ref, sum_out, gw_out, nk_out, nv_out) = refs[:6], refs[6:]
    g_ref, w_ref = ins[3], ins[4]
    upper = (block_index() & 1) == 1
    for h in range(sum_out.shape[0]):
        gw_out[h] = jnp.zeros(gw_out.shape[1:], jnp.float32)
        back, weight = near_head(scales[0], h, *ins, nk_out, nv_out, h)
        store_sums(sum_out, h, slice(None), back)
        store_sums(gw_out, h, pl.ds(0, 1), weight)
        products = nt(jnp.where(upper, r1_ref[h], 0), g_ref[h])
        sum_out[h] += (scales[1] * w_ref[h, pl.ds(1, 1), :]) * products
        gw_out[h, pl.ds(1, 1), :] = scales[1] * jnp.sum(
            products * qt_ref[h].astype(jnp.float32), axis=0, keepdims=True
        )


def far_kernel(bits, scales, *refs):
    k_ref, v_ref, g_ref, w_ref, qt_ref, sum_ref, weight_ref, nk_ref, nv_ref = refs[:9]
    (r1_ref, z2_ref, d2_ref), refs = refs[9:12], refs[12:]
    own_refs, other_refs, refs = refs[: bits - 2], refs[bits - 2 : 2 * bits - 4], refs[2 * bits - 4 :]
    gq_hbm, gk_hbm, gv_hbm, gw_hbm, gq_buf, gk_buf, gv_buf, gw_buf, sems, w_sem = refs
    heads, tokens, width = k_ref.shape
    half = heads // 2
    place = block_index()
    low_bit = place & 1
    copies = []
    gw_buf[...] = weight_ref[...]
    for h in range(heads):
        grad = g_ref[h]
        query_t = qt_ref[h].astype(jnp.float32)
        reverse = jnp.where(low_bit == 1, 0, r1_ref[h]).astype(jnp.float32)
        total = sum_ref[h]
        for level in range(2, bits + 1):
            if level == 2:
                got = z2_ref[h].astype(jnp.float32) + d2_ref[h].astype(jnp.float32)
            else:
                own_ref, other_ref = own_refs[level - 3], other_refs[level - 3]
                got = jnp.where(low_bit == h // half, own_ref[h % half], other_ref[h % half])
            upper = ((place >> (level - 1)) & 1) == 1
            sibling = jnp.where(upper, got, 0).astype(LOW)
            reverse = reverse + jnp.where(upper, 0, got).astype(jnp.float32)
            products = nt(sibling, grad)
            total = total + (scales[level] * w_ref[h, pl.ds(level, 1), :]) * products
            gw_buf[h, pl.ds(level, 1), :] = scales[level] * jnp.sum(
                products * query_t, axis=0, keepdims=True
            )
        low = reverse.astype(LOW)
        gq_buf[h] = total.astype(LOW).T
        gk_buf[h] = (nk_ref[h] + nt(v_ref[h], low)).astype(LOW)
        gv_buf[h] = (nv_ref[h] + nn(k_ref[h], low)).astype(LOW)
        for i, (buf, hbm) in enumerate(((gq_buf, gq_hbm), (gk_buf, gk_hbm), (gv_buf, gv_hbm))):
            copy = pltpu.make_async_copy(buf.at[h], hbm.at[:, pl.ds(h * width, width)], sems.at[i, h])
            copy.start()
            copies.append(copy)
    copy = pltpu.make_async_copy(gw_buf, gw_hbm, w_sem)
    copy.start()
    copies.append(copy)
    for copy in copies:
        copy.wait()


ANY = pl.BlockSpec(memory_space=pl.ANY)
IN_VMEM = pl.BlockSpec(memory_space=pltpu.VMEM)
LIMIT = 16 * 1024 * 1024


def in_hbm(array):
    return pltpu.with_memory_space_constraint(array, pltpu.HBM)


def call(kernel, name, flops, out_shape, operands):
    outs = [pltpu.VMEM(shape, dtype) for shape, dtype in out_shape]
    return pl.pallas_call(
        kernel,
        out_shape=outs,
        in_specs=[IN_VMEM] * len(operands),
        out_specs=[IN_VMEM] * len(outs),
        compiler_params=pltpu.CompilerParams(vmem_limit_bytes=LIMIT),
        cost_estimate=pl.CostEstimate(flops=flops, bytes_accessed=0, transcendentals=0),
        name=name,
    )(*[in_vmem(x) for x in operands])


def on_device(queries, keys, values, out_grad, level_weights):
    tokens = queries.shape[0]
    heads, levels, _ = level_weights.shape
    width = queries.shape[1] // heads
    half = heads // 2
    bits = lax.axis_size(AXES).bit_length() - 1
    scales = level_scales(width, tokens, levels)
    f32 = jnp.float32
    cost = 1000 * tokens * tokens * width
    by_head = ((heads, tokens, width), LOW)
    turned = ((heads, width, tokens), LOW)
    full = ((heads, width, width), LOW)
    halves = (((bits - 2) * half, width, width), LOW)
    weight_rows = ((heads, levels, tokens), f32)
    outs = [by_head] * 4 + [weight_rows, turned, halves, halves]
    q_v, k_v, v_v, g_v, w_v, t_v, own, other = pl.pallas_call(
        functools.partial(top_kernel, bits, scales),
        out_shape=[pltpu.VMEM(shape, dtype) for shape, dtype in outs],
        in_specs=[ANY] * 5,
        out_specs=[IN_VMEM] * len(outs),
        scratch_shapes=[pltpu.SemaphoreType.DMA((4, heads)), pltpu.SemaphoreType.DMA],
        compiler_params=pltpu.CompilerParams(vmem_limit_bytes=LIMIT),
        cost_estimate=pl.CostEstimate(flops=cost, bytes_accessed=0, transcendentals=0),
        name="top_states",
    )(*[in_hbm(x) for x in (queries, keys, values, out_grad, level_weights)])

    def as_f(array):
        return array.astype(f32)

    got_x = flip(other, 1)
    got_z = flip(own, 2)
    got_d = flip(other, 3)
    quad = as_f(own) + as_f(got_x) + as_f(got_z) + as_f(got_d)
    qt, kt, d1, d2 = call(
        functools.partial(low_kernel, bits, scales), "low_states", cost,
        [turned, turned, full, full], [q_v, k_v, v_v, g_v, w_v, t_v],
    )
    got_1 = flip(d1, 1)
    got_2 = flip(d2, 2)
    sums = []
    for bit in range(2, bits):
        sums.append(quad[:half].astype(LOW))
        quad = quad[half:]
        if bit < bits - 1:
            quad = quad + as_f(flip(quad.astype(LOW), 1 << bit))
    own_half = [flip(x, 1 << (i + 2)) for i, x in enumerate(sums)]
    other_half = [flip(x, (1 << (i + 2)) ^ 1) for i, x in enumerate(sums)]
    diagonal_2 = flip(got_2, 1)
    total, weights, near_k, near_v = call(
        functools.partial(near_kernel, scales), "near", cost,
        [((heads, width, tokens), f32), weight_rows, *[((heads, tokens, width), f32)] * 2],
        [q_v, k_v, v_v, g_v, w_v, kt, qt, got_1],
    )
    operands = [k_v, v_v, g_v, w_v, qt, total, weights, near_k, near_v]
    operands += [got_1, got_2, diagonal_2, *own_half, *other_half]
    out = jax.ShapeDtypeStruct((tokens, heads * width), LOW)
    return pl.pallas_call(
        functools.partial(far_kernel, bits, scales),
        out_shape=(out, out, out, jax.ShapeDtypeStruct((heads, levels, tokens), f32)),
        in_specs=[IN_VMEM] * len(operands),
        out_specs=(ANY,) * 4,
        scratch_shapes=[pltpu.VMEM((heads, tokens, width), LOW)] * 3
        + [
            pltpu.VMEM((heads, levels, tokens), f32),
            pltpu.SemaphoreType.DMA((3, heads)),
            pltpu.SemaphoreType.DMA,
        ],
        compiler_params=pltpu.CompilerParams(vmem_limit_bytes=LIMIT),
        cost_estimate=pl.CostEstimate(flops=cost, bytes_accessed=0, transcendentals=0),
        name="far",
    )(*[in_vmem(x) for x in operands])


def solution(mesh):
    rows = P(("groups", "seq", "heads"), "sub")
    weights = P("sub", None, ("groups", "seq", "heads"))
    return jax.shard_map(
        on_device,
        mesh=mesh,
        in_specs=(rows, rows, rows, rows, weights),
        out_specs=(rows, rows, rows, weights),
        check_vma=False,
    )
```

time: 25.4 us -> 23.6 us (0.929)
  waiting for transfers between devices: 3.77 us -> 2.15 us
  Pallas kernels: 8.24 us -> 7.32 us
  starting transfers between devices: 12.5 us -> 13.3 us
    ppermute x8, waiting for transfers between devices: 3.77 us -> 2.15 us  [flip(): return lax.ppermute(block, AXES, [(i, i ^ mask) for i in range(size)])]
    pallas_call x2, Pallas kernels: 4.92 us -> 3.88 us  [the longest x1 2.1 us: on_device(): pl.pallas_call(functools.partial(top_kernel, bits, scales), out_shape=[pl...]
    ppermute x8, starting transfers between devices: 12.5 us -> 13.3 us  [flip(): return lax.ppermute(block, AXES, [(i, i ^ mask) for i in range(size)])]
    pallas_call x3 -> x2, Pallas kernels: 3.32 us -> 3.44 us  [call(): pl.pallas_call(kernel, out_shape=outs, in_specs=[IN_VMEM] * len(operands)...]
  transfers between devices with their start and end apart: 8 -> 8, of which waited for: 4 -> 3; matrix products, arithmetic and copies ran while one was open for 0% -> 0% of each run, Pallas kernels for 13% -> 15%
where the time goes in v4:
time: 23.6 us; the launch traced here: 23.5 us
  starting transfers between devices  13.3 us (56%)
  Pallas kernels  7.32 us (31%)
  waiting for transfers between devices  2.15 us (9%)
  between operations  0.66 us (3%)
    ppermute x8, starting transfers between devices, flip(): return lax.ppermute(block, AXES, [(i, i ^ mask) for i in range(size)])  13.3 us
    pallas_call x2, Pallas kernels, call(): pl.pallas_call(kernel, out_shape=outs, in_specs=[IN_VMEM] * len(operands)...  3.44 us
    ppermute x8, waiting for transfers between devices, flip(): return lax.ppermute(block, AXES, [(i, i ^ mask) for i in range(size)])  2.15 us
    pallas_call x1, Pallas kernels, on_device(): pl.pallas_call(functools.partial(top_kernel, bits, scales), out_shape=[pl...  2.1 us
    pallas_call x1, Pallas kernels, on_device(): pl.pallas_call(functools.partial(far_kernel, bits, scales), out_shape=(ou...  1.78 us
  transfers between devices with their start and end apart: 8, of which 3 were waited for; matrix products, arithmetic and copies ran while one was open for 0% of the time, Pallas kernels for 15%

profile of v4, /device:TPU:0, one launch (start us, length us, event | category | flops | bytes accessed | tf_op | source)
XLA Modules:
  0.0 23.5 jit_solution(15171680653947856156)
XLA Ops:
  0.6 2.1 %top_states.1 = (bf16[4,512,128]{2,1,0:T(8,128)(2,1)S(1)}, bf16[4,512,128]{2,1,0:T(8,128)(2,1)S(1)}, bf16[4,512,128]{2,1,0:T(8,128)(2,1)S(1)}, bf16[4,512,128]{2...) custom-call(bf16[512,512]{1,0:T(8,128)(2,1)} %q_hbm.1, ...), custom_call_target="tpu_custom_call" | custom-call | flops 33554432000 | tf_op jit(solution)/shard_map/top_states/pallas_call | solution.py:284
  2.7 4.0 %collective-permute-start.5 = (bf16[2,128,128]{2,1,0:T(8,128)(2,1)S(1)}, bf16[2,128,128]{2,1,0:T(8,128)(2,1)S(1)}, u32[]{:S(2)}, u32[]{:S(2)}) collective-permute-start(bf16[2,128,128]{2,1,0:T(8,128)(2,1)S(1)} %get-tuple-element.35), channel_id=1, source_target_pairs={{0,6},{2,4},{4,2},{6,0},{8,14},{10,12},{12,10},{14,8},{1,7},{3,5},... | collective-permute-start | bytes 196616 | tf_op jit(solution)/shard_map/ppermute | solution.py:28
  6.8 0.5 %collective-permute-start.3 = (bf16[2,128,128]{2,1,0:T(8,128)(2,1)S(1)}, bf16[2,128,128]{2,1,0:T(8,128)(2,1)S(1)}, u32[]{:S(2)}, u32[]{:S(2)}) collective-permute-start(bf16[2,128,128]{2,1,0:T(8,128)(2,1)S(1)} %get-tuple-element.35), channel_id=1, source_target_pairs={{0,2},{2,0},{4,6},{6,4},{8,10},{10,8},{12,14},{14,12},{1,3},{3,1},... | collective-permute-start | bytes 196616 | tf_op jit(solution)/shard_map/ppermute | solution.py:28
  7.3 0.1 collective-permute-start.4
  7.4 0.7 %low_states.1 = (bf16[4,128,512]{2,1,0:T(8,128)(2,1)S(1)}, bf16[4,128,512]{2,1,0:T(8,128)(2,1)S(1)}, bf16[4,128,128]{2,1,0:T(8,128)(2,1)S(1)}, bf16[4,128,128]{2,1,0:T(8,128)(2,1)S(1)}) custom-call(bf16[4,512,128]{2,1,0:T(8,128)(2,1)S(1)} %get-tuple-element.24.q_ref.refs_0_, bf16[4,512,128]{2,1,0:T(8,128)(2,1)S(1)} %get-tuple-element.20.k_ref.refs_1_.refs_0_, ...), custom_call_target="tpu_custom_call" | custom-call | flops 33554432000 | tf_op jit(solution)/shard_map/low_states/pallas_call | solution.py:258
  8.1 1.9 %collective-permute-start = (bf16[4,128,128]{2,1,0:T(8,128)(2,1)S(1)}, bf16[4,128,128]{2,1,0:T(8,128)(2,1)S(1)}, u32[]{:S(2)}, u32[]{:S(2)}) collective-permute-start(bf16[4,128,128]{2,1,0:T(8,128)(2,1)S(1)} %get-tuple-element.28), channel_id=1, source_target_pairs={{0,2},{2,0},{4,6},{6,4},{8,10},{10,8},{12,14},{14,12},{1,3},{3,1},... | collective-permute-start | bytes 393224 | tf_op jit(solution)/shard_map/ppermute | solution.py:28
  10.0 1.6 %collective-permute-start.1 = (bf16[4,128,128]{2,1,0:T(8,128)(2,1)S(1)}, bf16[4,128,128]{2,1,0:T(8,128)(2,1)S(1)}, u32[]{:S(2)}, u32[]{:S(2)}) collective-permute-start(bf16[4,128,128]{2,1,0:T(8,128)(2,1)S(1)} %get-tuple-element.33), channel_id=1, source_target_pairs={{0,4},{2,6},{4,0},{6,2},{8,12},{10,14},{12,8},{14,10},{1,5},{3,7},... | collective-permute-start | bytes 393224 | tf_op jit(solution)/shard_map/ppermute | solution.py:28
  11.6 0.3 %collective-permute-done.4 = bf16[2,128,128]{2,1,0:T(8,128)(2,1)S(1)} collective-permute-done((bf16[2,128,128]{2,1,0:T(8,128)(2,1)S(1)}, bf16[2,128,128]{2,1,0:T(8,128)(2,1)S(1)}, u32[]{:S(2)}, u32[]{:S(2)}) %collective-permute-start.4) | collective-permute-done | bytes 65568 | tf_op jit(solution)/shard_map/ppermute | solution.py:28
  11.9 0.0 collective-permute-done.5
  11.9 0.0 collective-permute-done.3
  11.9 4.5 %collective-permute-start.7 = (bf16[2,128,128]{2,1,0:T(8,128)(2,1)S(1)}, bf16[2,128,128]{2,1,0:T(8,128)(2,1)S(1)}, u32[]{:S(2)}, u32[]{:S(2)}) collective-permute-start(bf16[2,128,128]{2,1,0:T(8,128)(2,1)S(1)} %add_convert_fusion), channel_id=1, source_target_pairs={{0,10},{2,8},{4,14},{6,12},{8,2},{10,0},{12,6},{14,4},{1,11},{3,9}... | collective-permute-start | bytes 196616 | tf_op jit(solution)/shard_map/ppermute | solution.py:28
  16.4 0.0 collective-permute-start.6
  16.4 0.0 collective-permute-done.1.refs_10_
  16.4 0.6 %collective-permute-start.2 = (bf16[4,128,128]{2,1,0:T(8,128)(2,1)S(1)}, bf16[4,128,128]{2,1,0:T(8,128)(2,1)S(1)}, u32[]{:S(2)}, u32[]{:S(2)}) collective-permute-start(bf16[4,128,128]{2,1,0:T(8,128)(2,1)S(1)} %collective-permute-done.1.refs_10_), channel_id=1, source_target_pairs={{0,2},{2,0},{4,6},{6,4},{8,10},{10,8},{12,14},{14,12},{1,3},{3,1},... | collective-permute-start | bytes 393224 | tf_op jit(solution)/shard_map/ppermute | solution.py:28
  17.1 0.0 collective-permute-done.refs_7_.refs_9_
  17.1 2.7 %near.1 = (f32[4,128,512]{2,1,0:T(8,128)S(1)}, f32[4,8,512]{2,1,0:T(8,128)S(1)}, f32[4,512,128]{2,1,0:T(8,128)S(1)}, f32[4,512,128]{2,1,0:T(8,128)S(1)}) custom-call(bf16[4,512,128]{2,1,0:T(8,128)(2,1)S(1)} %get-tuple-element.24.q_ref.refs_0_, bf16[4,512,128]{2,1,0:T(8,128)(2,1)S(1)} %get-tuple-element.20.k_ref.refs_1_.refs_0_, ...), custom_call_target="tpu_custom_call" | custom-call | flops 33554432000 | tf_op jit(solution)/shard_map/near/pallas_call | solution.py:258
  19.8 0.5 %collective-permute-done.7.refs_13_ = bf16[2,128,128]{2,1,0:T(8,128)(2,1)S(1)} collective-permute-done((bf16[2,128,128]{2,1,0:T(8,128)(2,1)S(1)}, bf16[2,128,128]{2,1,0:T(8,128)(2,1)S(1)}, u32[]{:S(2)}, u32[]{:S(2)}) %collective-permute-start.7) | collective-permute-done | bytes 65568 | tf_op jit(solution)/shard_map/ppermute | solution.py:28
  20.3 1.4 %collective-permute-done.6.refs_12_ = bf16[2,128,128]{2,1,0:T(8,128)(2,1)S(1)} collective-permute-done((bf16[2,128,128]{2,1,0:T(8,128)(2,1)S(1)}, bf16[2,128,128]{2,1,0:T(8,128)(2,1)S(1)}, u32[]{:S(2)}, u32[]{:S(2)}) %collective-permute-start.6) | collective-permute-done | bytes 65568 | tf_op jit(solution)/shard_map/ppermute | solution.py:28
  21.7 0.0 collective-permute-done.2.refs_11_
  21.7 1.8 %far.1 = (bf16[512,512]{1,0:T(8,128)(2,1)}, bf16[512,512]{1,0:T(8,128)(2,1)}, bf16[512,512]{1,0:T(8,128)(2,1)}, f32[4,8,512]{2,1,0:T(8,128)}) custom-call(bf16[4,512,128]{2,1,0:T(8,128)(2,1)S(1)} %get-tuple-element.20.k_ref.refs_1_.refs_0_, bf16[4,512,128]{2,1,0:T(8,128)(2,1)S(1)} %get-tuple-element.21.v_ref.refs_2_.refs_1_, ...), custom_call_target="tpu_custom_call" | custom-call | flops 33554432000 | tf_op jit(solution)/shard_map/far/pallas_call | solution.py:325
  (1 shorter events, 0.0 us)
Async XLA Ops:
  2.7 9.1 %collective-permute-start.5 = (bf16[2,128,128]{2,1,0:T(8,128)(2,1)S(1)}, bf16[2,128,128]{2,1,0:T(8,128)(2,1)S(1)}, u32[]{:S(2)}, u32[]{:S(2)}) collective-permute-start(bf16[2,128,128]{2,1,0:T(8,128)(2,1)S(1)} %get-tuple-element.35), channel_id=1, source_target_pairs={{0,6},{2,4},{4,2},{6,0},{8,14},{10,12},{12,10},{14,8},{1,7},{3,5},... | collective-permute-start | bytes 196616 | tf_op jit(solution)/shard_map/ppermute | solution.py:28
  6.8 5.1 %collective-permute-start.3 = (bf16[2,128,128]{2,1,0:T(8,128)(2,1)S(1)}, bf16[2,128,128]{2,1,0:T(8,128)(2,1)S(1)}, u32[]{:S(2)}, u32[]{:S(2)}) collective-permute-start(bf16[2,128,128]{2,1,0:T(8,128)(2,1)S(1)} %get-tuple-element.35), channel_id=1, source_target_pairs={{0,2},{2,0},{4,6},{6,4},{8,10},{10,8},{12,14},{14,12},{1,3},{3,1},... | collective-permute-start | bytes 196616 | tf_op jit(solution)/shard_map/ppermute | solution.py:28
  7.3 4.6 %collective-permute-start.4 = (bf16[2,128,128]{2,1,0:T(8,128)(2,1)S(1)}, bf16[2,128,128]{2,1,0:T(8,128)(2,1)S(1)}, u32[]{:S(2)}, u32[]{:S(2)}) collective-permute-start(bf16[2,128,128]{2,1,0:T(8,128)(2,1)S(1)} %get-tuple-element.34), channel_id=1, source_target_pairs={{0,4},{2,6},{4,0},{6,2},{8,12},{10,14},{12,8},{14,10},{1,5},{3,7},... | collective-permute-start | bytes 196616 | tf_op jit(solution)/shard_map/ppermute | solution.py:28
  8.1 9.0 %collective-permute-start = (bf16[4,128,128]{2,1,0:T(8,128)(2,1)S(1)}, bf16[4,128,128]{2,1,0:T(8,128)(2,1)S(1)}, u32[]{:S(2)}, u32[]{:S(2)}) collective-permute-start(bf16[4,128,128]{2,1,0:T(8,128)(2,1)S(1)} %get-tuple-element.28), channel_id=1, source_target_pairs={{0,2},{2,0},{4,6},{6,4},{8,10},{10,8},{12,14},{14,12},{1,3},{3,1},... | collective-permute-start | bytes 393224 | tf_op jit(solution)/shard_map/ppermute | solution.py:28
  10.0 6.4 %collective-permute-start.1 = (bf16[4,128,128]{2,1,0:T(8,128)(2,1)S(1)}, bf16[4,128,128]{2,1,0:T(8,128)(2,1)S(1)}, u32[]{:S(2)}, u32[]{:S(2)}) collective-permute-start(bf16[4,128,128]{2,1,0:T(8,128)(2,1)S(1)} %get-tuple-element.33), channel_id=1, source_target_pairs={{0,4},{2,6},{4,0},{6,2},{8,12},{10,14},{12,8},{14,10},{1,5},{3,7},... | collective-permute-start | bytes 393224 | tf_op jit(solution)/shard_map/ppermute | solution.py:28
  11.9 8.4 %collective-permute-start.7 = (bf16[2,128,128]{2,1,0:T(8,128)(2,1)S(1)}, bf16[2,128,128]{2,1,0:T(8,128)(2,1)S(1)}, u32[]{:S(2)}, u32[]{:S(2)}) collective-permute-start(bf16[2,128,128]{2,1,0:T(8,128)(2,1)S(1)} %add_convert_fusion), channel_id=1, source_target_pairs={{0,10},{2,8},{4,14},{6,12},{8,2},{10,0},{12,6},{14,4},{1,11},{3,9}... | collective-permute-start | bytes 196616 | tf_op jit(solution)/shard_map/ppermute | solution.py:28
  16.4 5.2 %collective-permute-start.6 = (bf16[2,128,128]{2,1,0:T(8,128)(2,1)S(1)}, bf16[2,128,128]{2,1,0:T(8,128)(2,1)S(1)}, u32[]{:S(2)}, u32[]{:S(2)}) collective-permute-start(bf16[2,128,128]{2,1,0:T(8,128)(2,1)S(1)} %add_convert_fusion), channel_id=1, source_target_pairs={{0,8},{2,10},{4,12},{6,14},{8,0},{10,2},{12,4},{14,6},{1,9},{3,11}... | collective-permute-start | bytes 196616 | tf_op jit(solution)/shard_map/ppermute | solution.py:28
  16.4 5.2 %collective-permute-start.2 = (bf16[4,128,128]{2,1,0:T(8,128)(2,1)S(1)}, bf16[4,128,128]{2,1,0:T(8,128)(2,1)S(1)}, u32[]{:S(2)}, u32[]{:S(2)}) collective-permute-start(bf16[4,128,128]{2,1,0:T(8,128)(2,1)S(1)} %collective-permute-done.1.refs_10_), channel_id=1, source_target_pairs={{0,2},{2,0},{4,6},{6,4},{8,10},{10,8},{12,14},{14,12},{1,3},{3,1},... | collective-permute-start | bytes 393224 | tf_op jit(solution)/shard_map/ppermute | solution.py:28

commit v5 on v4

v5 whole, which is shorter than its diff:
```python
import functools
import math

import jax
import jax.numpy as jnp
from jax import lax
from jax.experimental import pallas as pl
from jax.experimental.pallas import tpu as pltpu
from jax.sharding import PartitionSpec as P

AXES = ("seq", "heads")
LOW = jnp.bfloat16
ROWS = 256
GROUP = 2


def nt(left, right):
    return lax.dot_general(
        left, right, (((1,), (1,)), ((), ())), preferred_element_type=jnp.float32
    )


def nn(left, right):
    return jnp.dot(left, right, preferred_element_type=jnp.float32)


def flip(block, mask):
    size = lax.axis_size(AXES)
    return lax.ppermute(block, AXES, [(i, i ^ mask) for i in range(size)])


def block_index():
    return lax.axis_index("seq") * lax.axis_size("heads") + lax.axis_index("heads")


def head(ref, h, width, rows=slice(None)):
    return ref[rows, h * width : (h + 1) * width]


def in_vmem(array):
    return pltpu.with_memory_space_constraint(array, pltpu.VMEM)


def level_scales(width, tokens, count):
    base = 1.0 / math.sqrt(width * tokens)
    return [base] + [base / math.sqrt(2.0 ** (level - 1)) for level in range(1, count)]


def top_kernel(bits, scales, q_hbm, k_hbm, v_hbm, g_hbm, w_hbm, t_out, own_out, other_out, left_buf, right_buf, w_buf, sems):
    rows, heads, tokens, width = left_buf.shape
    half = heads // 2
    place = block_index()
    low_bit = place & 1

    def states(index, upper):
        level = index + 3
        for first in range(0, heads, GROUP):
            lefts, rights = [], []
            for h in range(first, first + GROUP):
                for copy in copies(index, h, upper):
                    copy.wait()
                turned = left_buf[index, h].T
                if level == bits:
                    t_out[h] = turned
                if upper:
                    turned = (w_buf[index, h] * turned.astype(jnp.float32)).astype(LOW)
                lefts.append(turned)
                rights.append(right_buf[index, h])
            product = nn(jnp.concatenate(lefts, 0), jnp.concatenate(rights, 1))
            for i in range(GROUP):
                h = first + i
                part = slice(i * width, i * width + width)
                state = product[part, part]
                if upper:
                    state = scales[level] * state
                state = state.astype(LOW)
                row = index * half + h % half

                @pl.when(low_bit == h // half)
                def _():
                    own_out[row] = state

                @pl.when(low_bit != h // half)
                def _():
                    other_out[row] = state

    def copies(index, h, upper):
        left, right = (q_hbm, g_hbm) if upper else (k_hbm, v_hbm)
        columns = pl.ds(h * width, width)
        made = [
            pltpu.make_async_copy(left.at[:, columns], left_buf.at[index, h], sems.at[0, index, h]),
            pltpu.make_async_copy(right.at[:, columns], right_buf.at[index, h], sems.at[1, index, h]),
        ]
        if upper:
            row = w_hbm.at[h, pl.ds(index + 3, 1), :]
            made.append(pltpu.make_async_copy(row, w_buf.at[index, h], sems.at[2, index, h]))
        return made

    for index in range(rows):
        bit = (place >> (index + 2)) & 1
        for value in (0, 1):

            @pl.when(bit == value)
            def _():
                for h in range(heads):
                    for copy in copies(index, h, value == 1):
                        copy.start()
                states(index, value == 1)


def low_kernel(
    bits, scales, q_ref, k_ref, v_ref, g_ref, w_ref, t_ref, qt_out, kt_out, d1_out, d2_out
):
    heads, width = t_ref.shape[:2]
    place = block_index()
    top = ((place >> (bits - 1)) & 1) == 1
    for h in range(heads):
        turned = t_ref[h]
        other = jnp.where(top, head(k_ref, h, width), head(q_ref, h, width)).T
        query_t = jnp.where(top, turned, other)
        key_t = jnp.where(top, other, turned)
        qt_out[h] = query_t
        kt_out[h] = key_t
        for level, out in ((1, d1_out), (2, d2_out)):
            upper = ((place >> (level - 1)) & 1) == 1
            scaled = (w_ref[h, pl.ds(level, 1), :] * query_t.astype(jnp.float32)).astype(LOW)
            left = jnp.where(upper, scaled, key_t)
            right = jnp.where(upper, head(g_ref, h, width), head(v_ref, h, width))
            out[h] = (jnp.where(upper, scales[level], 1.0) * nn(left, right)).astype(LOW)


def near_head(scale, h, q_ref, k_ref, v_ref, g_ref, w_ref, kt_ref, nk_out, nv_out, local):
    width, tokens = kt_ref.shape[1:]
    rows = min(ROWS, tokens)
    factor = scale * w_ref[h, pl.ds(0, 1), :]
    back, weight = [], []
    for start in range(0, tokens, rows):
        left = tokens - start
        key = head(k_ref, h, width, slice(start, start + rows))
        value = head(v_ref, h, width, slice(start, start + rows))
        query = head(q_ref, h, width, slice(start, None))
        grad = head(g_ref, h, width, slice(start, None))
        scores = nt(key, query)
        dots = nt(value, grad)
        allowed = lax.broadcasted_iota(jnp.int32, (rows, left), 0) <= lax.broadcasted_iota(
            jnp.int32, (rows, left), 1
        )
        scores = jnp.where(allowed, scores, 0.0)
        dots = jnp.where(allowed, dots, 0.0)
        part = jnp.sum(scores * dots, axis=0, keepdims=True)
        now = factor[:, start:]
        grad_mix = (now * dots).astype(LOW)
        score_mix = (now * scores).astype(LOW)
        nk_out[local, start : start + rows, :] = nn(grad_mix, query)
        nv_out[local, start : start + rows, :] = nn(score_mix, grad)
        back.append(nn(kt_ref[h, :, start : start + rows], grad_mix))
        weight.append(scale * part)
    return back, weight


def store_sums(ref, h, rows, parts):
    tokens = parts[0].shape[1]
    for i, part in enumerate(parts):
        start = tokens - part.shape[1]
        if i == 0:
            ref[h, rows, :] = part
        else:
            ref[h, rows, start:] += part


def near_kernel(scales, *refs):
    ins, (qt_ref, r1_ref, sum_out, gw_out, nk_out, nv_out) = refs[:6], refs[6:]
    g_ref, w_ref = ins[3], ins[4]
    upper = (block_index() & 1) == 1
    for h in range(sum_out.shape[0]):
        gw_out[h] = jnp.zeros(gw_out.shape[1:], jnp.float32)
        back, weight = near_head(scales[0], h, *ins, nk_out, nv_out, h)
        store_sums(sum_out, h, slice(None), back)
        store_sums(gw_out, h, pl.ds(0, 1), weight)
        products = nt(jnp.where(upper, r1_ref[h], 0), head(g_ref, h, sum_out.shape[1]))
        sum_out[h] += (scales[1] * w_ref[h, pl.ds(1, 1), :]) * products
        gw_out[h, pl.ds(1, 1), :] = scales[1] * jnp.sum(
            products * qt_ref[h].astype(jnp.float32), axis=0, keepdims=True
        )


def spread(blocks):
    zeros = jnp.zeros_like(blocks[0])
    return jnp.concatenate(
        [
            jnp.concatenate([block if i == j else zeros for j in range(len(blocks))], 1)
            for i, block in enumerate(blocks)
        ],
        0,
    )


def far_kernel(bits, scales, *refs):
    k_ref, v_ref, g_ref, w_ref, qt_ref, _, weight_ref, nk_ref, nv_ref = refs[:9]
    (r1_ref, z2_ref, d2_ref), refs = refs[9:12], refs[12:]
    own_refs, other_refs, refs = refs[: bits - 2], refs[bits - 2 : 2 * bits - 4], refs[2 * bits - 4 :]
    gq_hbm, gk_hbm, gv_hbm, gw_hbm, sum_ref, gq_buf, gk_buf, gv_buf, gw_buf, sems, w_sem = refs
    heads, width, tokens = sum_ref.shape
    half = heads // 2
    place = block_index()
    low_bit = place & 1
    copies = []

    def is_upper(level):
        return ((place >> (level - 1)) & 1) == 1

    def received(level, h):
        if level == 1:
            return r1_ref[h]
        if level == 2:
            return z2_ref[h].astype(jnp.float32) + d2_ref[h].astype(jnp.float32)
        own_ref, other_ref = own_refs[level - 3], other_refs[level - 3]
        return jnp.where(low_bit == h // half, own_ref[h % half], other_ref[h % half])

    def send(i, first, buf, hbm):
        span = pl.ds(first * width, GROUP * width)
        copy = pltpu.make_async_copy(buf.at[first // GROUP], hbm.at[:, span], sems.at[i, first])
        copy.start()
        copies.append(copy)

    gw_buf[...] = weight_ref[...]
    for first in range(0, heads, GROUP):
        group = range(first, first + GROUP)
        reverses = []
        for h in group:
            total = jnp.zeros((width, width), jnp.float32)
            for level in range(1, bits + 1):
                total = total + jnp.where(is_upper(level), 0, received(level, h)).astype(jnp.float32)
            reverses.append(total.astype(LOW))
        low = spread(reverses)
        near_k = jnp.concatenate([nk_ref[h] for h in group], 1)
        near_v = jnp.concatenate([nv_ref[h] for h in group], 1)
        value = v_ref[:, first * width : (first + GROUP) * width]
        key = k_ref[:, first * width : (first + GROUP) * width]
        gk_buf[first // GROUP] = (near_k + nt(value, low)).astype(LOW)
        gv_buf[first // GROUP] = (near_v + nn(key, low)).astype(LOW)
        send(0, first, gk_buf, gk_hbm)
        send(1, first, gv_buf, gv_hbm)
    for level in range(2, bits + 1):

        @pl.when(is_upper(level))
        def _():
            for first in range(0, heads, GROUP):
                group = range(first, first + GROUP)
                siblings = spread([received(level, h).astype(LOW) for h in group])
                products = nt(siblings, g_ref[:, first * width : (first + GROUP) * width])
                for i, h in enumerate(group):
                    mine = products[i * width : i * width + width]
                    sum_ref[h] += (scales[level] * w_ref[h, pl.ds(level, 1), :]) * mine
                    gw_buf[h, pl.ds(level, 1), :] = scales[level] * jnp.sum(
                        mine * qt_ref[h].astype(jnp.float32), axis=0, keepdims=True
                    )

    copy = pltpu.make_async_copy(gw_buf, gw_hbm, w_sem)
    copy.start()
    copies.append(copy)
    for first in range(0, heads, GROUP):
        for i in range(GROUP):
            gq_buf[first // GROUP, :, i * width : i * width + width] = sum_ref[first + i].astype(LOW).T
        send(2, first, gq_buf, gq_hbm)
    for copy in copies:
        copy.wait()


ANY = pl.BlockSpec(memory_space=pl.ANY)
IN_VMEM = pl.BlockSpec(memory_space=pltpu.VMEM)
LIMIT = 16 * 1024 * 1024


def in_hbm(array):
    return pltpu.with_memory_space_constraint(array, pltpu.HBM)


def call(kernel, name, flops, out_shape, operands):
    outs = [pltpu.VMEM(shape, dtype) for shape, dtype in out_shape]
    return pl.pallas_call(
        kernel,
        out_shape=outs,
        in_specs=[IN_VMEM] * len(operands),
        out_specs=[IN_VMEM] * len(outs),
        compiler_params=pltpu.CompilerParams(vmem_limit_bytes=LIMIT),
        cost_estimate=pl.CostEstimate(flops=flops, bytes_accessed=0, transcendentals=0),
        name=name,
    )(*[in_vmem(x) for x in operands])


def on_device(queries, keys, values, out_grad, level_weights):
    tokens = queries.shape[0]
    heads, levels, _ = level_weights.shape
    width = queries.shape[1] // heads
    half = heads // 2
    bits = lax.axis_size(AXES).bit_length() - 1
    scales = level_scales(width, tokens, levels)
    f32 = jnp.float32
    cost = 1000 * tokens * tokens * width
    turned = ((heads, width, tokens), LOW)
    full = ((heads, width, width), LOW)
    halves = (((bits - 2) * half, width, width), LOW)
    weight_rows = ((heads, levels, tokens), f32)
    outs = [turned, halves, halves]
    chosen = pltpu.VMEM((bits - 2, heads, tokens, width), LOW)
    t_v, own, other = pl.pallas_call(
        functools.partial(top_kernel, bits, scales),
        out_shape=[pltpu.VMEM(shape, dtype) for shape, dtype in outs],
        in_specs=[ANY] * 5,
        out_specs=[IN_VMEM] * len(outs),
        scratch_shapes=[
            chosen, chosen, pltpu.VMEM((bits - 2, heads, 1, tokens), f32),
            pltpu.SemaphoreType.DMA((3, bits - 2, heads)),
        ],
        compiler_params=pltpu.CompilerParams(vmem_limit_bytes=LIMIT),
        cost_estimate=pl.CostEstimate(flops=cost, bytes_accessed=0, transcendentals=0),
        name="top_states",
    )(*[in_hbm(x) for x in (queries, keys, values, out_grad, level_weights)])
    q_v, k_v, v_v, g_v, w_v = queries, keys, values, out_grad, level_weights

    def as_f(array):
        return array.astype(f32)

    got_x = flip(other, 1)
    got_z = flip(own, 2)
    got_d = flip(other, 3)
    quad = as_f(own) + as_f(got_x) + as_f(got_z) + as_f(got_d)
    qt, kt, d1, d2 = call(
        functools.partial(low_kernel, bits, scales), "low_states", cost,
        [turned, turned, full, full], [q_v, k_v, v_v, g_v, w_v, t_v],
    )
    got_1 = flip(d1, 1)
    got_2 = flip(d2, 2)
    sums = []
    for bit in range(2, bits):
        sums.append(quad[:half].astype(LOW))
        quad = quad[half:]
        if bit < bits - 1:
            quad = quad + as_f(flip(quad.astype(LOW), 1 << bit))
    own_half = [flip(x, 1 << (i + 2)) for i, x in enumerate(sums)]
    other_half = [flip(x, (1 << (i + 2)) ^ 1) for i, x in enumerate(sums)]
    diagonal_2 = flip(got_2, 1)
    total, weights, near_k, near_v = call(
        functools.partial(near_kernel, scales), "near", cost,
        [((heads, width, tokens), f32), weight_rows, *[((heads, tokens, width), f32)] * 2],
        [q_v, k_v, v_v, g_v, w_v, kt, qt, got_1],
    )
    operands = [k_v, v_v, g_v, w_v, qt, total, weights, near_k, near_v]
    operands += [got_1, got_2, diagonal_2, *own_half, *other_half]
    out = jax.ShapeDtypeStruct((tokens, heads * width), LOW)
    return pl.pallas_call(
        functools.partial(far_kernel, bits, scales),
        out_shape=(out, out, out, jax.ShapeDtypeStruct((heads, levels, tokens), f32), pltpu.VMEM((heads, width, tokens), f32)),
        in_specs=[IN_VMEM] * len(operands),
        out_specs=(ANY,) * 4 + (IN_VMEM,),
        input_output_aliases={5: 4},
        scratch_shapes=[pltpu.VMEM((heads // GROUP, tokens, GROUP * width), LOW)] * 3
        + [
            pltpu.VMEM((heads, levels, tokens), f32),
            pltpu.SemaphoreType.DMA((3, heads)),
            pltpu.SemaphoreType.DMA,
        ],
        compiler_params=pltpu.CompilerParams(vmem_limit_bytes=LIMIT),
        cost_estimate=pl.CostEstimate(flops=cost, bytes_accessed=0, transcendentals=0),
        name="far",
    )(*[in_vmem(x) for x in operands])[:4]


def solution(mesh):
    rows = P(("groups", "seq", "heads"), "sub")
    weights = P("sub", None, ("groups", "seq", "heads"))
    return jax.shard_map(
        on_device,
        mesh=mesh,
        in_specs=(rows, rows, rows, rows, weights),
        out_specs=(rows, rows, rows, weights),
        check_vma=False,
    )
```

time: 23.6 us -> 22.9 us (0.970)
  starting transfers between devices: 13.3 us -> 12.7 us
    ppermute x8, starting transfers between devices: 13.3 us -> 12.7 us  [flip(): return lax.ppermute(block, AXES, [(i, i ^ mask) for i in range(size)])]
  transfers between devices with their start and end apart: 8 -> 8, of which waited for: 3 -> 4; matrix products, arithmetic and copies ran while one was open for 0% -> 0% of each run, Pallas kernels for 15% -> 15%
where the time goes in v5:
time: 22.9 us; the launch traced here: 22.8 us
  starting transfers between devices  12.7 us (55%)
  Pallas kernels  7.13 us (31%)
  waiting for transfers between devices  2.11 us (9%)
  between operations  0.72 us (3%)
    ppermute x8, starting transfers between devices, flip(): return lax.ppermute(block, AXES, [(i, i ^ mask) for i in range(size)])  12.7 us
    pallas_call x2, Pallas kernels, call(): pl.pallas_call(kernel, out_shape=outs, in_specs=[IN_VMEM] * len(operands)...  3.46 us
    ppermute x8, waiting for transfers between devices, flip(): return lax.ppermute(block, AXES, [(i, i ^ mask) for i in range(size)])  2.11 us
    pallas_call x1, Pallas kernels, on_device(): pl.pallas_call(functools.partial(top_kernel, bits, scales), out_shape=[pl...  2.05 us
    pallas_call x1, Pallas kernels, on_device(): pl.pallas_call(functools.partial(far_kernel, bits, scales), out_shape=(ou...  1.61 us
  transfers between devices with their start and end apart: 8, of which 4 were waited for; matrix products, arithmetic and copies ran while one was open for 0% of the time, Pallas kernels for 15%

profile of v5, /device:TPU:0, one launch (start us, length us, event | category | flops | bytes accessed | tf_op | source)
XLA Modules:
  0.0 22.8 jit_solution(7872886071429359881)
XLA Ops:
  0.6 0.0 copy-start.4
  0.6 0.0 copy-start.3
  0.7 0.0 copy-start.2
  0.7 0.0 copy-start.1
  0.7 0.0 copy-start
  0.7 2.1 %top_states.1 = (bf16[4,128,512]{2,1,0:T(8,128)(2,1)S(1)}, bf16[2,128,128]{2,1,0:T(8,128)(2,1)S(1)}, bf16[2,128,128]{2,1,0:T(8,128)(2,1)S(1)}) custom-call(bf16[512,512]{1,0:T(8,128)(2,1)} %refs_0_.2, bf16[512,512]{1,0:T(8,128)(2,1)} %refs_0_.3, bf16[512,512]{1,0:T(8,128)(2,1)} %refs_1_.3, bf16[512,512]{1,0:T(8,128)(2,1)} %refs_2_.3, f32[4,8,512]{2,1,0:T(8,128)} %refs_3_.3), custom_call_target="tpu_custom_call" | custom-call | flops 33554432000 | tf_op jit(solution)/shard_map/top_states/pallas_call | solution.py:307
  2.7 4.0 %collective-permute-start.5 = (bf16[2,128,128]{2,1,0:T(8,128)(2,1)S(1)}, bf16[2,128,128]{2,1,0:T(8,128)(2,1)S(1)}, u32[]{:S(2)}, u32[]{:S(2)}) collective-permute-start(bf16[2,128,128]{2,1,0:T(8,128)(2,1)S(1)} %get-tuple-element.29), channel_id=1, source_target_pairs={{0,6},{2,4},{4,2},{6,0},{8,14},{10,12},{12,10},{14,8},{1,7},{3,5},... | collective-permute-start | bytes 196616 | tf_op jit(solution)/shard_map/ppermute | solution.py:29
  6.8 0.5 %collective-permute-start.3 = (bf16[2,128,128]{2,1,0:T(8,128)(2,1)S(1)}, bf16[2,128,128]{2,1,0:T(8,128)(2,1)S(1)}, u32[]{:S(2)}, u32[]{:S(2)}) collective-permute-start(bf16[2,128,128]{2,1,0:T(8,128)(2,1)S(1)} %get-tuple-element.29), channel_id=1, source_target_pairs={{0,2},{2,0},{4,6},{6,4},{8,10},{10,8},{12,14},{14,12},{1,3},{3,1},... | collective-permute-start | bytes 196616 | tf_op jit(solution)/shard_map/ppermute | solution.py:29
  7.3 0.1 collective-permute-start.4
  7.4 0.0 copy-done.4
  7.4 0.0 copy-done.3
  7.4 0.0 copy-done.2
  7.4 0.0 copy-done.1
  7.4 0.0 copy-done
  7.4 0.7 %low_states.1 = (bf16[4,128,512]{2,1,0:T(8,128)(2,1)S(1)}, bf16[4,128,512]{2,1,0:T(8,128)(2,1)S(1)}, bf16[4,128,128]{2,1,0:T(8,128)(2,1)S(1)}, bf16[4,128,128]{2,1,0:T(8,128)(2,1)S(1)}) custom-call(bf16[512,512]{1,0:T(8,128)(2,1)S(1)} %copy-done, bf16[512,512]{1,0:T(8,128)(2,1)S(1)} %copy-done.1, bf16[512,512]{1,0:T(8,128)(2,1)S(1)} %copy-done.2, ...), custom_call_target="tpu_custom_call" | custom-call | flops 33554432000 | tf_op jit(solution)/shard_map/low_states/pallas_call | solution.py:281
  8.2 1.9 %collective-permute-start = (bf16[4,128,128]{2,1,0:T(8,128)(2,1)S(1)}, bf16[4,128,128]{2,1,0:T(8,128)(2,1)S(1)}, u32[]{:S(2)}, u32[]{:S(2)}) collective-permute-start(bf16[4,128,128]{2,1,0:T(8,128)(2,1)S(1)} %get-tuple-element.22), channel_id=1, source_target_pairs={{0,2},{2,0},{4,6},{6,4},{8,10},{10,8},{12,14},{14,12},{1,3},{3,1},... | collective-permute-start | bytes 393224 | tf_op jit(solution)/shard_map/ppermute | solution.py:29
  10.1 1.6 %collective-permute-start.1 = (bf16[4,128,128]{2,1,0:T(8,128)(2,1)S(1)}, bf16[4,128,128]{2,1,0:T(8,128)(2,1)S(1)}, u32[]{:S(2)}, u32[]{:S(2)}) collective-permute-start(bf16[4,128,128]{2,1,0:T(8,128)(2,1)S(1)} %get-tuple-element.27), channel_id=1, source_target_pairs={{0,4},{2,6},{4,0},{6,2},{8,12},{10,14},{12,8},{14,10},{1,5},{3,7},... | collective-permute-start | bytes 393224 | tf_op jit(solution)/shard_map/ppermute | solution.py:29
  11.6 0.2 collective-permute-done.4
  11.8 0.0 collective-permute-done.5
  11.8 0.0 collective-permute-done.3
  11.9 4.0 %collective-permute-start.7 = (bf16[2,128,128]{2,1,0:T(8,128)(2,1)S(1)}, bf16[2,128,128]{2,1,0:T(8,128)(2,1)S(1)}, u32[]{:S(2)}, u32[]{:S(2)}) collective-permute-start(bf16[2,128,128]{2,1,0:T(8,128)(2,1)S(1)} %add_convert_fusion), channel_id=1, source_target_pairs={{0,10},{2,8},{4,14},{6,12},{8,2},{10,0},{12,6},{14,4},{1,11},{3,9}... | collective-permute-start | bytes 196616 | tf_op jit(solution)/shard_map/ppermute | solution.py:29
  15.8 0.3 %collective-permute-start.6 = (bf16[2,128,128]{2,1,0:T(8,128)(2,1)S(1)}, bf16[2,128,128]{2,1,0:T(8,128)(2,1)S(1)}, u32[]{:S(2)}, u32[]{:S(2)}) collective-permute-start(bf16[2,128,128]{2,1,0:T(8,128)(2,1)S(1)} %add_convert_fusion), channel_id=1, source_target_pairs={{0,8},{2,10},{4,12},{6,14},{8,0},{10,2},{12,4},{14,6},{1,9},{3,11}... | collective-permute-start | bytes 196616 | tf_op jit(solution)/shard_map/ppermute | solution.py:29
  16.2 0.0 collective-permute-done.1.refs_10_
  16.2 0.3 %collective-permute-start.2 = (bf16[4,128,128]{2,1,0:T(8,128)(2,1)S(1)}, bf16[4,128,128]{2,1,0:T(8,128)(2,1)S(1)}, u32[]{:S(2)}, u32[]{:S(2)}) collective-permute-start(bf16[4,128,128]{2,1,0:T(8,128)(2,1)S(1)} %collective-permute-done.1.refs_10_), channel_id=1, source_target_pairs={{0,2},{2,0},{4,6},{6,4},{8,10},{10,8},{12,14},{14,12},{1,3},{3,1},... | collective-permute-start | bytes 393224 | tf_op jit(solution)/shard_map/ppermute | solution.py:29
  16.5 0.0 collective-permute-done.refs_7_.refs_9_
  16.5 2.7 %near.1 = (f32[4,128,512]{2,1,0:T(8,128)S(1)}, f32[4,8,512]{2,1,0:T(8,128)S(1)}, f32[4,512,128]{2,1,0:T(8,128)S(1)}, f32[4,512,128]{2,1,0:T(8,128)S(1)}) custom-call(bf16[512,512]{1,0:T(8,128)(2,1)S(1)} %copy-done, bf16[512,512]{1,0:T(8,128)(2,1)S(1)} %copy-done.1, bf16[512,512]{1,0:T(8,128)(2,1)S(1)} %copy-done.2, bf16[512,512]{1,0:T(8,128)(2,1)S(1)} %copy-done.3, ...), custom_call_target="tpu_custom_call" | custom-call | flops 33554432000 | tf_op jit(solution)/shard_map/near/pallas_call | solution.py:281
  19.2 0.5 %collective-permute-done.7.refs_13_ = bf16[2,128,128]{2,1,0:T(8,128)(2,1)S(1)} collective-permute-done((bf16[2,128,128]{2,1,0:T(8,128)(2,1)S(1)}, bf16[2,128,128]{2,1,0:T(8,128)(2,1)S(1)}, u32[]{:S(2)}, u32[]{:S(2)}) %collective-permute-start.7) | collective-permute-done | bytes 65568 | tf_op jit(solution)/shard_map/ppermute | solution.py:29
  19.7 1.3 %collective-permute-done.6.refs_12_ = bf16[2,128,128]{2,1,0:T(8,128)(2,1)S(1)} collective-permute-done((bf16[2,128,128]{2,1,0:T(8,128)(2,1)S(1)}, bf16[2,128,128]{2,1,0:T(8,128)(2,1)S(1)}, u32[]{:S(2)}, u32[]{:S(2)}) %collective-permute-start.6) | collective-permute-done | bytes 65568 | tf_op jit(solution)/shard_map/ppermute | solution.py:29
  21.1 0.1 collective-permute-done.2.refs_11_
  21.1 1.6 %far.1 = (bf16[512,512]{1,0:T(8,128)(2,1)}, bf16[512,512]{1,0:T(8,128)(2,1)}, bf16[512,512]{1,0:T(8,128)(2,1)}, f32[4,8,512]{2,1,0:T(8,128)}, f32[4,128,512]{2,1,0:T(8,128)S(1)}) custom-call(bf16[512,512]{1,0:T(8,128)(2,1)S(1)} %copy-done.1, bf16[512,512]{1,0:T(8,128)(2,1)S(1)} %copy-done.2, ...), custom_call_target="tpu_custom_call", output_to_operand_aliasing={{4}: (5, {})} | custom-call | flops 33554432000 | tf_op jit(solution)/shard_map/far/pallas_call | solution.py:352
  (1 shorter events, 0.0 us)
Async XLA Ops:
  0.6 6.8 %copy-start.4 = (f32[4,8,512]{2,1,0:T(8,128)S(1)}, f32[4,8,512]{2,1,0:T(8,128)}, u32[]{:S(2)}) copy-start(f32[4,8,512]{2,1,0:T(8,128)} %refs_3_.3) | copy-start | bytes 196612
  0.6 6.8 %copy-start.3 = (bf16[512,512]{1,0:T(8,128)(2,1)S(1)}, bf16[512,512]{1,0:T(8,128)(2,1)}, u32[]{:S(2)}) copy-start(bf16[512,512]{1,0:T(8,128)(2,1)} %refs_2_.3) | copy-start | bytes 1572868
  0.7 6.8 %copy-start.2 = (bf16[512,512]{1,0:T(8,128)(2,1)S(1)}, bf16[512,512]{1,0:T(8,128)(2,1)}, u32[]{:S(2)}) copy-start(bf16[512,512]{1,0:T(8,128)(2,1)} %refs_1_.3) | copy-start | bytes 1572868
  0.7 6.8 %copy-start.1 = (bf16[512,512]{1,0:T(8,128)(2,1)S(1)}, bf16[512,512]{1,0:T(8,128)(2,1)}, u32[]{:S(2)}) copy-start(bf16[512,512]{1,0:T(8,128)(2,1)} %refs_0_.3) | copy-start | bytes 1572868
  0.7 6.7 %copy-start = (bf16[512,512]{1,0:T(8,128)(2,1)S(1)}, bf16[512,512]{1,0:T(8,128)(2,1)}, u32[]{:S(2)}) copy-start(bf16[512,512]{1,0:T(8,128)(2,1)} %refs_0_.2) | copy-start | bytes 1572868
  2.7 9.1 %collective-permute-start.5 = (bf16[2,128,128]{2,1,0:T(8,128)(2,1)S(1)}, bf16[2,128,128]{2,1,0:T(8,128)(2,1)S(1)}, u32[]{:S(2)}, u32[]{:S(2)}) collective-permute-start(bf16[2,128,128]{2,1,0:T(8,128)(2,1)S(1)} %get-tuple-element.29), channel_id=1, source_target_pairs={{0,6},{2,4},{4,2},{6,0},{8,14},{10,12},{12,10},{14,8},{1,7},{3,5},... | collective-permute-start | bytes 196616 | tf_op jit(solution)/shard_map/ppermute | solution.py:29
  6.8 5.1 %collective-permute-start.3 = (bf16[2,128,128]{2,1,0:T(8,128)(2,1)S(1)}, bf16[2,128,128]{2,1,0:T(8,128)(2,1)S(1)}, u32[]{:S(2)}, u32[]{:S(2)}) collective-permute-start(bf16[2,128,128]{2,1,0:T(8,128)(2,1)S(1)} %get-tuple-element.29), channel_id=1, source_target_pairs={{0,2},{2,0},{4,6},{6,4},{8,10},{10,8},{12,14},{14,12},{1,3},{3,1},... | collective-permute-start | bytes 196616 | tf_op jit(solution)/shard_map/ppermute | solution.py:29
  7.3 4.5 %collective-permute-start.4 = (bf16[2,128,128]{2,1,0:T(8,128)(2,1)S(1)}, bf16[2,128,128]{2,1,0:T(8,128)(2,1)S(1)}, u32[]{:S(2)}, u32[]{:S(2)}) collective-permute-start(bf16[2,128,128]{2,1,0:T(8,128)(2,1)S(1)} %get-tuple-element.28), channel_id=1, source_target_pairs={{0,4},{2,6},{4,0},{6,2},{8,12},{10,14},{12,8},{14,10},{1,5},{3,7},... | collective-permute-start | bytes 196616 | tf_op jit(solution)/shard_map/ppermute | solution.py:29
  8.2 8.3 %collective-permute-start = (bf16[4,128,128]{2,1,0:T(8,128)(2,1)S(1)}, bf16[4,128,128]{2,1,0:T(8,128)(2,1)S(1)}, u32[]{:S(2)}, u32[]{:S(2)}) collective-permute-start(bf16[4,128,128]{2,1,0:T(8,128)(2,1)S(1)} %get-tuple-element.22), channel_id=1, source_target_pairs={{0,2},{2,0},{4,6},{6,4},{8,10},{10,8},{12,14},{14,12},{1,3},{3,1},... | collective-permute-start | bytes 393224 | tf_op jit(solution)/shard_map/ppermute | solution.py:29
  10.1 6.1 %collective-permute-start.1 = (bf16[4,128,128]{2,1,0:T(8,128)(2,1)S(1)}, bf16[4,128,128]{2,1,0:T(8,128)(2,1)S(1)}, u32[]{:S(2)}, u32[]{:S(2)}) collective-permute-start(bf16[4,128,128]{2,1,0:T(8,128)(2,1)S(1)} %get-tuple-element.27), channel_id=1, source_target_pairs={{0,4},{2,6},{4,0},{6,2},{8,12},{10,14},{12,8},{14,10},{1,5},{3,7},... | collective-permute-start | bytes 393224 | tf_op jit(solution)/shard_map/ppermute | solution.py:29
  11.9 7.9 %collective-permute-start.7 = (bf16[2,128,128]{2,1,0:T(8,128)(2,1)S(1)}, bf16[2,128,128]{2,1,0:T(8,128)(2,1)S(1)}, u32[]{:S(2)}, u32[]{:S(2)}) collective-permute-start(bf16[2,128,128]{2,1,0:T(8,128)(2,1)S(1)} %add_convert_fusion), channel_id=1, source_target_pairs={{0,10},{2,8},{4,14},{6,12},{8,2},{10,0},{12,6},{14,4},{1,11},{3,9}... | collective-permute-start | bytes 196616 | tf_op jit(solution)/shard_map/ppermute | solution.py:29
  15.8 5.2 %collective-permute-start.6 = (bf16[2,128,128]{2,1,0:T(8,128)(2,1)S(1)}, bf16[2,128,128]{2,1,0:T(8,128)(2,1)S(1)}, u32[]{:S(2)}, u32[]{:S(2)}) collective-permute-start(bf16[2,128,128]{2,1,0:T(8,128)(2,1)S(1)} %add_convert_fusion), channel_id=1, source_target_pairs={{0,8},{2,10},{4,12},{6,14},{8,0},{10,2},{12,4},{14,6},{1,9},{3,11}... | collective-permute-start | bytes 196616 | tf_op jit(solution)/shard_map/ppermute | solution.py:29
  16.2 5.0 %collective-permute-start.2 = (bf16[4,128,128]{2,1,0:T(8,128)(2,1)S(1)}, bf16[4,128,128]{2,1,0:T(8,128)(2,1)S(1)}, u32[]{:S(2)}, u32[]{:S(2)}) collective-permute-start(bf16[4,128,128]{2,1,0:T(8,128)(2,1)S(1)} %collective-permute-done.1.refs_10_), channel_id=1, source_target_pairs={{0,2},{2,0},{4,6},{6,4},{8,10},{10,8},{12,14},{14,12},{1,3},{3,1},... | collective-permute-start | bytes 393224 | tf_op jit(solution)/shard_map/ppermute | solution.py:29

commit v6 on v5

--- a/solution.py
+++ b/solution.py
@@ -12,6 +12,7 @@
 LOW = jnp.bfloat16
 ROWS = 256
 GROUP = 2
+CHUNKS = 1
 
 
 def nt(left, right):
@@ -29,6 +30,14 @@
     return lax.ppermute(block, AXES, [(i, i ^ mask) for i in range(size)])
 
 
+def swap_halves(block, bit, upper_turns):
+    routes = []
+    for i in range(lax.axis_size(AXES)):
+        upper = (i >> bit) & 1 == 1
+        routes.append((i, i ^ (1 << bit) ^ (1 if upper == upper_turns else 0)))
+    return lax.ppermute(block, AXES, routes)
+
+
 def block_index():
     return lax.axis_index("seq") * lax.axis_size("heads") + lax.axis_index("heads")
 
@@ -46,71 +55,89 @@
     return [base] + [base / math.sqrt(2.0 ** (level - 1)) for level in range(1, count)]
 
 
-def top_kernel(bits, scales, q_hbm, k_hbm, v_hbm, g_hbm, w_hbm, t_out, own_out, other_out, left_buf, right_buf, w_buf, sems):
-    rows, heads, tokens, width = left_buf.shape
+def top_kernel(
+    bits, scales, q_hbm, k_hbm, v_hbm, g_hbm, w_hbm, t_out, own_out, other_out, left_buf, right_buf, w_buf, sems
+):
+    heads, width, tokens = t_out.shape
     half = heads // 2
+    span = tokens // CHUNKS
     place = block_index()
     low_bit = place & 1
 
+    def copies(index, upper):
+        left, right = (q_hbm, g_hbm) if upper else (k_hbm, v_hbm)
+        made = []
+        for chunk in range(CHUNKS):
+            rows = pl.ds(chunk * span, span)
+            made.append(
+                [
+                    pltpu.make_async_copy(left.at[rows], left_buf.at[index, rows], sems.at[0, index, chunk]),
+                    pltpu.make_async_copy(right.at[rows], right_buf.at[index, rows], sems.at[1, index, chunk]),
+                ]
+            )
+        if upper:
+            level_row = w_hbm.at[:, pl.ds(index + 3, 1), :]
+            made[0].append(pltpu.make_async_copy(level_row, w_buf.at[index], sems.at[2, index, 0]))
+        return made
+
     def states(index, upper):
         level = index + 3
-        for first in range(0, heads, GROUP):
-            lefts, rights = [], []
-            for h in range(first, first + GROUP):
-                for copy in copies(index, h, upper):
-                    copy.wait()
-                turned = left_buf[index, h].T
-                if level == bits:
-                    t_out[h] = turned
-                if upper:
-                    turned = (w_buf[index, h] * turned.astype(jnp.float32)).astype(LOW)
-                lefts.append(turned)
-                rights.append(right_buf[index, h])
-            product = nn(jnp.concatenate(lefts, 0), jnp.concatenate(rights, 1))
-            for i in range(GROUP):
-                h = first + i
-                part = slice(i * width, i * width + width)
-                state = product[part, part]
-                if upper:
-                    state = scales[level] * state
-                state = state.astype(LOW)
-                row = index * half + h % half
-
-                @pl.when(low_bit == h // half)
-                def _():
-                    own_out[row] = state
-
-                @pl.when(low_bit != h // half)
-                def _():
-                    other_out[row] = state
-
-    def copies(index, h, upper):
-        left, right = (q_hbm, g_hbm) if upper else (k_hbm, v_hbm)
-        columns = pl.ds(h * width, width)
-        made = [
-            pltpu.make_async_copy(left.at[:, columns], left_buf.at[index, h], sems.at[0, index, h]),
-            pltpu.make_async_copy(right.at[:, columns], right_buf.at[index, h], sems.at[1, index, h]),
-        ]
-        if upper:
-            row = w_hbm.at[h, pl.ds(index + 3, 1), :]
-            made.append(pltpu.make_async_copy(row, w_buf.at[index, h], sems.at[2, index, h]))
-        return made
-
-    for index in range(rows):
+        made = copies(index, upper)
+        for group in made:
+            for copy in group:
+                copy.start()
+        totals = [None] * (heads // GROUP)
+        for chunk, group in enumerate(made):
+            for copy in group:
+                copy.wait()
+            rows = slice(chunk * span, chunk * span + span)
+            for pair in range(heads // GROUP):
+                lefts = []
+                for h in range(pair * GROUP, pair * GROUP + GROUP):
+                    turned = left_buf[index, rows, h * width : (h + 1) * width].T
+                    if level == bits:
+                        t_out[h, :, rows] = turned
+                    if upper:
+                        turned = (w_buf[index, h, :, rows] * turned.astype(jnp.float32)).astype(LOW)
+                    lefts.append(turned)
+                columns = slice(pair * GROUP * width, (pair + 1) * GROUP * width)
+                part = nn(jnp.concatenate(lefts, 0), right_buf[index, rows, columns])
+                totals[pair] = part if totals[pair] is None else totals[pair] + part
+        for h in range(heads):
+            block = slice(h % GROUP * width, h % GROUP * width + width)
+            state = totals[h // GROUP][block, block]
+            if upper:
+                state = scales[level] * state
+            state = state.astype(LOW)
+            row = index * half + h % half
+
+            @pl.when(low_bit == h // half)
+            def _():
+                own_out[row] = state
+
+            @pl.when(low_bit != h // half)
+            def _():
+                other_out[row] = state
+
+    for index in range(bits - 2):
         bit = (place >> (index + 2)) & 1
         for value in (0, 1):
 
             @pl.when(bit == value)
             def _():
-                for h in range(heads):
-                    for copy in copies(index, h, value == 1):
-                        copy.start()
                 states(index, value == 1)
 
 
-def low_kernel(
-    bits, scales, q_ref, k_ref, v_ref, g_ref, w_ref, t_ref, qt_out, kt_out, d1_out, d2_out
-):
+def mixed_state(level, scale, h, place, query_t, key_t, w_ref, v_ref, g_ref):
+    width = query_t.shape[0]
+    upper = ((place >> (level - 1)) & 1) == 1
+    scaled = (w_ref[h, pl.ds(level, 1), :] * query_t.astype(jnp.float32)).astype(LOW)
+    left = jnp.where(upper, scaled, key_t)
+    right = jnp.where(upper, head(g_ref, h, width), head(v_ref, h, width))
+    return (jnp.where(upper, scale, 1.0) * nn(left, right)).astype(LOW)
+
+
+def second_kernel(bits, scale, q_ref, k_ref, v_ref, g_ref, w_ref, t_ref, qt_out, kt_out, d2_out):
     heads, width = t_ref.shape[:2]
     place = block_index()
     top = ((place >> (bits - 1)) & 1) == 1
@@ -121,12 +148,13 @@
         key_t = jnp.where(top, other, turned)
         qt_out[h] = query_t
         kt_out[h] = key_t
-        for level, out in ((1, d1_out), (2, d2_out)):
-            upper = ((place >> (level - 1)) & 1) == 1
-            scaled = (w_ref[h, pl.ds(level, 1), :] * query_t.astype(jnp.float32)).astype(LOW)
-            left = jnp.where(upper, scaled, key_t)
-            right = jnp.where(upper, head(g_ref, h, width), head(v_ref, h, width))
-            out[h] = (jnp.where(upper, scales[level], 1.0) * nn(left, right)).astype(LOW)
+        d2_out[h] = mixed_state(2, scale, h, place, query_t, key_t, w_ref, v_ref, g_ref)
+
+
+def first_kernel(scale, v_ref, g_ref, w_ref, qt_ref, kt_ref, d1_out):
+    place = block_index()
+    for h in range(qt_ref.shape[0]):
+        d1_out[h] = mixed_state(1, scale, h, place, qt_ref[h], kt_ref[h], w_ref, v_ref, g_ref)
 
 
 def near_head(scale, h, q_ref, k_ref, v_ref, g_ref, w_ref, kt_ref, nk_out, nv_out, local):
@@ -168,20 +196,13 @@
             ref[h, rows, start:] += part
 
 
-def near_kernel(scales, *refs):
-    ins, (qt_ref, r1_ref, sum_out, gw_out, nk_out, nv_out) = refs[:6], refs[6:]
-    g_ref, w_ref = ins[3], ins[4]
-    upper = (block_index() & 1) == 1
+def near_kernel(scale, *refs):
+    ins, (sum_out, gw_out, nk_out, nv_out) = refs[:6], refs[6:]
     for h in range(sum_out.shape[0]):
         gw_out[h] = jnp.zeros(gw_out.shape[1:], jnp.float32)
-        back, weight = near_head(scales[0], h, *ins, nk_out, nv_out, h)
+        back, weight = near_head(scale, h, *ins, nk_out, nv_out, h)
         store_sums(sum_out, h, slice(None), back)
         store_sums(gw_out, h, pl.ds(0, 1), weight)
-        products = nt(jnp.where(upper, r1_ref[h], 0), head(g_ref, h, sum_out.shape[1]))
-        sum_out[h] += (scales[1] * w_ref[h, pl.ds(1, 1), :]) * products
-        gw_out[h, pl.ds(1, 1), :] = scales[1] * jnp.sum(
-            products * qt_ref[h].astype(jnp.float32), axis=0, keepdims=True
-        )
 
 
 def spread(blocks):
@@ -198,7 +219,7 @@
 def far_kernel(bits, scales, *refs):
     k_ref, v_ref, g_ref, w_ref, qt_ref, _, weight_ref, nk_ref, nv_ref = refs[:9]
     (r1_ref, z2_ref, d2_ref), refs = refs[9:12], refs[12:]
-    own_refs, other_refs, refs = refs[: bits - 2], refs[bits - 2 : 2 * bits - 4], refs[2 * bits - 4 :]
+    late_refs, early_refs, refs = refs[: bits - 2], refs[bits - 2 : 2 * bits - 4], refs[2 * bits - 4 :]
     gq_hbm, gk_hbm, gv_hbm, gw_hbm, sum_ref, gq_buf, gk_buf, gv_buf, gw_buf, sems, w_sem = refs
     heads, width, tokens = sum_ref.shape
     half = heads // 2
@@ -214,8 +235,9 @@
             return r1_ref[h]
         if level == 2:
             return z2_ref[h].astype(jnp.float32) + d2_ref[h].astype(jnp.float32)
-        own_ref, other_ref = own_refs[level - 3], other_refs[level - 3]
-        return jnp.where(low_bit == h // half, own_ref[h % half], other_ref[h % half])
+        early_ref, late_ref = early_refs[level - 3], late_refs[level - 3]
+        early = (low_bit == h // half) == is_upper(level)
+        return jnp.where(early, early_ref[h % half], late_ref[h % half])
 
     def send(i, first, buf, hbm):
         span = pl.ds(first * width, GROUP * width)
@@ -224,6 +246,28 @@
         copies.append(copy)
 
     gw_buf[...] = weight_ref[...]
+    for level in range(1, bits + 1):
+
+        @pl.when(is_upper(level))
+        def _():
+            for first in range(0, heads, GROUP):
+                group = range(first, first + GROUP)
+                siblings = spread([received(level, h).astype(LOW) for h in group])
+                products = nt(siblings, g_ref[:, first * width : (first + GROUP) * width])
+                for i, h in enumerate(group):
+                    mine = products[i * width : i * width + width]
+                    sum_ref[h] += (scales[level] * w_ref[h, pl.ds(level, 1), :]) * mine
+                    gw_buf[h, pl.ds(level, 1), :] = scales[level] * jnp.sum(
+                        mine * qt_ref[h].astype(jnp.float32), axis=0, keepdims=True
+                    )
+
+    copy = pltpu.make_async_copy(gw_buf, gw_hbm, w_sem)
+    copy.start()
+    copies.append(copy)
+    for first in range(0, heads, GROUP):
+        for i in range(GROUP):
+            gq_buf[first // GROUP, :, i * width : i * width + width] = sum_ref[first + i].astype(LOW).T
+        send(2, first, gq_buf, gq_hbm)
     for first in range(0, heads, GROUP):
         group = range(first, first + GROUP)
         reverses = []
@@ -241,28 +285,6 @@
         gv_buf[first // GROUP] = (near_v + nn(key, low)).astype(LOW)
         send(0, first, gk_buf, gk_hbm)
         send(1, first, gv_buf, gv_hbm)
-    for level in range(2, bits + 1):
-
-        @pl.when(is_upper(level))
-        def _():
-            for first in range(0, heads, GROUP):
-                group = range(first, first + GROUP)
-                siblings = spread([received(level, h).astype(LOW) for h in group])
-                products = nt(siblings, g_ref[:, first * width : (first + GROUP) * width])
-                for i, h in enumerate(group):
-                    mine = products[i * width : i * width + width]
-                    sum_ref[h] += (scales[level] * w_ref[h, pl.ds(level, 1), :]) * mine
-                    gw_buf[h, pl.ds(level, 1), :] = scales[level] * jnp.sum(
-                        mine * qt_ref[h].astype(jnp.float32), axis=0, keepdims=True
-                    )
-
-    copy = pltpu.make_async_copy(gw_buf, gw_hbm, w_sem)
-    copy.start()
-    copies.append(copy)
-    for first in range(0, heads, GROUP):
-        for i in range(GROUP):
-            gq_buf[first // GROUP, :, i * width : i * width + width] = sum_ref[first + i].astype(LOW).T
-        send(2, first, gq_buf, gq_hbm)
     for copy in copies:
         copy.wait()
 
@@ -303,7 +325,7 @@
     halves = (((bits - 2) * half, width, width), LOW)
     weight_rows = ((heads, levels, tokens), f32)
     outs = [turned, halves, halves]
-    chosen = pltpu.VMEM((bits - 2, heads, tokens, width), LOW)
+    chosen = pltpu.VMEM((bits - 2, tokens, heads * width), LOW)
     t_v, own, other = pl.pallas_call(
         functools.partial(top_kernel, bits, scales),
         out_shape=[pltpu.VMEM(shape, dtype) for shape, dtype in outs],
@@ -311,7 +333,7 @@
         out_specs=[IN_VMEM] * len(outs),
         scratch_shapes=[
             chosen, chosen, pltpu.VMEM((bits - 2, heads, 1, tokens), f32),
-            pltpu.SemaphoreType.DMA((3, bits - 2, heads)),
+            pltpu.SemaphoreType.DMA((3, bits - 2, CHUNKS)),
         ],
         compiler_params=pltpu.CompilerParams(vmem_limit_bytes=LIMIT),
         cost_estimate=pl.CostEstimate(flops=cost, bytes_accessed=0, transcendentals=0),
@@ -326,28 +348,32 @@
     got_z = flip(own, 2)
     got_d = flip(other, 3)
     quad = as_f(own) + as_f(got_x) + as_f(got_z) + as_f(got_d)
-    qt, kt, d1, d2 = call(
-        functools.partial(low_kernel, bits, scales), "low_states", cost,
-        [turned, turned, full, full], [q_v, k_v, v_v, g_v, w_v, t_v],
+    qt, kt, d2 = call(
+        functools.partial(second_kernel, bits, scales[2]), "second_level", cost,
+        [turned, turned, full], [q_v, k_v, v_v, g_v, w_v, t_v],
+    )
+    got_2 = flip(d2, 2)
+    (d1,) = call(
+        functools.partial(first_kernel, scales[1]), "first_level", cost,
+        [full], [v_v, g_v, w_v, qt, kt],
     )
     got_1 = flip(d1, 1)
-    got_2 = flip(d2, 2)
     sums = []
     for bit in range(2, bits):
         sums.append(quad[:half].astype(LOW))
         quad = quad[half:]
         if bit < bits - 1:
             quad = quad + as_f(flip(quad.astype(LOW), 1 << bit))
-    own_half = [flip(x, 1 << (i + 2)) for i, x in enumerate(sums)]
-    other_half = [flip(x, (1 << (i + 2)) ^ 1) for i, x in enumerate(sums)]
+    early_half = [swap_halves(x, i + 2, True) for i, x in enumerate(sums)]
+    late_half = [swap_halves(x, i + 2, False) for i, x in enumerate(sums)]
     diagonal_2 = flip(got_2, 1)
     total, weights, near_k, near_v = call(
-        functools.partial(near_kernel, scales), "near", cost,
+        functools.partial(near_kernel, scales[0]), "near", cost,
         [((heads, width, tokens), f32), weight_rows, *[((heads, tokens, width), f32)] * 2],
-        [q_v, k_v, v_v, g_v, w_v, kt, qt, got_1],
+        [q_v, k_v, v_v, g_v, w_v, kt],
     )
     operands = [k_v, v_v, g_v, w_v, qt, total, weights, near_k, near_v]
-    operands += [got_1, got_2, diagonal_2, *own_half, *other_half]
+    operands += [got_1, got_2, diagonal_2, *late_half, *early_half]
     out = jax.ShapeDtypeStruct((tokens, heads * width), LOW)
     return pl.pallas_call(
         functools.partial(far_kernel, bits, scales),

time: 22.9 us -> 22.4 us (0.978)
  waiting for transfers between devices: 2.11 us -> 0.89 us
  starting transfers between devices: 12.7 us -> 13.9 us
  Pallas kernels: 7.13 us -> 6.61 us
    ppermute x0 -> x2, starting transfers between devices: none -> 4.08 us  [swap_halves(): return lax.ppermute(block, AXES, routes)]
    ppermute x8 -> x6, starting transfers between devices: 12.7 us -> 9.86 us  [flip(): return lax.ppermute(block, AXES, [(i, i ^ mask) for i in range(size)])]
    ppermute x8 -> x6, waiting for transfers between devices: 2.11 us -> 0.38 us  [flip(): return lax.ppermute(block, AXES, [(i, i ^ mask) for i in range(size)])]
    ppermute x0 -> x2, waiting for transfers between devices: none -> 0.51 us  [swap_halves(): return lax.ppermute(block, AXES, routes)]
    pallas_call x1, Pallas kernels: 2.05 us -> 1.76 us  [on_device(): pl.pallas_call(functools.partial(top_kernel, bits, scales), out_shape=[pl...]
    pallas_call x2 -> x3, Pallas kernels: 3.46 us -> 3.37 us  [call(): pl.pallas_call(kernel, out_shape=outs, in_specs=[IN_VMEM] * len(operands)...]
  transfers between devices with their start and end apart: 8 -> 8, of which waited for: 4 -> 3; matrix products, arithmetic and copies ran while one was open for 0% -> 0% of each run, Pallas kernels for 15% -> 15%
where the time goes in v6:
time: 22.4 us; the launch traced here: 22.2 us
  starting transfers between devices  13.9 us (62%)
  Pallas kernels  6.61 us (30%)
  waiting for transfers between devices  0.89 us (4%)
  between operations  0.72 us (3%)
    ppermute x6, starting transfers between devices, flip(): return lax.ppermute(block, AXES, [(i, i ^ mask) for i in range(size)])  9.86 us
    ppermute x2, starting transfers between devices, swap_halves(): return lax.ppermute(block, AXES, routes)  4.08 us
    pallas_call x3, Pallas kernels, call(): pl.pallas_call(kernel, out_shape=outs, in_specs=[IN_VMEM] * len(operands)...  3.37 us
    pallas_call x1, Pallas kernels, on_device(): pl.pallas_call(functools.partial(top_kernel, bits, scales), out_shape=[pl...  1.76 us
    pallas_call x1, Pallas kernels, on_device(): pl.pallas_call(functools.partial(far_kernel, bits, scales), out_shape=(ou...  1.48 us
    ppermute x2, waiting for transfers between devices, swap_halves(): return lax.ppermute(block, AXES, routes)  0.51 us
  transfers between devices with their start and end apart: 8, of which 3 were waited for; matrix products, arithmetic and copies ran while one was open for 0% of the time, Pallas kernels for 15%

profile of v6, /device:TPU:0, one launch (start us, length us, event | category | flops | bytes accessed | tf_op | source)
XLA Modules:
  0.0 22.2 jit_solution(7096020425370219952)
XLA Ops:
  0.6 0.0 copy-start.4
  0.6 0.0 copy-start.3
  0.7 0.0 copy-start.2
  0.7 0.0 copy-start.1
  0.7 0.0 copy-start
  0.7 1.8 %top_states.1 = (bf16[4,128,512]{2,1,0:T(8,128)(2,1)S(1)}, bf16[2,128,128]{2,1,0:T(8,128)(2,1)S(1)}, bf16[2,128,128]{2,1,0:T(8,128)(2,1)S(1)}) custom-call(bf16[512,512]{1,0:T(8,128)(2,1)} %refs_0_.2, bf16[512,512]{1,0:T(8,128)(2,1)} %refs_0_.3, bf16[512,512]{1,0:T(8,128)(2,1)} %refs_1_.3, bf16[512,512]{1,0:T(8,128)(2,1)} %refs_2_.3, f32[4,8,512]{2,1,0:T(8,128)} %refs_3_.3), custom_call_target="tpu_custom_call" | custom-call | flops 33554432000 | tf_op jit(solution)/shard_map/top_states/pallas_call | solution.py:329
  2.4 4.0 %collective-permute-start.5 = (bf16[2,128,128]{2,1,0:T(8,128)(2,1)S(1)}, bf16[2,128,128]{2,1,0:T(8,128)(2,1)S(1)}, u32[]{:S(2)}, u32[]{:S(2)}) collective-permute-start(bf16[2,128,128]{2,1,0:T(8,128)(2,1)S(1)} %get-tuple-element.27), channel_id=1, source_target_pairs={{0,6},{2,4},{4,2},{6,0},{8,14},{10,12},{12,10},{14,8},{1,7},{3,5},... | collective-permute-start | bytes 196616 | tf_op jit(solution)/shard_map/ppermute | solution.py:30
  6.5 0.5 %collective-permute-start.3 = (bf16[2,128,128]{2,1,0:T(8,128)(2,1)S(1)}, bf16[2,128,128]{2,1,0:T(8,128)(2,1)S(1)}, u32[]{:S(2)}, u32[]{:S(2)}) collective-permute-start(bf16[2,128,128]{2,1,0:T(8,128)(2,1)S(1)} %get-tuple-element.27), channel_id=1, source_target_pairs={{0,2},{2,0},{4,6},{6,4},{8,10},{10,8},{12,14},{14,12},{1,3},{3,1},... | collective-permute-start | bytes 196616 | tf_op jit(solution)/shard_map/ppermute | solution.py:30
  7.0 0.1 collective-permute-start.4
  7.1 0.0 copy-done.4
  7.1 0.0 copy-done.3
  7.1 0.0 copy-done.2
  7.1 0.0 copy-done.1
  7.1 0.0 copy-done
  7.1 0.5 %second_level.1 = (bf16[4,128,512]{2,1,0:T(8,128)(2,1)S(1)}, bf16[4,128,512]{2,1,0:T(8,128)(2,1)S(1)}, bf16[4,128,128]{2,1,0:T(8,128)(2,1)S(1)}) custom-call(bf16[512,512]{1,0:T(8,128)(2,1)S(1)} %copy-done, bf16[512,512]{1,0:T(8,128)(2,1)S(1)} %copy-done.1, bf16[512,512]{1,0:T(8,128)(2,1)S(1)} %copy-done.2, bf16[512,512]{1,0:T(8,128)(2,1)S(1)} %copy-done.3, ...), custom_call_target="tpu_custom_call" | custom-call | flops 33554432000 | tf_op jit(solution)/shard_map/second_level/pallas_call | solution.py:303
  7.6 0.3 %first_level.1 = bf16[4,128,128]{2,1,0:T(8,128)(2,1)S(1)} custom-call(bf16[512,512]{1,0:T(8,128)(2,1)S(1)} %copy-done.2, bf16[512,512]{1,0:T(8,128)(2,1)S(1)} %copy-done.3, f32[4,8,512]{2,1,0:T(8,128)S(1)} %copy-done.4, bf16[4,128,512]{2,1,0:T(8,128)(2,1)S(1)} %get-tuple-element.19.qt_ref.refs_4_, bf16[4,128,512]{2,1,0:T(8,128)(2,1)S(1)} %get-tuple-element.20.refs_5_.kt_ref), custom_call_target="tpu_custom_call" | custom-call | flops 33554432000 | tf_op jit(solution)/shard_map/first_level/pallas_call | solution.py:303
  7.9 1.9 %collective-permute-start = (bf16[4,128,128]{2,1,0:T(8,128)(2,1)S(1)}, bf16[4,128,128]{2,1,0:T(8,128)(2,1)S(1)}, u32[]{:S(2)}, u32[]{:S(2)}) collective-permute-start(bf16[4,128,128]{2,1,0:T(8,128)(2,1)S(1)} %first_level.1), channel_id=1, source_target_pairs={{0,2},{2,0},{4,6},{6,4},{8,10},{10,8},{12,14},{14,12},{1,3},{3,1},... | collective-permute-start | bytes 393224 | tf_op jit(solution)/shard_map/ppermute | solution.py:30
  9.9 1.6 %collective-permute-start.1 = (bf16[4,128,128]{2,1,0:T(8,128)(2,1)S(1)}, bf16[4,128,128]{2,1,0:T(8,128)(2,1)S(1)}, u32[]{:S(2)}, u32[]{:S(2)}) collective-permute-start(bf16[4,128,128]{2,1,0:T(8,128)(2,1)S(1)} %get-tuple-element.25), channel_id=1, source_target_pairs={{0,4},{2,6},{4,0},{6,2},{8,12},{10,14},{12,8},{14,10},{1,5},{3,7},... | collective-permute-start | bytes 393224 | tf_op jit(solution)/shard_map/ppermute | solution.py:30
  11.4 0.0 collective-permute-done.4
  11.4 0.0 collective-permute-done.5
  11.4 0.0 collective-permute-done.3
  11.5 2.7 %collective-permute-start.7 = (bf16[2,128,128]{2,1,0:T(8,128)(2,1)S(1)}, bf16[2,128,128]{2,1,0:T(8,128)(2,1)S(1)}, u32[]{:S(2)}, u32[]{:S(2)}) collective-permute-start(bf16[2,128,128]{2,1,0:T(8,128)(2,1)S(1)} %add_convert_fusion), channel_id=1, source_target_pairs={{0,8},{2,10},{4,12},{6,14},{8,2},{10,0},{12,6},{14,4},{1,9},{3,11}... | collective-permute-start | bytes 196616 | tf_op jit(solution)/shard_map/ppermute | solution.py:38
  14.1 1.4 %collective-permute-start.6 = (bf16[2,128,128]{2,1,0:T(8,128)(2,1)S(1)}, bf16[2,128,128]{2,1,0:T(8,128)(2,1)S(1)}, u32[]{:S(2)}, u32[]{:S(2)}) collective-permute-start(bf16[2,128,128]{2,1,0:T(8,128)(2,1)S(1)} %add_convert_fusion), channel_id=1, source_target_pairs={{0,10},{2,8},{4,14},{6,12},{8,0},{10,2},{12,4},{14,6},{1,11},{3,9}... | collective-permute-start | bytes 196616 | tf_op jit(solution)/shard_map/ppermute | solution.py:38
  15.6 0.0 collective-permute-done.1.refs_10_
  15.6 1.7 %collective-permute-start.2 = (bf16[4,128,128]{2,1,0:T(8,128)(2,1)S(1)}, bf16[4,128,128]{2,1,0:T(8,128)(2,1)S(1)}, u32[]{:S(2)}, u32[]{:S(2)}) collective-permute-start(bf16[4,128,128]{2,1,0:T(8,128)(2,1)S(1)} %collective-permute-done.1.refs_10_), channel_id=1, source_target_pairs={{0,2},{2,0},{4,6},{6,4},{8,10},{10,8},{12,14},{14,12},{1,3},{3,1},... | collective-permute-start | bytes 393224 | tf_op jit(solution)/shard_map/ppermute | solution.py:30
  17.3 2.6 %near.1 = (f32[4,128,512]{2,1,0:T(8,128)S(1)}, f32[4,8,512]{2,1,0:T(8,128)S(1)}, f32[4,512,128]{2,1,0:T(8,128)S(1)}, f32[4,512,128]{2,1,0:T(8,128)S(1)}) custom-call(bf16[512,512]{1,0:T(8,128)(2,1)S(1)} %copy-done, bf16[512,512]{1,0:T(8,128)(2,1)S(1)} %copy-done.1, bf16[512,512]{1,0:T(8,128)(2,1)S(1)} %copy-done.2, bf16[512,512]{1,0:T(8,128)(2,1)S(1)} %copy-done.3, ...), custom_call_target="tpu_custom_call" | custom-call | flops 33554432000 | tf_op jit(solution)/shard_map/near/pallas_call | solution.py:303
  19.9 0.3 %collective-permute-done.7.refs_13_ = bf16[2,128,128]{2,1,0:T(8,128)(2,1)S(1)} collective-permute-done((bf16[2,128,128]{2,1,0:T(8,128)(2,1)S(1)}, bf16[2,128,128]{2,1,0:T(8,128)(2,1)S(1)}, u32[]{:S(2)}, u32[]{:S(2)}) %collective-permute-start.7) | collective-permute-done | bytes 65568 | tf_op jit(solution)/shard_map/ppermute | solution.py:38
  20.1 0.2 %collective-permute-done.6.refs_12_ = bf16[2,128,128]{2,1,0:T(8,128)(2,1)S(1)} collective-permute-done((bf16[2,128,128]{2,1,0:T(8,128)(2,1)S(1)}, bf16[2,128,128]{2,1,0:T(8,128)(2,1)S(1)}, u32[]{:S(2)}, u32[]{:S(2)}) %collective-permute-start.6) | collective-permute-done | bytes 65568 | tf_op jit(solution)/shard_map/ppermute | solution.py:38
  20.4 0.0 collective-permute-done.refs_9_
  20.4 0.4 %collective-permute-done.2.refs_11_ = bf16[4,128,128]{2,1,0:T(8,128)(2,1)S(1)} collective-permute-done((bf16[4,128,128]{2,1,0:T(8,128)(2,1)S(1)}, bf16[4,128,128]{2,1,0:T(8,128)(2,1)S(1)}, u32[]{:S(2)}, u32[]{:S(2)}) %collective-permute-start.2) | collective-permute-done | bytes 131104 | tf_op jit(solution)/shard_map/ppermute | solution.py:30
  20.7 1.5 %far.1 = (bf16[512,512]{1,0:T(8,128)(2,1)}, bf16[512,512]{1,0:T(8,128)(2,1)}, bf16[512,512]{1,0:T(8,128)(2,1)}, f32[4,8,512]{2,1,0:T(8,128)}, f32[4,128,512]{2,1,0:T(8,128)S(1)}) custom-call(bf16[512,512]{1,0:T(8,128)(2,1)S(1)} %copy-done.1, bf16[512,512]{1,0:T(8,128)(2,1)S(1)} %copy-done.2, ...), custom_call_target="tpu_custom_call", output_to_operand_aliasing={{4}: (5, {})} | custom-call | flops 33554432000 | tf_op jit(solution)/shard_map/far/pallas_call | solution.py:378
  (1 shorter events, 0.0 us)
Async XLA Ops:
  0.6 6.5 %copy-start.4 = (f32[4,8,512]{2,1,0:T(8,128)S(1)}, f32[4,8,512]{2,1,0:T(8,128)}, u32[]{:S(2)}) copy-start(f32[4,8,512]{2,1,0:T(8,128)} %refs_3_.3) | copy-start | bytes 196612
  0.6 6.5 %copy-start.3 = (bf16[512,512]{1,0:T(8,128)(2,1)S(1)}, bf16[512,512]{1,0:T(8,128)(2,1)}, u32[]{:S(2)}) copy-start(bf16[512,512]{1,0:T(8,128)(2,1)} %refs_2_.3) | copy-start | bytes 1572868
  0.7 6.5 %copy-start.2 = (bf16[512,512]{1,0:T(8,128)(2,1)S(1)}, bf16[512,512]{1,0:T(8,128)(2,1)}, u32[]{:S(2)}) copy-start(bf16[512,512]{1,0:T(8,128)(2,1)} %refs_1_.3) | copy-start | bytes 1572868
  0.7 6.5 %copy-start.1 = (bf16[512,512]{1,0:T(8,128)(2,1)S(1)}, bf16[512,512]{1,0:T(8,128)(2,1)}, u32[]{:S(2)}) copy-start(bf16[512,512]{1,0:T(8,128)(2,1)} %refs_0_.3) | copy-start | bytes 1572868
  0.7 6.4 %copy-start = (bf16[512,512]{1,0:T(8,128)(2,1)S(1)}, bf16[512,512]{1,0:T(8,128)(2,1)}, u32[]{:S(2)}) copy-start(bf16[512,512]{1,0:T(8,128)(2,1)} %refs_0_.2) | copy-start | bytes 1572868
  2.4 9.0 %collective-permute-start.5 = (bf16[2,128,128]{2,1,0:T(8,128)(2,1)S(1)}, bf16[2,128,128]{2,1,0:T(8,128)(2,1)S(1)}, u32[]{:S(2)}, u32[]{:S(2)}) collective-permute-start(bf16[2,128,128]{2,1,0:T(8,128)(2,1)S(1)} %get-tuple-element.27), channel_id=1, source_target_pairs={{0,6},{2,4},{4,2},{6,0},{8,14},{10,12},{12,10},{14,8},{1,7},{3,5},... | collective-permute-start | bytes 196616 | tf_op jit(solution)/shard_map/ppermute | solution.py:30
  6.5 5.0 %collective-permute-start.3 = (bf16[2,128,128]{2,1,0:T(8,128)(2,1)S(1)}, bf16[2,128,128]{2,1,0:T(8,128)(2,1)S(1)}, u32[]{:S(2)}, u32[]{:S(2)}) collective-permute-start(bf16[2,128,128]{2,1,0:T(8,128)(2,1)S(1)} %get-tuple-element.27), channel_id=1, source_target_pairs={{0,2},{2,0},{4,6},{6,4},{8,10},{10,8},{12,14},{14,12},{1,3},{3,1},... | collective-permute-start | bytes 196616 | tf_op jit(solution)/shard_map/ppermute | solution.py:30
  7.0 4.4 %collective-permute-start.4 = (bf16[2,128,128]{2,1,0:T(8,128)(2,1)S(1)}, bf16[2,128,128]{2,1,0:T(8,128)(2,1)S(1)}, u32[]{:S(2)}, u32[]{:S(2)}) collective-permute-start(bf16[2,128,128]{2,1,0:T(8,128)(2,1)S(1)} %get-tuple-element.26), channel_id=1, source_target_pairs={{0,4},{2,6},{4,0},{6,2},{8,12},{10,14},{12,8},{14,10},{1,5},{3,7},... | collective-permute-start | bytes 196616 | tf_op jit(solution)/shard_map/ppermute | solution.py:30
  7.9 12.4 %collective-permute-start = (bf16[4,128,128]{2,1,0:T(8,128)(2,1)S(1)}, bf16[4,128,128]{2,1,0:T(8,128)(2,1)S(1)}, u32[]{:S(2)}, u32[]{:S(2)}) collective-permute-start(bf16[4,128,128]{2,1,0:T(8,128)(2,1)S(1)} %first_level.1), channel_id=1, source_target_pairs={{0,2},{2,0},{4,6},{6,4},{8,10},{10,8},{12,14},{14,12},{1,3},{3,1},... | collective-permute-start | bytes 393224 | tf_op jit(solution)/shard_map/ppermute | solution.py:30
  9.9 5.7 %collective-permute-start.1 = (bf16[4,128,128]{2,1,0:T(8,128)(2,1)S(1)}, bf16[4,128,128]{2,1,0:T(8,128)(2,1)S(1)}, u32[]{:S(2)}, u32[]{:S(2)}) collective-permute-start(bf16[4,128,128]{2,1,0:T(8,128)(2,1)S(1)} %get-tuple-element.25), channel_id=1, source_target_pairs={{0,4},{2,6},{4,0},{6,2},{8,12},{10,14},{12,8},{14,10},{1,5},{3,7},... | collective-permute-start | bytes 393224 | tf_op jit(solution)/shard_map/ppermute | solution.py:30
  11.5 8.7 %collective-permute-start.7 = (bf16[2,128,128]{2,1,0:T(8,128)(2,1)S(1)}, bf16[2,128,128]{2,1,0:T(8,128)(2,1)S(1)}, u32[]{:S(2)}, u32[]{:S(2)}) collective-permute-start(bf16[2,128,128]{2,1,0:T(8,128)(2,1)S(1)} %add_convert_fusion), channel_id=1, source_target_pairs={{0,8},{2,10},{4,12},{6,14},{8,2},{10,0},{12,6},{14,4},{1,9},{3,11}... | collective-permute-start | bytes 196616 | tf_op jit(solution)/shard_map/ppermute | solution.py:38
  14.1 6.2 %collective-permute-start.6 = (bf16[2,128,128]{2,1,0:T(8,128)(2,1)S(1)}, bf16[2,128,128]{2,1,0:T(8,128)(2,1)S(1)}, u32[]{:S(2)}, u32[]{:S(2)}) collective-permute-start(bf16[2,128,128]{2,1,0:T(8,128)(2,1)S(1)} %add_convert_fusion), channel_id=1, source_target_pairs={{0,10},{2,8},{4,14},{6,12},{8,0},{10,2},{12,4},{14,6},{1,11},{3,9}... | collective-permute-start | bytes 196616 | tf_op jit(solution)/shard_map/ppermute | solution.py:38
  15.6 5.2 %collective-permute-start.2 = (bf16[4,128,128]{2,1,0:T(8,128)(2,1)S(1)}, bf16[4,128,128]{2,1,0:T(8,128)(2,1)S(1)}, u32[]{:S(2)}, u32[]{:S(2)}) collective-permute-start(bf16[4,128,128]{2,1,0:T(8,128)(2,1)S(1)} %collective-permute-done.1.refs_10_), channel_id=1, source_target_pairs={{0,2},{2,0},{4,6},{6,4},{8,10},{10,8},{12,14},{14,12},{1,3},{3,1},... | collective-permute-start | bytes 393224 | tf_op jit(solution)/shard_map/ppermute | solution.py:30

commit v7 on v6

--- a/solution.py
+++ b/solution.py
@@ -103,21 +103,15 @@
                 columns = slice(pair * GROUP * width, (pair + 1) * GROUP * width)
                 part = nn(jnp.concatenate(lefts, 0), right_buf[index, rows, columns])
                 totals[pair] = part if totals[pair] is None else totals[pair] + part
+        held = []
         for h in range(heads):
             block = slice(h % GROUP * width, h % GROUP * width + width)
             state = totals[h // GROUP][block, block]
-            if upper:
-                state = scales[level] * state
-            state = state.astype(LOW)
-            row = index * half + h % half
-
-            @pl.when(low_bit == h // half)
-            def _():
-                own_out[row] = state
-
-            @pl.when(low_bit != h // half)
-            def _():
-                other_out[row] = state
+            held.append((scales[level] * state if upper else state).astype(LOW))
+        for i in range(half):
+            low, high = held[i], held[half + i]
+            own_out[index * half + i] = jnp.where(low_bit == 0, low, high)
+            other_out[index * half + i] = jnp.where(low_bit == 0, high, low)
 
     for index in range(bits - 2):
         bit = (place >> (index + 2)) & 1
@@ -137,7 +131,7 @@
     return (jnp.where(upper, scale, 1.0) * nn(left, right)).astype(LOW)
 
 
-def second_kernel(bits, scale, q_ref, k_ref, v_ref, g_ref, w_ref, t_ref, qt_out, kt_out, d2_out):
+def low_kernel(bits, scales, q_ref, k_ref, v_ref, g_ref, w_ref, t_ref, qt_out, kt_out, d1_out, d2_out):
     heads, width = t_ref.shape[:2]
     place = block_index()
     top = ((place >> (bits - 1)) & 1) == 1
@@ -148,13 +142,10 @@
         key_t = jnp.where(top, other, turned)
         qt_out[h] = query_t
         kt_out[h] = key_t
-        d2_out[h] = mixed_state(2, scale, h, place, query_t, key_t, w_ref, v_ref, g_ref)
-
-
-def first_kernel(scale, v_ref, g_ref, w_ref, qt_ref, kt_ref, d1_out):
-    place = block_index()
-    for h in range(qt_ref.shape[0]):
-        d1_out[h] = mixed_state(1, scale, h, place, qt_ref[h], kt_ref[h], w_ref, v_ref, g_ref)
+        for level, out in ((1, d1_out), (2, d2_out)):
+            out[h] = mixed_state(
+                level, scales[level], h, place, query_t, key_t, w_ref, v_ref, g_ref
+            )
 
 
 def near_head(scale, h, q_ref, k_ref, v_ref, g_ref, w_ref, kt_ref, nk_out, nv_out, local):
@@ -203,6 +194,14 @@
         back, weight = near_head(scale, h, *ins, nk_out, nv_out, h)
         store_sums(sum_out, h, slice(None), back)
         store_sums(gw_out, h, pl.ds(0, 1), weight)
+
+
+def sum_kernel(*refs):
+    *parts, out = refs
+    total = parts[0][...].astype(jnp.float32)
+    for part in parts[1:]:
+        total = total + part[...].astype(jnp.float32)
+    out[...] = total.astype(LOW)
 
 
 def spread(blocks):
@@ -347,23 +346,19 @@
     got_x = flip(other, 1)
     got_z = flip(own, 2)
     got_d = flip(other, 3)
-    quad = as_f(own) + as_f(got_x) + as_f(got_z) + as_f(got_d)
-    qt, kt, d2 = call(
-        functools.partial(second_kernel, bits, scales[2]), "second_level", cost,
-        [turned, turned, full], [q_v, k_v, v_v, g_v, w_v, t_v],
-    )
-    got_2 = flip(d2, 2)
-    (d1,) = call(
-        functools.partial(first_kernel, scales[1]), "first_level", cost,
-        [full], [v_v, g_v, w_v, qt, kt],
+    (quad,) = call(sum_kernel, "quad_sum", cost, [halves], [own, got_x, got_z, got_d])
+    qt, kt, d1, d2 = call(
+        functools.partial(low_kernel, bits, scales), "low_states", cost,
+        [turned, turned, full, full], [q_v, k_v, v_v, g_v, w_v, t_v],
     )
     got_1 = flip(d1, 1)
+    got_2 = flip(d2, 2)
     sums = []
     for bit in range(2, bits):
-        sums.append(quad[:half].astype(LOW))
+        sums.append(quad[:half])
         quad = quad[half:]
         if bit < bits - 1:
-            quad = quad + as_f(flip(quad.astype(LOW), 1 << bit))
+            quad = (as_f(quad) + as_f(flip(quad, 1 << bit))).astype(LOW)
     early_half = [swap_halves(x, i + 2, True) for i, x in enumerate(sums)]
     late_half = [swap_halves(x, i + 2, False) for i, x in enumerate(sums)]
     diagonal_2 = flip(got_2, 1)

time: 22.4 us -> 22.4 us (level)
    ppermute x6, waiting for transfers between devices: 0.38 us -> 0.61 us  [flip(): return lax.ppermute(block, AXES, [(i, i ^ mask) for i in range(size)])]
where the time goes in v7:
time: 22.4 us; the launch traced here: 22.2 us
  starting transfers between devices  13.9 us (62%)
  Pallas kernels  6.54 us (29%)
  waiting for transfers between devices  1.06 us (5%)
  between operations  0.72 us (3%)
    ppermute x6, starting transfers between devices, flip(): return lax.ppermute(block, AXES, [(i, i ^ mask) for i in range(size)])  9.86 us
    ppermute x2, starting transfers between devices, swap_halves(): return lax.ppermute(block, AXES, routes)  4 us
    pallas_call x3, Pallas kernels, call(): pl.pallas_call(kernel, out_shape=outs, in_specs=[IN_VMEM] * len(operands)...  3.33 us
    pallas_call x1, Pallas kernels, on_device(): pl.pallas_call(functools.partial(top_kernel, bits, scales), out_shape=[pl...  1.73 us
    pallas_call x1, Pallas kernels, on_device(): pl.pallas_call(functools.partial(far_kernel, bits, scales), out_shape=(ou...  1.48 us
    ppermute x6, waiting for transfers between devices, flip(): return lax.ppermute(block, AXES, [(i, i ^ mask) for i in range(size)])  0.61 us
    ppermute x2, waiting for transfers between devices, swap_halves(): return lax.ppermute(block, AXES, routes)  0.45 us
  transfers between devices with their start and end apart: 8, of which 3 were waited for; matrix products, arithmetic and copies ran while one was open for 0% of the time, Pallas kernels for 15%

profile of v7, /device:TPU:0, one launch (start us, length us, event | category | flops | bytes accessed | tf_op | source)
XLA Modules:
  0.0 22.2 jit_solution(9440965448460837479)
XLA Ops:
  0.6 0.0 copy-start.4
  0.6 0.0 copy-start.3
  0.7 0.0 copy-start.2
  0.7 0.0 copy-start.1
  0.7 0.0 copy-start
  0.7 1.7 %top_states.1 = (bf16[4,128,512]{2,1,0:T(8,128)(2,1)S(1)}, bf16[2,128,128]{2,1,0:T(8,128)(2,1)S(1)}, bf16[2,128,128]{2,1,0:T(8,128)(2,1)S(1)}) custom-call(bf16[512,512]{1,0:T(8,128)(2,1)} %refs_0_.2, bf16[512,512]{1,0:T(8,128)(2,1)} %refs_0_.3, bf16[512,512]{1,0:T(8,128)(2,1)} %refs_1_.3, bf16[512,512]{1,0:T(8,128)(2,1)} %refs_2_.3, f32[4,8,512]{2,1,0:T(8,128)} %refs_3_.3), custom_call_target="tpu_custom_call" | custom-call | flops 33554432000 | tf_op jit(solution)/shard_map/top_states/pallas_call | solution.py:328
  2.4 4.0 %collective-permute-start.5 = (bf16[2,128,128]{2,1,0:T(8,128)(2,1)S(1)}, bf16[2,128,128]{2,1,0:T(8,128)(2,1)S(1)}, u32[]{:S(2)}, u32[]{:S(2)}) collective-permute-start(bf16[2,128,128]{2,1,0:T(8,128)(2,1)S(1)} %get-tuple-element.29), channel_id=1, source_target_pairs={{0,6},{2,4},{4,2},{6,0},{8,14},{10,12},{12,10},{14,8},{1,7},{3,5},... | collective-permute-start | bytes 196616 | tf_op jit(solution)/shard_map/ppermute | solution.py:30
  6.4 0.5 %collective-permute-start.3 = (bf16[2,128,128]{2,1,0:T(8,128)(2,1)S(1)}, bf16[2,128,128]{2,1,0:T(8,128)(2,1)S(1)}, u32[]{:S(2)}, u32[]{:S(2)}) collective-permute-start(bf16[2,128,128]{2,1,0:T(8,128)(2,1)S(1)} %get-tuple-element.29), channel_id=1, source_target_pairs={{0,2},{2,0},{4,6},{6,4},{8,10},{10,8},{12,14},{14,12},{1,3},{3,1},... | collective-permute-start | bytes 196616 | tf_op jit(solution)/shard_map/ppermute | solution.py:30
  7.0 0.1 collective-permute-start.4
  7.1 0.0 copy-done.4
  7.1 0.0 copy-done.3
  7.1 0.0 copy-done.2
  7.1 0.0 copy-done.1
  7.1 0.0 copy-done
  7.1 0.7 %low_states.1 = (bf16[4,128,512]{2,1,0:T(8,128)(2,1)S(1)}, bf16[4,128,512]{2,1,0:T(8,128)(2,1)S(1)}, bf16[4,128,128]{2,1,0:T(8,128)(2,1)S(1)}, bf16[4,128,128]{2,1,0:T(8,128)(2,1)S(1)}) custom-call(bf16[512,512]{1,0:T(8,128)(2,1)S(1)} %copy-done, bf16[512,512]{1,0:T(8,128)(2,1)S(1)} %copy-done.1, bf16[512,512]{1,0:T(8,128)(2,1)S(1)} %copy-done.2, ...), custom_call_target="tpu_custom_call" | custom-call | flops 33554432000 | tf_op jit(solution)/shard_map/low_states/pallas_call | solution.py:302
  7.8 1.9 %collective-permute-start = (bf16[4,128,128]{2,1,0:T(8,128)(2,1)S(1)}, bf16[4,128,128]{2,1,0:T(8,128)(2,1)S(1)}, u32[]{:S(2)}, u32[]{:S(2)}) collective-permute-start(bf16[4,128,128]{2,1,0:T(8,128)(2,1)S(1)} %get-tuple-element.26), channel_id=1, source_target_pairs={{0,2},{2,0},{4,6},{6,4},{8,10},{10,8},{12,14},{14,12},{1,3},{3,1},... | collective-permute-start | bytes 393224 | tf_op jit(solution)/shard_map/ppermute | solution.py:30
  9.7 1.6 %collective-permute-start.1 = (bf16[4,128,128]{2,1,0:T(8,128)(2,1)S(1)}, bf16[4,128,128]{2,1,0:T(8,128)(2,1)S(1)}, u32[]{:S(2)}, u32[]{:S(2)}) collective-permute-start(bf16[4,128,128]{2,1,0:T(8,128)(2,1)S(1)} %get-tuple-element.27), channel_id=1, source_target_pairs={{0,4},{2,6},{4,0},{6,2},{8,12},{10,14},{12,8},{14,10},{1,5},{3,7},... | collective-permute-start | bytes 393224 | tf_op jit(solution)/shard_map/ppermute | solution.py:30
  11.3 0.2 collective-permute-done.4.refs_2_
  11.5 0.0 collective-permute-done.5.refs_3_
  11.5 0.0 collective-permute-done.3.refs_1_
  11.6 2.7 %collective-permute-start.7 = (bf16[2,128,128]{2,1,0:T(8,128)(2,1)S(1)}, bf16[2,128,128]{2,1,0:T(8,128)(2,1)S(1)}, u32[]{:S(2)}, u32[]{:S(2)}) collective-permute-start(bf16[2,128,128]{2,1,0:T(8,128)(2,1)S(1)} %quad_sum.1), channel_id=1, source_target_pairs={{0,8},{2,10},{4,12},{6,14},{8,2},{10,0},{12,6},{14,4},{1,9},{3,11}... | collective-permute-start | bytes 196616 | tf_op jit(solution)/shard_map/ppermute | solution.py:38
  14.2 1.3 %collective-permute-start.6 = (bf16[2,128,128]{2,1,0:T(8,128)(2,1)S(1)}, bf16[2,128,128]{2,1,0:T(8,128)(2,1)S(1)}, u32[]{:S(2)}, u32[]{:S(2)}) collective-permute-start(bf16[2,128,128]{2,1,0:T(8,128)(2,1)S(1)} %quad_sum.1), channel_id=1, source_target_pairs={{0,10},{2,8},{4,14},{6,12},{8,0},{10,2},{12,4},{14,6},{1,11},{3,9}... | collective-permute-start | bytes 196616 | tf_op jit(solution)/shard_map/ppermute | solution.py:38
  15.6 0.0 collective-permute-done.1.refs_10_
  15.6 1.7 %collective-permute-start.2 = (bf16[4,128,128]{2,1,0:T(8,128)(2,1)S(1)}, bf16[4,128,128]{2,1,0:T(8,128)(2,1)S(1)}, u32[]{:S(2)}, u32[]{:S(2)}) collective-permute-start(bf16[4,128,128]{2,1,0:T(8,128)(2,1)S(1)} %collective-permute-done.1.refs_10_), channel_id=1, source_target_pairs={{0,2},{2,0},{4,6},{6,4},{8,10},{10,8},{12,14},{14,12},{1,3},{3,1},... | collective-permute-start | bytes 393224 | tf_op jit(solution)/shard_map/ppermute | solution.py:30
  17.3 2.6 %near.1 = (f32[4,128,512]{2,1,0:T(8,128)S(1)}, f32[4,8,512]{2,1,0:T(8,128)S(1)}, f32[4,512,128]{2,1,0:T(8,128)S(1)}, f32[4,512,128]{2,1,0:T(8,128)S(1)}) custom-call(bf16[512,512]{1,0:T(8,128)(2,1)S(1)} %copy-done, bf16[512,512]{1,0:T(8,128)(2,1)S(1)} %copy-done.1, bf16[512,512]{1,0:T(8,128)(2,1)S(1)} %copy-done.2, bf16[512,512]{1,0:T(8,128)(2,1)S(1)} %copy-done.3, ...), custom_call_target="tpu_custom_call" | custom-call | flops 33554432000 | tf_op jit(solution)/shard_map/near/pallas_call | solution.py:302
  19.8 0.0 collective-permute-done.7.refs_13_
  19.9 0.4 %collective-permute-done.6.refs_12_ = bf16[2,128,128]{2,1,0:T(8,128)(2,1)S(1)} collective-permute-done((bf16[2,128,128]{2,1,0:T(8,128)(2,1)S(1)}, bf16[2,128,128]{2,1,0:T(8,128)(2,1)S(1)}, u32[]{:S(2)}, u32[]{:S(2)}) %collective-permute-start.6) | collective-permute-done | bytes 65568 | tf_op jit(solution)/shard_map/ppermute | solution.py:38
  20.3 0.0 collective-permute-done.refs_9_
  20.3 0.4 %collective-permute-done.2.refs_11_ = bf16[4,128,128]{2,1,0:T(8,128)(2,1)S(1)} collective-permute-done((bf16[4,128,128]{2,1,0:T(8,128)(2,1)S(1)}, bf16[4,128,128]{2,1,0:T(8,128)(2,1)S(1)}, u32[]{:S(2)}, u32[]{:S(2)}) %collective-permute-start.2) | collective-permute-done | bytes 131104 | tf_op jit(solution)/shard_map/ppermute | solution.py:30
  20.7 1.5 %far.1 = (bf16[512,512]{1,0:T(8,128)(2,1)}, bf16[512,512]{1,0:T(8,128)(2,1)}, bf16[512,512]{1,0:T(8,128)(2,1)}, f32[4,8,512]{2,1,0:T(8,128)}, f32[4,128,512]{2,1,0:T(8,128)S(1)}) custom-call(bf16[512,512]{1,0:T(8,128)(2,1)S(1)} %copy-done.1, bf16[512,512]{1,0:T(8,128)(2,1)S(1)} %copy-done.2, ...), custom_call_target="tpu_custom_call", output_to_operand_aliasing={{4}: (5, {})} | custom-call | flops 33554432000 | tf_op jit(solution)/shard_map/far/pallas_call | solution.py:373
  (1 shorter events, 0.0 us)
Async XLA Ops:
  0.6 6.5 %copy-start.4 = (f32[4,8,512]{2,1,0:T(8,128)S(1)}, f32[4,8,512]{2,1,0:T(8,128)}, u32[]{:S(2)}) copy-start(f32[4,8,512]{2,1,0:T(8,128)} %refs_3_.3) | copy-start | bytes 196612
  0.6 6.4 %copy-start.3 = (bf16[512,512]{1,0:T(8,128)(2,1)S(1)}, bf16[512,512]{1,0:T(8,128)(2,1)}, u32[]{:S(2)}) copy-start(bf16[512,512]{1,0:T(8,128)(2,1)} %refs_2_.3) | copy-start | bytes 1572868
  0.7 6.4 %copy-start.2 = (bf16[512,512]{1,0:T(8,128)(2,1)S(1)}, bf16[512,512]{1,0:T(8,128)(2,1)}, u32[]{:S(2)}) copy-start(bf16[512,512]{1,0:T(8,128)(2,1)} %refs_1_.3) | copy-start | bytes 1572868
  0.7 6.4 %copy-start.1 = (bf16[512,512]{1,0:T(8,128)(2,1)S(1)}, bf16[512,512]{1,0:T(8,128)(2,1)}, u32[]{:S(2)}) copy-start(bf16[512,512]{1,0:T(8,128)(2,1)} %refs_0_.3) | copy-start | bytes 1572868
  0.7 6.4 %copy-start = (bf16[512,512]{1,0:T(8,128)(2,1)S(1)}, bf16[512,512]{1,0:T(8,128)(2,1)}, u32[]{:S(2)}) copy-start(bf16[512,512]{1,0:T(8,128)(2,1)} %refs_0_.2) | copy-start | bytes 1572868
  2.4 9.1 %collective-permute-start.5 = (bf16[2,128,128]{2,1,0:T(8,128)(2,1)S(1)}, bf16[2,128,128]{2,1,0:T(8,128)(2,1)S(1)}, u32[]{:S(2)}, u32[]{:S(2)}) collective-permute-start(bf16[2,128,128]{2,1,0:T(8,128)(2,1)S(1)} %get-tuple-element.29), channel_id=1, source_target_pairs={{0,6},{2,4},{4,2},{6,0},{8,14},{10,12},{12,10},{14,8},{1,7},{3,5},... | collective-permute-start | bytes 196616 | tf_op jit(solution)/shard_map/ppermute | solution.py:30
  6.4 5.1 %collective-permute-start.3 = (bf16[2,128,128]{2,1,0:T(8,128)(2,1)S(1)}, bf16[2,128,128]{2,1,0:T(8,128)(2,1)S(1)}, u32[]{:S(2)}, u32[]{:S(2)}) collective-permute-start(bf16[2,128,128]{2,1,0:T(8,128)(2,1)S(1)} %get-tuple-element.29), channel_id=1, source_target_pairs={{0,2},{2,0},{4,6},{6,4},{8,10},{10,8},{12,14},{14,12},{1,3},{3,1},... | collective-permute-start | bytes 196616 | tf_op jit(solution)/shard_map/ppermute | solution.py:30
  7.0 4.5 %collective-permute-start.4 = (bf16[2,128,128]{2,1,0:T(8,128)(2,1)S(1)}, bf16[2,128,128]{2,1,0:T(8,128)(2,1)S(1)}, u32[]{:S(2)}, u32[]{:S(2)}) collective-permute-start(bf16[2,128,128]{2,1,0:T(8,128)(2,1)S(1)} %get-tuple-element.28.refs_0_), channel_id=1, source_target_pairs={{0,4},{2,6},{4,0},{6,2},{8,12},{10,14},{12,8},{14,10},{1,5},{3,7},... | collective-permute-start | bytes 196616 | tf_op jit(solution)/shard_map/ppermute | solution.py:30
  7.8 12.5 %collective-permute-start = (bf16[4,128,128]{2,1,0:T(8,128)(2,1)S(1)}, bf16[4,128,128]{2,1,0:T(8,128)(2,1)S(1)}, u32[]{:S(2)}, u32[]{:S(2)}) collective-permute-start(bf16[4,128,128]{2,1,0:T(8,128)(2,1)S(1)} %get-tuple-element.26), channel_id=1, source_target_pairs={{0,2},{2,0},{4,6},{6,4},{8,10},{10,8},{12,14},{14,12},{1,3},{3,1},... | collective-permute-start | bytes 393224 | tf_op jit(solution)/shard_map/ppermute | solution.py:30
  9.7 5.8 %collective-permute-start.1 = (bf16[4,128,128]{2,1,0:T(8,128)(2,1)S(1)}, bf16[4,128,128]{2,1,0:T(8,128)(2,1)S(1)}, u32[]{:S(2)}, u32[]{:S(2)}) collective-permute-start(bf16[4,128,128]{2,1,0:T(8,128)(2,1)S(1)} %get-tuple-element.27), channel_id=1, source_target_pairs={{0,4},{2,6},{4,0},{6,2},{8,12},{10,14},{12,8},{14,10},{1,5},{3,7},... | collective-permute-start | bytes 393224 | tf_op jit(solution)/shard_map/ppermute | solution.py:30
  11.6 8.3 %collective-permute-start.7 = (bf16[2,128,128]{2,1,0:T(8,128)(2,1)S(1)}, bf16[2,128,128]{2,1,0:T(8,128)(2,1)S(1)}, u32[]{:S(2)}, u32[]{:S(2)}) collective-permute-start(bf16[2,128,128]{2,1,0:T(8,128)(2,1)S(1)} %quad_sum.1), channel_id=1, source_target_pairs={{0,8},{2,10},{4,12},{6,14},{8,2},{10,0},{12,6},{14,4},{1,9},{3,11}... | collective-permute-start | bytes 196616 | tf_op jit(solution)/shard_map/ppermute | solution.py:38
  14.2 6.1 %collective-permute-start.6 = (bf16[2,128,128]{2,1,0:T(8,128)(2,1)S(1)}, bf16[2,128,128]{2,1,0:T(8,128)(2,1)S(1)}, u32[]{:S(2)}, u32[]{:S(2)}) collective-permute-start(bf16[2,128,128]{2,1,0:T(8,128)(2,1)S(1)} %quad_sum.1), channel_id=1, source_target_pairs={{0,10},{2,8},{4,14},{6,12},{8,0},{10,2},{12,4},{14,6},{1,11},{3,9}... | collective-permute-start | bytes 196616 | tf_op jit(solution)/shard_map/ppermute | solution.py:38
  15.6 5.2 %collective-permute-start.2 = (bf16[4,128,128]{2,1,0:T(8,128)(2,1)S(1)}, bf16[4,128,128]{2,1,0:T(8,128)(2,1)S(1)}, u32[]{:S(2)}, u32[]{:S(2)}) collective-permute-start(bf16[4,128,128]{2,1,0:T(8,128)(2,1)S(1)} %collective-permute-done.1.refs_10_), channel_id=1, source_target_pairs={{0,2},{2,0},{4,6},{6,4},{8,10},{10,8},{12,14},{14,12},{1,3},{3,1},... | collective-permute-start | bytes 393224 | tf_op jit(solution)/shard_map/ppermute | solution.py:30

commit v8 on v7

--- a/solution.py
+++ b/solution.py
@@ -12,7 +12,6 @@
 LOW = jnp.bfloat16
 ROWS = 256
 GROUP = 2
-CHUNKS = 1
 
 
 def nt(left, right):
@@ -60,54 +59,39 @@
 ):
     heads, width, tokens = t_out.shape
     half = heads // 2
-    span = tokens // CHUNKS
     place = block_index()
     low_bit = place & 1
 
-    def copies(index, upper):
-        left, right = (q_hbm, g_hbm) if upper else (k_hbm, v_hbm)
-        made = []
-        for chunk in range(CHUNKS):
-            rows = pl.ds(chunk * span, span)
-            made.append(
-                [
-                    pltpu.make_async_copy(left.at[rows], left_buf.at[index, rows], sems.at[0, index, chunk]),
-                    pltpu.make_async_copy(right.at[rows], right_buf.at[index, rows], sems.at[1, index, chunk]),
-                ]
-            )
-        if upper:
-            level_row = w_hbm.at[:, pl.ds(index + 3, 1), :]
-            made[0].append(pltpu.make_async_copy(level_row, w_buf.at[index], sems.at[2, index, 0]))
-        return made
-
     def states(index, upper):
         level = index + 3
-        made = copies(index, upper)
-        for group in made:
-            for copy in group:
-                copy.start()
-        totals = [None] * (heads // GROUP)
-        for chunk, group in enumerate(made):
-            for copy in group:
-                copy.wait()
-            rows = slice(chunk * span, chunk * span + span)
-            for pair in range(heads // GROUP):
-                lefts = []
-                for h in range(pair * GROUP, pair * GROUP + GROUP):
-                    turned = left_buf[index, rows, h * width : (h + 1) * width].T
-                    if level == bits:
-                        t_out[h, :, rows] = turned
-                    if upper:
-                        turned = (w_buf[index, h, :, rows] * turned.astype(jnp.float32)).astype(LOW)
-                    lefts.append(turned)
-                columns = slice(pair * GROUP * width, (pair + 1) * GROUP * width)
-                part = nn(jnp.concatenate(lefts, 0), right_buf[index, rows, columns])
-                totals[pair] = part if totals[pair] is None else totals[pair] + part
+        left, right = (q_hbm, g_hbm) if upper else (k_hbm, v_hbm)
+        copies = [
+            pltpu.make_async_copy(left, left_buf.at[index], sems.at[0, index]),
+            pltpu.make_async_copy(right, right_buf.at[index], sems.at[1, index]),
+        ]
+        if upper:
+            level_row = w_hbm.at[:, pl.ds(level, 1), :]
+            copies.append(pltpu.make_async_copy(level_row, w_buf.at[index], sems.at[2, index]))
+        for copy in copies:
+            copy.start()
+        for copy in copies:
+            copy.wait()
         held = []
-        for h in range(heads):
-            block = slice(h % GROUP * width, h % GROUP * width + width)
-            state = totals[h // GROUP][block, block]
-            held.append((scales[level] * state if upper else state).astype(LOW))
+        for first in range(0, heads, GROUP):
+            lefts = []
+            for h in range(first, first + GROUP):
+                turned = head(left_buf.at[index], h, width).T
+                if level == bits:
+                    t_out[h] = turned
+                if upper:
+                    turned = (w_buf[index, h] * turned.astype(jnp.float32)).astype(LOW)
+                lefts.append(turned)
+            columns = slice(first * width, (first + GROUP) * width)
+            product = nn(jnp.concatenate(lefts, 0), right_buf[index, :, columns])
+            for i in range(GROUP):
+                block = slice(i * width, i * width + width)
+                state = product[block, block]
+                held.append((scales[level] * state if upper else state).astype(LOW))
         for i in range(half):
             low, high = held[i], held[half + i]
             own_out[index * half + i] = jnp.where(low_bit == 0, low, high)
@@ -148,7 +132,7 @@
             )
 
 
-def near_head(scale, h, q_ref, k_ref, v_ref, g_ref, w_ref, kt_ref, nk_out, nv_out, local):
+def near_head(scale, h, q_ref, k_ref, v_ref, g_ref, w_ref, kt_ref, nk_out, nv_out):
     width, tokens = kt_ref.shape[1:]
     rows = min(ROWS, tokens)
     factor = scale * w_ref[h, pl.ds(0, 1), :]
@@ -170,8 +154,8 @@
         now = factor[:, start:]
         grad_mix = (now * dots).astype(LOW)
         score_mix = (now * scores).astype(LOW)
-        nk_out[local, start : start + rows, :] = nn(grad_mix, query)
-        nv_out[local, start : start + rows, :] = nn(score_mix, grad)
+        nk_out[h, start : start + rows, :] = nn(grad_mix, query)
+        nv_out[h, start : start + rows, :] = nn(score_mix, grad)
         back.append(nn(kt_ref[h, :, start : start + rows], grad_mix))
         weight.append(scale * part)
     return back, weight
@@ -191,9 +175,13 @@
     ins, (sum_out, gw_out, nk_out, nv_out) = refs[:6], refs[6:]
     for h in range(sum_out.shape[0]):
         gw_out[h] = jnp.zeros(gw_out.shape[1:], jnp.float32)
-        back, weight = near_head(scale, h, *ins, nk_out, nv_out, h)
+        back, weight = near_head(scale, h, *ins, nk_out, nv_out)
         store_sums(sum_out, h, slice(None), back)
         store_sums(gw_out, h, pl.ds(0, 1), weight)
+
+
+def copy_kernel(source, out):
+    out[...] = source[...]
 
 
 def sum_kernel(*refs):
@@ -332,24 +320,24 @@
         out_specs=[IN_VMEM] * len(outs),
         scratch_shapes=[
             chosen, chosen, pltpu.VMEM((bits - 2, heads, 1, tokens), f32),
-            pltpu.SemaphoreType.DMA((3, bits - 2, CHUNKS)),
+            pltpu.SemaphoreType.DMA((3, bits - 2)),
         ],
         compiler_params=pltpu.CompilerParams(vmem_limit_bytes=LIMIT),
         cost_estimate=pl.CostEstimate(flops=cost, bytes_accessed=0, transcendentals=0),
         name="top_states",
     )(*[in_hbm(x) for x in (queries, keys, values, out_grad, level_weights)])
-    q_v, k_v, v_v, g_v, w_v = queries, keys, values, out_grad, level_weights
 
     def as_f(array):
         return array.astype(f32)
 
-    got_x = flip(other, 1)
     got_z = flip(own, 2)
     got_d = flip(other, 3)
+    (other_x,) = call(copy_kernel, "x_part", cost, [halves], [other])
+    got_x = flip(other_x, 1)
     (quad,) = call(sum_kernel, "quad_sum", cost, [halves], [own, got_x, got_z, got_d])
     qt, kt, d1, d2 = call(
         functools.partial(low_kernel, bits, scales), "low_states", cost,
-        [turned, turned, full, full], [q_v, k_v, v_v, g_v, w_v, t_v],
+        [turned, turned, full, full], [queries, keys, values, out_grad, level_weights, t_v],
     )
     got_1 = flip(d1, 1)
     got_2 = flip(d2, 2)
@@ -365,14 +353,17 @@
     total, weights, near_k, near_v = call(
         functools.partial(near_kernel, scales[0]), "near", cost,
         [((heads, width, tokens), f32), weight_rows, *[((heads, tokens, width), f32)] * 2],
-        [q_v, k_v, v_v, g_v, w_v, kt],
-    )
-    operands = [k_v, v_v, g_v, w_v, qt, total, weights, near_k, near_v]
+        [queries, keys, values, out_grad, level_weights, kt],
+    )
+    operands = [keys, values, out_grad, level_weights, qt, total, weights, near_k, near_v]
     operands += [got_1, got_2, diagonal_2, *late_half, *early_half]
     out = jax.ShapeDtypeStruct((tokens, heads * width), LOW)
     return pl.pallas_call(
         functools.partial(far_kernel, bits, scales),
-        out_shape=(out, out, out, jax.ShapeDtypeStruct((heads, levels, tokens), f32), pltpu.VMEM((heads, width, tokens), f32)),
+        out_shape=(
+            out, out, out, jax.ShapeDtypeStruct((heads, levels, tokens), f32),
+            pltpu.VMEM((heads, width, tokens), f32),
+        ),
         in_specs=[IN_VMEM] * len(operands),
         out_specs=(ANY,) * 4 + (IN_VMEM,),
         input_output_aliases={5: 4},

time: 22.4 us -> 22.2 us (level)
    pallas_call x3 -> x4, Pallas kernels: 3.33 us -> 3.33 us  [call(): pl.pallas_call(kernel, out_shape=outs, in_specs=[IN_VMEM] * len(operands)...]
  transfers between devices with their start and end apart: 8 -> 8, of which waited for: 3 -> 4; matrix products, arithmetic and copies ran while one was open for 0% -> 0% of each run, Pallas kernels for 15% -> 15%
where the time goes in v8:
time: 22.2 us; the launch traced here: 22.1 us
  starting transfers between devices  13.9 us (63%)
  Pallas kernels  6.41 us (29%)
  waiting for transfers between devices  1.06 us (5%)
  between operations  0.72 us (3%)
    ppermute x6, starting transfers between devices, flip(): return lax.ppermute(block, AXES, [(i, i ^ mask) for i in range(size)])  9.85 us
    ppermute x2, starting transfers between devices, swap_halves(): return lax.ppermute(block, AXES, routes)  4.01 us
    pallas_call x4, Pallas kernels, call(): pl.pallas_call(kernel, out_shape=outs, in_specs=[IN_VMEM] * len(operands)...  3.33 us
    pallas_call x1, Pallas kernels, on_device(): pl.pallas_call(functools.partial(top_kernel, bits, scales), out_shape=[pl...  1.59 us
    pallas_call x1, Pallas kernels, on_device(): pl.pallas_call(functools.partial(far_kernel, bits, scales), out_shape=(ou...  1.49 us
    ppermute x6, waiting for transfers between devices, flip(): return lax.ppermute(block, AXES, [(i, i ^ mask) for i in range(size)])  0.6 us
    ppermute x2, waiting for transfers between devices, swap_halves(): return lax.ppermute(block, AXES, routes)  0.45 us
  transfers between devices with their start and end apart: 8, of which 4 were waited for; matrix products, arithmetic and copies ran while one was open for 0% of the time, Pallas kernels for 15%

profile of v8, /device:TPU:0, one launch (start us, length us, event | category | flops | bytes accessed | tf_op | source)
XLA Modules:
  0.0 22.1 jit_solution(5480624349825953372)
XLA Ops:
  0.6 1.6 %top_states.1 = (bf16[4,128,512]{2,1,0:T(8,128)(2,1)S(1)}, bf16[2,128,128]{2,1,0:T(8,128)(2,1)S(1)}, bf16[2,128,128]{2,1,0:T(8,128)(2,1)S(1)}) custom-call(bf16[512,512]{1,0:T(8,128)(2,1)} %refs_0_.2, bf16[512,512]{1,0:T(8,128)(2,1)} %refs_0_.3, bf16[512,512]{1,0:T(8,128)(2,1)} %refs_1_.3, bf16[512,512]{1,0:T(8,128)(2,1)} %refs_2_.3, f32[4,8,512]{2,1,0:T(8,128)} %refs_3_.3), custom_call_target="tpu_custom_call" | custom-call | flops 33554432000 | tf_op jit(solution)/shard_map/top_states/pallas_call | solution.py:316
  2.2 0.0 copy-start
  2.2 0.0 copy-start.1
  2.3 0.0 copy-start.2
  2.3 0.0 copy-start.3
  2.3 0.0 copy-start.4
  2.3 4.0 %collective-permute-start.5 = (bf16[2,128,128]{2,1,0:T(8,128)(2,1)S(1)}, bf16[2,128,128]{2,1,0:T(8,128)(2,1)S(1)}, u32[]{:S(2)}, u32[]{:S(2)}) collective-permute-start(bf16[2,128,128]{2,1,0:T(8,128)(2,1)S(1)} %get-tuple-element.29.source), channel_id=1, source_target_pairs={{0,6},{2,4},{4,2},{6,0},{8,14},{10,12},{12,10},{14,8},{1,7},{3,5},... | collective-permute-start | bytes 196616 | tf_op jit(solution)/shard_map/ppermute | solution.py:29
  6.3 0.5 %collective-permute-start.3 = (bf16[2,128,128]{2,1,0:T(8,128)(2,1)S(1)}, bf16[2,128,128]{2,1,0:T(8,128)(2,1)S(1)}, u32[]{:S(2)}, u32[]{:S(2)}) collective-permute-start(bf16[2,128,128]{2,1,0:T(8,128)(2,1)S(1)} %x_part.1), channel_id=1, source_target_pairs={{0,2},{2,0},{4,6},{6,4},{8,10},{10,8},{12,14},{14,12},{1,3},{3,1},... | collective-permute-start | bytes 196616 | tf_op jit(solution)/shard_map/ppermute | solution.py:29
  6.9 0.1 collective-permute-start.4
  7.0 0.0 copy-done
  7.0 0.0 copy-done.1
  7.0 0.0 copy-done.2
  7.0 0.0 copy-done.3
  7.0 0.0 copy-done.4
  7.0 0.7 %low_states.1 = (bf16[4,128,512]{2,1,0:T(8,128)(2,1)S(1)}, bf16[4,128,512]{2,1,0:T(8,128)(2,1)S(1)}, bf16[4,128,128]{2,1,0:T(8,128)(2,1)S(1)}, bf16[4,128,128]{2,1,0:T(8,128)(2,1)S(1)}) custom-call(bf16[512,512]{1,0:T(8,128)(2,1)S(1)} %copy-done, bf16[512,512]{1,0:T(8,128)(2,1)S(1)} %copy-done.1, bf16[512,512]{1,0:T(8,128)(2,1)S(1)} %copy-done.2, ...), custom_call_target="tpu_custom_call" | custom-call | flops 33554432000 | tf_op jit(solution)/shard_map/low_states/pallas_call | solution.py:290
  7.7 1.9 %collective-permute-start = (bf16[4,128,128]{2,1,0:T(8,128)(2,1)S(1)}, bf16[4,128,128]{2,1,0:T(8,128)(2,1)S(1)}, u32[]{:S(2)}, u32[]{:S(2)}) collective-permute-start(bf16[4,128,128]{2,1,0:T(8,128)(2,1)S(1)} %get-tuple-element.26), channel_id=1, source_target_pairs={{0,2},{2,0},{4,6},{6,4},{8,10},{10,8},{12,14},{14,12},{1,3},{3,1},... | collective-permute-start | bytes 393224 | tf_op jit(solution)/shard_map/ppermute | solution.py:29
  9.6 1.6 %collective-permute-start.1 = (bf16[4,128,128]{2,1,0:T(8,128)(2,1)S(1)}, bf16[4,128,128]{2,1,0:T(8,128)(2,1)S(1)}, u32[]{:S(2)}, u32[]{:S(2)}) collective-permute-start(bf16[4,128,128]{2,1,0:T(8,128)(2,1)S(1)} %get-tuple-element.27), channel_id=1, source_target_pairs={{0,4},{2,6},{4,0},{6,2},{8,12},{10,14},{12,8},{14,10},{1,5},{3,7},... | collective-permute-start | bytes 393224 | tf_op jit(solution)/shard_map/ppermute | solution.py:29
  11.2 0.1 collective-permute-done.3.refs_1_
  11.3 0.1 collective-permute-done.4.refs_2_
  11.4 0.0 collective-permute-done.5.refs_3_
  11.4 2.7 %collective-permute-start.7 = (bf16[2,128,128]{2,1,0:T(8,128)(2,1)S(1)}, bf16[2,128,128]{2,1,0:T(8,128)(2,1)S(1)}, u32[]{:S(2)}, u32[]{:S(2)}) collective-permute-start(bf16[2,128,128]{2,1,0:T(8,128)(2,1)S(1)} %quad_sum.1), channel_id=1, source_target_pairs={{0,8},{2,10},{4,12},{6,14},{8,2},{10,0},{12,6},{14,4},{1,9},{3,11}... | collective-permute-start | bytes 196616 | tf_op jit(solution)/shard_map/ppermute | solution.py:37
  14.1 1.4 %collective-permute-start.6 = (bf16[2,128,128]{2,1,0:T(8,128)(2,1)S(1)}, bf16[2,128,128]{2,1,0:T(8,128)(2,1)S(1)}, u32[]{:S(2)}, u32[]{:S(2)}) collective-permute-start(bf16[2,128,128]{2,1,0:T(8,128)(2,1)S(1)} %quad_sum.1), channel_id=1, source_target_pairs={{0,10},{2,8},{4,14},{6,12},{8,0},{10,2},{12,4},{14,6},{1,11},{3,9}... | collective-permute-start | bytes 196616 | tf_op jit(solution)/shard_map/ppermute | solution.py:37
  15.4 0.0 collective-permute-done.1.refs_10_
  15.4 1.7 %collective-permute-start.2 = (bf16[4,128,128]{2,1,0:T(8,128)(2,1)S(1)}, bf16[4,128,128]{2,1,0:T(8,128)(2,1)S(1)}, u32[]{:S(2)}, u32[]{:S(2)}) collective-permute-start(bf16[4,128,128]{2,1,0:T(8,128)(2,1)S(1)} %collective-permute-done.1.refs_10_), channel_id=1, source_target_pairs={{0,2},{2,0},{4,6},{6,4},{8,10},{10,8},{12,14},{14,12},{1,3},{3,1},... | collective-permute-start | bytes 393224 | tf_op jit(solution)/shard_map/ppermute | solution.py:29
  17.2 2.6 %near.1 = (f32[4,128,512]{2,1,0:T(8,128)S(1)}, f32[4,8,512]{2,1,0:T(8,128)S(1)}, f32[4,512,128]{2,1,0:T(8,128)S(1)}, f32[4,512,128]{2,1,0:T(8,128)S(1)}) custom-call(bf16[512,512]{1,0:T(8,128)(2,1)S(1)} %copy-done, bf16[512,512]{1,0:T(8,128)(2,1)S(1)} %copy-done.1, bf16[512,512]{1,0:T(8,128)(2,1)S(1)} %copy-done.2, bf16[512,512]{1,0:T(8,128)(2,1)S(1)} %copy-done.3, ...), custom_call_target="tpu_custom_call" | custom-call | flops 33554432000 | tf_op jit(solution)/shard_map/near/pallas_call | solution.py:290
  19.7 0.0 collective-permute-done.7.refs_13_
  19.7 0.4 %collective-permute-done.6.refs_12_ = bf16[2,128,128]{2,1,0:T(8,128)(2,1)S(1)} collective-permute-done((bf16[2,128,128]{2,1,0:T(8,128)(2,1)S(1)}, bf16[2,128,128]{2,1,0:T(8,128)(2,1)S(1)}, u32[]{:S(2)}, u32[]{:S(2)}) %collective-permute-start.6) | collective-permute-done | bytes 65568 | tf_op jit(solution)/shard_map/ppermute | solution.py:37
  20.2 0.0 collective-permute-done.refs_9_
  20.2 0.4 %collective-permute-done.2.refs_11_ = bf16[4,128,128]{2,1,0:T(8,128)(2,1)S(1)} collective-permute-done((bf16[4,128,128]{2,1,0:T(8,128)(2,1)S(1)}, bf16[4,128,128]{2,1,0:T(8,128)(2,1)S(1)}, u32[]{:S(2)}, u32[]{:S(2)}) %collective-permute-start.2) | collective-permute-done | bytes 131104 | tf_op jit(solution)/shard_map/ppermute | solution.py:29
  20.6 1.5 %far.1 = (bf16[512,512]{1,0:T(8,128)(2,1)}, bf16[512,512]{1,0:T(8,128)(2,1)}, bf16[512,512]{1,0:T(8,128)(2,1)}, f32[4,8,512]{2,1,0:T(8,128)}, f32[4,128,512]{2,1,0:T(8,128)S(1)}) custom-call(bf16[512,512]{1,0:T(8,128)(2,1)S(1)} %copy-done.1, bf16[512,512]{1,0:T(8,128)(2,1)S(1)} %copy-done.2, ...), custom_call_target="tpu_custom_call", output_to_operand_aliasing={{4}: (5, {})} | custom-call | flops 33554432000 | tf_op jit(solution)/shard_map/far/pallas_call | solution.py:361
  (2 shorter events, 0.0 us)
Async XLA Ops:
  2.2 4.7 %copy-start = (bf16[512,512]{1,0:T(8,128)(2,1)S(1)}, bf16[512,512]{1,0:T(8,128)(2,1)}, u32[]{:S(2)}) copy-start(bf16[512,512]{1,0:T(8,128)(2,1)} %refs_0_.2) | copy-start | bytes 1572868
  2.2 4.7 %copy-start.1 = (bf16[512,512]{1,0:T(8,128)(2,1)S(1)}, bf16[512,512]{1,0:T(8,128)(2,1)}, u32[]{:S(2)}) copy-start(bf16[512,512]{1,0:T(8,128)(2,1)} %refs_0_.3) | copy-start | bytes 1572868
  2.3 4.7 %copy-start.2 = (bf16[512,512]{1,0:T(8,128)(2,1)S(1)}, bf16[512,512]{1,0:T(8,128)(2,1)}, u32[]{:S(2)}) copy-start(bf16[512,512]{1,0:T(8,128)(2,1)} %refs_1_.3) | copy-start | bytes 1572868
  2.3 4.7 %copy-start.3 = (bf16[512,512]{1,0:T(8,128)(2,1)S(1)}, bf16[512,512]{1,0:T(8,128)(2,1)}, u32[]{:S(2)}) copy-start(bf16[512,512]{1,0:T(8,128)(2,1)} %refs_2_.3) | copy-start | bytes 1572868
  2.3 4.7 %copy-start.4 = (f32[4,8,512]{2,1,0:T(8,128)S(1)}, f32[4,8,512]{2,1,0:T(8,128)}, u32[]{:S(2)}) copy-start(f32[4,8,512]{2,1,0:T(8,128)} %refs_3_.3) | copy-start | bytes 196612
  2.3 9.1 %collective-permute-start.5 = (bf16[2,128,128]{2,1,0:T(8,128)(2,1)S(1)}, bf16[2,128,128]{2,1,0:T(8,128)(2,1)S(1)}, u32[]{:S(2)}, u32[]{:S(2)}) collective-permute-start(bf16[2,128,128]{2,1,0:T(8,128)(2,1)S(1)} %get-tuple-element.29.source), channel_id=1, source_target_pairs={{0,6},{2,4},{4,2},{6,0},{8,14},{10,12},{12,10},{14,8},{1,7},{3,5},... | collective-permute-start | bytes 196616 | tf_op jit(solution)/shard_map/ppermute | solution.py:29
  6.3 5.0 %collective-permute-start.3 = (bf16[2,128,128]{2,1,0:T(8,128)(2,1)S(1)}, bf16[2,128,128]{2,1,0:T(8,128)(2,1)S(1)}, u32[]{:S(2)}, u32[]{:S(2)}) collective-permute-start(bf16[2,128,128]{2,1,0:T(8,128)(2,1)S(1)} %x_part.1), channel_id=1, source_target_pairs={{0,2},{2,0},{4,6},{6,4},{8,10},{10,8},{12,14},{14,12},{1,3},{3,1},... | collective-permute-start | bytes 196616 | tf_op jit(solution)/shard_map/ppermute | solution.py:29
  6.9 4.5 %collective-permute-start.4 = (bf16[2,128,128]{2,1,0:T(8,128)(2,1)S(1)}, bf16[2,128,128]{2,1,0:T(8,128)(2,1)S(1)}, u32[]{:S(2)}, u32[]{:S(2)}) collective-permute-start(bf16[2,128,128]{2,1,0:T(8,128)(2,1)S(1)} %get-tuple-element.28.refs_0_), channel_id=1, source_target_pairs={{0,4},{2,6},{4,0},{6,2},{8,12},{10,14},{12,8},{14,10},{1,5},{3,7},... | collective-permute-start | bytes 196616 | tf_op jit(solution)/shard_map/ppermute | solution.py:29
  7.7 12.5 %collective-permute-start = (bf16[4,128,128]{2,1,0:T(8,128)(2,1)S(1)}, bf16[4,128,128]{2,1,0:T(8,128)(2,1)S(1)}, u32[]{:S(2)}, u32[]{:S(2)}) collective-permute-start(bf16[4,128,128]{2,1,0:T(8,128)(2,1)S(1)} %get-tuple-element.26), channel_id=1, source_target_pairs={{0,2},{2,0},{4,6},{6,4},{8,10},{10,8},{12,14},{14,12},{1,3},{3,1},... | collective-permute-start | bytes 393224 | tf_op jit(solution)/shard_map/ppermute | solution.py:29
  9.6 5.8 %collective-permute-start.1 = (bf16[4,128,128]{2,1,0:T(8,128)(2,1)S(1)}, bf16[4,128,128]{2,1,0:T(8,128)(2,1)S(1)}, u32[]{:S(2)}, u32[]{:S(2)}) collective-permute-start(bf16[4,128,128]{2,1,0:T(8,128)(2,1)S(1)} %get-tuple-element.27), channel_id=1, source_target_pairs={{0,4},{2,6},{4,0},{6,2},{8,12},{10,14},{12,8},{14,10},{1,5},{3,7},... | collective-permute-start | bytes 393224 | tf_op jit(solution)/shard_map/ppermute | solution.py:29
  11.4 8.3 %collective-permute-start.7 = (bf16[2,128,128]{2,1,0:T(8,128)(2,1)S(1)}, bf16[2,128,128]{2,1,0:T(8,128)(2,1)S(1)}, u32[]{:S(2)}, u32[]{:S(2)}) collective-permute-start(bf16[2,128,128]{2,1,0:T(8,128)(2,1)S(1)} %quad_sum.1), channel_id=1, source_target_pairs={{0,8},{2,10},{4,12},{6,14},{8,2},{10,0},{12,6},{14,4},{1,9},{3,11}... | collective-permute-start | bytes 196616 | tf_op jit(solution)/shard_map/ppermute | solution.py:37
  14.1 6.1 %collective-permute-start.6 = (bf16[2,128,128]{2,1,0:T(8,128)(2,1)S(1)}, bf16[2,128,128]{2,1,0:T(8,128)(2,1)S(1)}, u32[]{:S(2)}, u32[]{:S(2)}) collective-permute-start(bf16[2,128,128]{2,1,0:T(8,128)(2,1)S(1)} %quad_sum.1), channel_id=1, source_target_pairs={{0,10},{2,8},{4,14},{6,12},{8,0},{10,2},{12,4},{14,6},{1,11},{3,9}... | collective-permute-start | bytes 196616 | tf_op jit(solution)/shard_map/ppermute | solution.py:37
  15.4 5.2 %collective-permute-start.2 = (bf16[4,128,128]{2,1,0:T(8,128)(2,1)S(1)}, bf16[4,128,128]{2,1,0:T(8,128)(2,1)S(1)}, u32[]{:S(2)}, u32[]{:S(2)}) collective-permute-start(bf16[4,128,128]{2,1,0:T(8,128)(2,1)S(1)} %collective-permute-done.1.refs_10_), channel_id=1, source_target_pairs={{0,2},{2,0},{4,6},{6,4},{8,10},{10,8},{12,14},{14,12},{1,3},{3,1},... | collective-permute-start | bytes 393224 | tf_op jit(solution)/shard_map/ppermute | solution.py:29

commit v9 on v8

--- a/solution.py
+++ b/solution.py
@@ -172,12 +172,22 @@
 
 
 def near_kernel(scale, *refs):
-    ins, (sum_out, gw_out, nk_out, nv_out) = refs[:6], refs[6:]
+    ins, (sum_out, gw_out, nk_out, nv_out, gq_out) = refs[:6], refs[6:]
     for h in range(sum_out.shape[0]):
         gw_out[h] = jnp.zeros(gw_out.shape[1:], jnp.float32)
         back, weight = near_head(scale, h, *ins, nk_out, nv_out)
         store_sums(sum_out, h, slice(None), back)
         store_sums(gw_out, h, pl.ds(0, 1), weight)
+
+    @pl.when(block_index() == 0)
+    def _():
+        store_queries(sum_out, gq_out)
+
+
+def store_queries(sum_ref, gq_ref):
+    heads, width, _ = sum_ref.shape
+    for h in range(heads):
+        gq_ref[:, h * width : (h + 1) * width] = sum_ref[h].astype(LOW).T
 
 
 def copy_kernel(source, out):
@@ -205,9 +215,9 @@
 
 def far_kernel(bits, scales, *refs):
     k_ref, v_ref, g_ref, w_ref, qt_ref, _, weight_ref, nk_ref, nv_ref = refs[:9]
-    (r1_ref, z2_ref, d2_ref), refs = refs[9:12], refs[12:]
+    (gq_ref, r1_ref, z2_ref, d2_ref), refs = refs[9:13], refs[13:]
     late_refs, early_refs, refs = refs[: bits - 2], refs[bits - 2 : 2 * bits - 4], refs[2 * bits - 4 :]
-    gq_hbm, gk_hbm, gv_hbm, gw_hbm, sum_ref, gq_buf, gk_buf, gv_buf, gw_buf, sems, w_sem = refs
+    gq_hbm, gk_hbm, gv_hbm, gw_hbm, sum_ref, gq_buf, gk_buf, gv_buf, gw_buf, sems, w_sem, gq_sem = refs
     heads, width, tokens = sum_ref.shape
     half = heads // 2
     place = block_index()
@@ -231,6 +241,10 @@
         copy = pltpu.make_async_copy(buf.at[first // GROUP], hbm.at[:, span], sems.at[i, first])
         copy.start()
         copies.append(copy)
+
+    @pl.when(place == 0)
+    def _():
+        pltpu.make_async_copy(gq_ref, gq_hbm, gq_sem).start()
 
     gw_buf[...] = weight_ref[...]
     for level in range(1, bits + 1):
@@ -251,10 +265,12 @@
     copy = pltpu.make_async_copy(gw_buf, gw_hbm, w_sem)
     copy.start()
     copies.append(copy)
-    for first in range(0, heads, GROUP):
-        for i in range(GROUP):
-            gq_buf[first // GROUP, :, i * width : i * width + width] = sum_ref[first + i].astype(LOW).T
-        send(2, first, gq_buf, gq_hbm)
+
+    @pl.when(place != 0)
+    def _():
+        store_queries(sum_ref, gq_buf)
+        pltpu.make_async_copy(gq_buf, gq_hbm, gq_sem).start()
+
     for first in range(0, heads, GROUP):
         group = range(first, first + GROUP)
         reverses = []
@@ -272,6 +288,7 @@
         gv_buf[first // GROUP] = (near_v + nn(key, low)).astype(LOW)
         send(0, first, gk_buf, gk_hbm)
         send(1, first, gv_buf, gv_hbm)
+    pltpu.make_async_copy(gq_buf, gq_hbm, gq_sem).wait()
     for copy in copies:
         copy.wait()
 
@@ -350,13 +367,14 @@
     early_half = [swap_halves(x, i + 2, True) for i, x in enumerate(sums)]
     late_half = [swap_halves(x, i + 2, False) for i, x in enumerate(sums)]
     diagonal_2 = flip(got_2, 1)
-    total, weights, near_k, near_v = call(
+    flat = ((tokens, heads * width), LOW)
+    total, weights, near_k, near_v, early_q = call(
         functools.partial(near_kernel, scales[0]), "near", cost,
-        [((heads, width, tokens), f32), weight_rows, *[((heads, tokens, width), f32)] * 2],
+        [((heads, width, tokens), f32), weight_rows, *[((heads, tokens, width), f32)] * 2, flat],
         [queries, keys, values, out_grad, level_weights, kt],
     )
     operands = [keys, values, out_grad, level_weights, qt, total, weights, near_k, near_v]
-    operands += [got_1, got_2, diagonal_2, *late_half, *early_half]
+    operands += [early_q, got_1, got_2, diagonal_2, *late_half, *early_half]
     out = jax.ShapeDtypeStruct((tokens, heads * width), LOW)
     return pl.pallas_call(
         functools.partial(far_kernel, bits, scales),
@@ -367,10 +385,12 @@
         in_specs=[IN_VMEM] * len(operands),
         out_specs=(ANY,) * 4 + (IN_VMEM,),
         input_output_aliases={5: 4},
-        scratch_shapes=[pltpu.VMEM((heads // GROUP, tokens, GROUP * width), LOW)] * 3
+        scratch_shapes=[pltpu.VMEM(*flat)]
+        + [pltpu.VMEM((heads // GROUP, tokens, GROUP * width), LOW)] * 2
         + [
             pltpu.VMEM((heads, levels, tokens), f32),
-            pltpu.SemaphoreType.DMA((3, heads)),
+            pltpu.SemaphoreType.DMA((2, heads)),
+            pltpu.SemaphoreType.DMA,
             pltpu.SemaphoreType.DMA,
         ],
         compiler_params=pltpu.CompilerParams(vmem_limit_bytes=LIMIT),

time: 22.2 us -> 22.1 us (level)
  transfers between devices with their start and end apart: 8 -> 8, of which waited for: 4 -> 4; matrix products, arithmetic and copies ran while one was open for 0% -> 0% of each run, Pallas kernels for 15% -> 16%
where the time goes in v9:
time: 22.1 us; the launch traced here: 22 us
  starting transfers between devices  13.9 us (63%)
  Pallas kernels  6.49 us (29%)
  waiting for transfers between devices  0.88 us (4%)
  between operations  0.72 us (3%)
    ppermute x6, starting transfers between devices, flip(): return lax.ppermute(block, AXES, [(i, i ^ mask) for i in range(size)])  9.85 us
    ppermute x2, starting transfers between devices, swap_halves(): return lax.ppermute(block, AXES, routes)  4.01 us
    pallas_call x4, Pallas kernels, call(): pl.pallas_call(kernel, out_shape=outs, in_specs=[IN_VMEM] * len(operands)...  3.5 us
    pallas_call x1, Pallas kernels, on_device(): pl.pallas_call(functools.partial(top_kernel, bits, scales), out_shape=[pl...  1.59 us
    pallas_call x1, Pallas kernels, on_device(): pl.pallas_call(functools.partial(far_kernel, bits, scales), out_shape=(ou...  1.4 us
    ppermute x6, waiting for transfers between devices, flip(): return lax.ppermute(block, AXES, [(i, i ^ mask) for i in range(size)])  0.6 us
  transfers between devices with their start and end apart: 8, of which 4 were waited for; matrix products, arithmetic and copies ran while one was open for 0% of the time, Pallas kernels for 16%

profile of v9, /device:TPU:0, one launch (start us, length us, event | category | flops | bytes accessed | tf_op | source)
XLA Modules:
  0.0 22.0 jit_solution(8562887016961533109)
XLA Ops:
  0.6 1.6 %top_states.1 = (bf16[4,128,512]{2,1,0:T(8,128)(2,1)S(1)}, bf16[2,128,128]{2,1,0:T(8,128)(2,1)S(1)}, bf16[2,128,128]{2,1,0:T(8,128)(2,1)S(1)}) custom-call(bf16[512,512]{1,0:T(8,128)(2,1)} %refs_0_.2, bf16[512,512]{1,0:T(8,128)(2,1)} %refs_0_.3, bf16[512,512]{1,0:T(8,128)(2,1)} %refs_1_.3, bf16[512,512]{1,0:T(8,128)(2,1)} %refs_2_.3, f32[4,8,512]{2,1,0:T(8,128)} %refs_3_.3), custom_call_target="tpu_custom_call" | custom-call | flops 33554432000 | tf_op jit(solution)/shard_map/top_states/pallas_call | solution.py:333
  2.2 0.0 copy-start
  2.2 0.0 copy-start.1
  2.3 0.0 copy-start.2
  2.3 0.0 copy-start.3
  2.3 0.0 copy-start.4
  2.3 4.0 %collective-permute-start.5 = (bf16[2,128,128]{2,1,0:T(8,128)(2,1)S(1)}, bf16[2,128,128]{2,1,0:T(8,128)(2,1)S(1)}, u32[]{:S(2)}, u32[]{:S(2)}) collective-permute-start(bf16[2,128,128]{2,1,0:T(8,128)(2,1)S(1)} %get-tuple-element.31.source), channel_id=1, source_target_pairs={{0,6},{2,4},{4,2},{6,0},{8,14},{10,12},{12,10},{14,8},{1,7},{3,5},... | collective-permute-start | bytes 196616 | tf_op jit(solution)/shard_map/ppermute | solution.py:29
  6.3 0.5 %collective-permute-start.3 = (bf16[2,128,128]{2,1,0:T(8,128)(2,1)S(1)}, bf16[2,128,128]{2,1,0:T(8,128)(2,1)S(1)}, u32[]{:S(2)}, u32[]{:S(2)}) collective-permute-start(bf16[2,128,128]{2,1,0:T(8,128)(2,1)S(1)} %x_part.1), channel_id=1, source_target_pairs={{0,2},{2,0},{4,6},{6,4},{8,10},{10,8},{12,14},{14,12},{1,3},{3,1},... | collective-permute-start | bytes 196616 | tf_op jit(solution)/shard_map/ppermute | solution.py:29
  6.9 0.1 collective-permute-start.4
  7.0 0.0 copy-done
  7.0 0.0 copy-done.1
  7.0 0.0 copy-done.2
  7.0 0.0 copy-done.3
  7.0 0.0 copy-done.4
  7.0 0.7 %low_states.1 = (bf16[4,128,512]{2,1,0:T(8,128)(2,1)S(1)}, bf16[4,128,512]{2,1,0:T(8,128)(2,1)S(1)}, bf16[4,128,128]{2,1,0:T(8,128)(2,1)S(1)}, bf16[4,128,128]{2,1,0:T(8,128)(2,1)S(1)}) custom-call(bf16[512,512]{1,0:T(8,128)(2,1)S(1)} %copy-done, bf16[512,512]{1,0:T(8,128)(2,1)S(1)} %copy-done.1, bf16[512,512]{1,0:T(8,128)(2,1)S(1)} %copy-done.2, ...), custom_call_target="tpu_custom_call" | custom-call | flops 33554432000 | tf_op jit(solution)/shard_map/low_states/pallas_call | solution.py:307
  7.7 1.9 %collective-permute-start = (bf16[4,128,128]{2,1,0:T(8,128)(2,1)S(1)}, bf16[4,128,128]{2,1,0:T(8,128)(2,1)S(1)}, u32[]{:S(2)}, u32[]{:S(2)}) collective-permute-start(bf16[4,128,128]{2,1,0:T(8,128)(2,1)S(1)} %get-tuple-element.28), channel_id=1, source_target_pairs={{0,2},{2,0},{4,6},{6,4},{8,10},{10,8},{12,14},{14,12},{1,3},{3,1},... | collective-permute-start | bytes 393224 | tf_op jit(solution)/shard_map/ppermute | solution.py:29
  9.6 1.6 %collective-permute-start.1 = (bf16[4,128,128]{2,1,0:T(8,128)(2,1)S(1)}, bf16[4,128,128]{2,1,0:T(8,128)(2,1)S(1)}, u32[]{:S(2)}, u32[]{:S(2)}) collective-permute-start(bf16[4,128,128]{2,1,0:T(8,128)(2,1)S(1)} %get-tuple-element.29), channel_id=1, source_target_pairs={{0,4},{2,6},{4,0},{6,2},{8,12},{10,14},{12,8},{14,10},{1,5},{3,7},... | collective-permute-start | bytes 393224 | tf_op jit(solution)/shard_map/ppermute | solution.py:29
  11.2 0.1 collective-permute-done.3.refs_1_
  11.3 0.1 collective-permute-done.4.refs_2_
  11.4 0.0 collective-permute-done.5.refs_3_
  11.4 2.7 %collective-permute-start.7 = (bf16[2,128,128]{2,1,0:T(8,128)(2,1)S(1)}, bf16[2,128,128]{2,1,0:T(8,128)(2,1)S(1)}, u32[]{:S(2)}, u32[]{:S(2)}) collective-permute-start(bf16[2,128,128]{2,1,0:T(8,128)(2,1)S(1)} %quad_sum.1), channel_id=1, source_target_pairs={{0,8},{2,10},{4,12},{6,14},{8,2},{10,0},{12,6},{14,4},{1,9},{3,11}... | collective-permute-start | bytes 196616 | tf_op jit(solution)/shard_map/ppermute | solution.py:37
  14.1 1.4 %collective-permute-start.6 = (bf16[2,128,128]{2,1,0:T(8,128)(2,1)S(1)}, bf16[2,128,128]{2,1,0:T(8,128)(2,1)S(1)}, u32[]{:S(2)}, u32[]{:S(2)}) collective-permute-start(bf16[2,128,128]{2,1,0:T(8,128)(2,1)S(1)} %quad_sum.1), channel_id=1, source_target_pairs={{0,10},{2,8},{4,14},{6,12},{8,0},{10,2},{12,4},{14,6},{1,11},{3,9}... | collective-permute-start | bytes 196616 | tf_op jit(solution)/shard_map/ppermute | solution.py:37
  15.4 0.0 collective-permute-done.1.refs_11_
  15.4 1.7 %collective-permute-start.2 = (bf16[4,128,128]{2,1,0:T(8,128)(2,1)S(1)}, bf16[4,128,128]{2,1,0:T(8,128)(2,1)S(1)}, u32[]{:S(2)}, u32[]{:S(2)}) collective-permute-start(bf16[4,128,128]{2,1,0:T(8,128)(2,1)S(1)} %collective-permute-done.1.refs_11_), channel_id=1, source_target_pairs={{0,2},{2,0},{4,6},{6,4},{8,10},{10,8},{12,14},{14,12},{1,3},{3,1},... | collective-permute-start | bytes 393224 | tf_op jit(solution)/shard_map/ppermute | solution.py:29
  17.2 2.7 %near.1 = (f32[4,128,512]{2,1,0:T(8,128)S(1)}, f32[4,8,512]{2,1,0:T(8,128)S(1)}, f32[4,512,128]{2,1,0:T(8,128)S(1)}, f32[4,512,128]{2,1,0:T(8,128)S(1)}, bf16[512,512]{1,0:T(8,128)(2,1)S(1)}) custom-call(bf16[512,512]{1,0:T(8,128)(2,1)S(1)} %copy-done, bf16[512,512]{1,0:T(8,128)(2,1)S(1)} %copy-done.1, bf16[512,512]{1,0:T(8,128)(2,1)S(1)} %copy-done.2, ...), custom_call_target="tpu_custom_call" | custom-call | flops 33554432000 | tf_op jit(solution)/shard_map/near/pallas_call | solution.py:307
  19.9 0.0 collective-permute-done.7.refs_14_
  19.9 0.3 %collective-permute-done.6.refs_13_ = bf16[2,128,128]{2,1,0:T(8,128)(2,1)S(1)} collective-permute-done((bf16[2,128,128]{2,1,0:T(8,128)(2,1)S(1)}, bf16[2,128,128]{2,1,0:T(8,128)(2,1)S(1)}, u32[]{:S(2)}, u32[]{:S(2)}) %collective-permute-start.6) | collective-permute-done | bytes 65568 | tf_op jit(solution)/shard_map/ppermute | solution.py:37
  20.2 0.0 collective-permute-done.refs_10_
  20.2 0.4 %collective-permute-done.2.refs_12_ = bf16[4,128,128]{2,1,0:T(8,128)(2,1)S(1)} collective-permute-done((bf16[4,128,128]{2,1,0:T(8,128)(2,1)S(1)}, bf16[4,128,128]{2,1,0:T(8,128)(2,1)S(1)}, u32[]{:S(2)}, u32[]{:S(2)}) %collective-permute-start.2) | collective-permute-done | bytes 131104 | tf_op jit(solution)/shard_map/ppermute | solution.py:29
  20.6 1.4 %far.1 = (bf16[512,512]{1,0:T(8,128)(2,1)}, bf16[512,512]{1,0:T(8,128)(2,1)}, bf16[512,512]{1,0:T(8,128)(2,1)}, f32[4,8,512]{2,1,0:T(8,128)}, f32[4,128,512]{2,1,0:T(8,128)S(1)}) custom-call(bf16[512,512]{1,0:T(8,128)(2,1)S(1)} %copy-done.1, bf16[512,512]{1,0:T(8,128)(2,1)S(1)} %copy-done.2, ...), custom_call_target="tpu_custom_call", output_to_operand_aliasing={{4}: (5, {})} | custom-call | flops 33554432000 | tf_op jit(solution)/shard_map/far/pallas_call | solution.py:379
  (2 shorter events, 0.0 us)
Async XLA Ops:
  2.2 4.7 %copy-start = (bf16[512,512]{1,0:T(8,128)(2,1)S(1)}, bf16[512,512]{1,0:T(8,128)(2,1)}, u32[]{:S(2)}) copy-start(bf16[512,512]{1,0:T(8,128)(2,1)} %refs_0_.2) | copy-start | bytes 1572868
  2.2 4.7 %copy-start.1 = (bf16[512,512]{1,0:T(8,128)(2,1)S(1)}, bf16[512,512]{1,0:T(8,128)(2,1)}, u32[]{:S(2)}) copy-start(bf16[512,512]{1,0:T(8,128)(2,1)} %refs_0_.3) | copy-start | bytes 1572868
  2.3 4.7 %copy-start.2 = (bf16[512,512]{1,0:T(8,128)(2,1)S(1)}, bf16[512,512]{1,0:T(8,128)(2,1)}, u32[]{:S(2)}) copy-start(bf16[512,512]{1,0:T(8,128)(2,1)} %refs_1_.3) | copy-start | bytes 1572868
  2.3 4.7 %copy-start.3 = (bf16[512,512]{1,0:T(8,128)(2,1)S(1)}, bf16[512,512]{1,0:T(8,128)(2,1)}, u32[]{:S(2)}) copy-start(bf16[512,512]{1,0:T(8,128)(2,1)} %refs_2_.3) | copy-start | bytes 1572868
  2.3 4.7 %copy-start.4 = (f32[4,8,512]{2,1,0:T(8,128)S(1)}, f32[4,8,512]{2,1,0:T(8,128)}, u32[]{:S(2)}) copy-start(f32[4,8,512]{2,1,0:T(8,128)} %refs_3_.3) | copy-start | bytes 196612
  2.3 9.1 %collective-permute-start.5 = (bf16[2,128,128]{2,1,0:T(8,128)(2,1)S(1)}, bf16[2,128,128]{2,1,0:T(8,128)(2,1)S(1)}, u32[]{:S(2)}, u32[]{:S(2)}) collective-permute-start(bf16[2,128,128]{2,1,0:T(8,128)(2,1)S(1)} %get-tuple-element.31.source), channel_id=1, source_target_pairs={{0,6},{2,4},{4,2},{6,0},{8,14},{10,12},{12,10},{14,8},{1,7},{3,5},... | collective-permute-start | bytes 196616 | tf_op jit(solution)/shard_map/ppermute | solution.py:29
  6.3 5.0 %collective-permute-start.3 = (bf16[2,128,128]{2,1,0:T(8,128)(2,1)S(1)}, bf16[2,128,128]{2,1,0:T(8,128)(2,1)S(1)}, u32[]{:S(2)}, u32[]{:S(2)}) collective-permute-start(bf16[2,128,128]{2,1,0:T(8,128)(2,1)S(1)} %x_part.1), channel_id=1, source_target_pairs={{0,2},{2,0},{4,6},{6,4},{8,10},{10,8},{12,14},{14,12},{1,3},{3,1},... | collective-permute-start | bytes 196616 | tf_op jit(solution)/shard_map/ppermute | solution.py:29
  6.9 4.5 %collective-permute-start.4 = (bf16[2,128,128]{2,1,0:T(8,128)(2,1)S(1)}, bf16[2,128,128]{2,1,0:T(8,128)(2,1)S(1)}, u32[]{:S(2)}, u32[]{:S(2)}) collective-permute-start(bf16[2,128,128]{2,1,0:T(8,128)(2,1)S(1)} %get-tuple-element.30.refs_0_), channel_id=1, source_target_pairs={{0,4},{2,6},{4,0},{6,2},{8,12},{10,14},{12,8},{14,10},{1,5},{3,7},... | collective-permute-start | bytes 196616 | tf_op jit(solution)/shard_map/ppermute | solution.py:29
  7.7 12.5 %collective-permute-start = (bf16[4,128,128]{2,1,0:T(8,128)(2,1)S(1)}, bf16[4,128,128]{2,1,0:T(8,128)(2,1)S(1)}, u32[]{:S(2)}, u32[]{:S(2)}) collective-permute-start(bf16[4,128,128]{2,1,0:T(8,128)(2,1)S(1)} %get-tuple-element.28), channel_id=1, source_target_pairs={{0,2},{2,0},{4,6},{6,4},{8,10},{10,8},{12,14},{14,12},{1,3},{3,1},... | collective-permute-start | bytes 393224 | tf_op jit(solution)/shard_map/ppermute | solution.py:29
  9.6 5.8 %collective-permute-start.1 = (bf16[4,128,128]{2,1,0:T(8,128)(2,1)S(1)}, bf16[4,128,128]{2,1,0:T(8,128)(2,1)S(1)}, u32[]{:S(2)}, u32[]{:S(2)}) collective-permute-start(bf16[4,128,128]{2,1,0:T(8,128)(2,1)S(1)} %get-tuple-element.29), channel_id=1, source_target_pairs={{0,4},{2,6},{4,0},{6,2},{8,12},{10,14},{12,8},{14,10},{1,5},{3,7},... | collective-permute-start | bytes 393224 | tf_op jit(solution)/shard_map/ppermute | solution.py:29
  11.4 8.5 %collective-permute-start.7 = (bf16[2,128,128]{2,1,0:T(8,128)(2,1)S(1)}, bf16[2,128,128]{2,1,0:T(8,128)(2,1)S(1)}, u32[]{:S(2)}, u32[]{:S(2)}) collective-permute-start(bf16[2,128,128]{2,1,0:T(8,128)(2,1)S(1)} %quad_sum.1), channel_id=1, source_target_pairs={{0,8},{2,10},{4,12},{6,14},{8,2},{10,0},{12,6},{14,4},{1,9},{3,11}... | collective-permute-start | bytes 196616 | tf_op jit(solution)/shard_map/ppermute | solution.py:37
  14.1 6.1 %collective-permute-start.6 = (bf16[2,128,128]{2,1,0:T(8,128)(2,1)S(1)}, bf16[2,128,128]{2,1,0:T(8,128)(2,1)S(1)}, u32[]{:S(2)}, u32[]{:S(2)}) collective-permute-start(bf16[2,128,128]{2,1,0:T(8,128)(2,1)S(1)} %quad_sum.1), channel_id=1, source_target_pairs={{0,10},{2,8},{4,14},{6,12},{8,0},{10,2},{12,4},{14,6},{1,11},{3,9}... | collective-permute-start | bytes 196616 | tf_op jit(solution)/shard_map/ppermute | solution.py:37
  15.4 5.2 %collective-permute-start.2 = (bf16[4,128,128]{2,1,0:T(8,128)(2,1)S(1)}, bf16[4,128,128]{2,1,0:T(8,128)(2,1)S(1)}, u32[]{:S(2)}, u32[]{:S(2)}) collective-permute-start(bf16[4,128,128]{2,1,0:T(8,128)(2,1)S(1)} %collective-permute-done.1.refs_11_), channel_id=1, source_target_pairs={{0,2},{2,0},{4,6},{6,4},{8,10},{10,8},{12,14},{14,12},{1,3},{3,1},... | collective-permute-start | bytes 393224 | tf_op jit(solution)/shard_map/ppermute | solution.py:29

commit v10 on v9

--- a/solution.py
+++ b/solution.py
@@ -356,8 +356,9 @@
         functools.partial(low_kernel, bits, scales), "low_states", cost,
         [turned, turned, full, full], [queries, keys, values, out_grad, level_weights, t_v],
     )
+    got_2 = flip(d2, 2)
+    (d1,) = call(copy_kernel, "first_level", cost, [full], [d1])
     got_1 = flip(d1, 1)
-    got_2 = flip(d2, 2)
     sums = []
     for bit in range(2, bits):
         sums.append(quad[:half])

time: 22.1 us -> 22.1 us (level)
    pallas_call x4 -> x5, Pallas kernels: 3.5 us -> 3.51 us  [call(): pl.pallas_call(kernel, out_shape=outs, in_specs=[IN_VMEM] * len(operands)...]
  transfers between devices with their start and end apart: 8 -> 8, of which waited for: 4 -> 5; matrix products, arithmetic and copies ran while one was open for 0% -> 0% of each run, Pallas kernels for 16% -> 16%
where the time goes in v10:
time: 22.1 us; the launch traced here: 22 us
  starting transfers between devices  13.9 us (63%)
  Pallas kernels  6.5 us (29%)
  waiting for transfers between devices  0.86 us (4%)
  between operations  0.72 us (3%)
    ppermute x6, starting transfers between devices, flip(): return lax.ppermute(block, AXES, [(i, i ^ mask) for i in range(size)])  9.85 us
    ppermute x2, starting transfers between devices, swap_halves(): return lax.ppermute(block, AXES, routes)  4.02 us
    pallas_call x5, Pallas kernels, call(): pl.pallas_call(kernel, out_shape=outs, in_specs=[IN_VMEM] * len(operands)...  3.51 us
    pallas_call x1, Pallas kernels, on_device(): pl.pallas_call(functools.partial(top_kernel, bits, scales), out_shape=[pl...  1.59 us
    pallas_call x1, Pallas kernels, on_device(): pl.pallas_call(functools.partial(far_kernel, bits, scales), out_shape=(ou...  1.4 us
    ppermute x6, waiting for transfers between devices, flip(): return lax.ppermute(block, AXES, [(i, i ^ mask) for i in range(size)])  0.57 us
  transfers between devices with their start and end apart: 8, of which 5 were waited for; matrix products, arithmetic and copies ran while one was open for 0% of the time, Pallas kernels for 16%

profile of v10, /device:TPU:0, one launch (start us, length us, event | category | flops | bytes accessed | tf_op | source)
XLA Modules:
  0.0 22.0 jit_solution(1492246559367325765)
XLA Ops:
  0.6 1.6 %top_states.1 = (bf16[4,128,512]{2,1,0:T(8,128)(2,1)S(1)}, bf16[2,128,128]{2,1,0:T(8,128)(2,1)S(1)}, bf16[2,128,128]{2,1,0:T(8,128)(2,1)S(1)}) custom-call(bf16[512,512]{1,0:T(8,128)(2,1)} %refs_0_.2, bf16[512,512]{1,0:T(8,128)(2,1)} %refs_0_.3, bf16[512,512]{1,0:T(8,128)(2,1)} %refs_1_.3, bf16[512,512]{1,0:T(8,128)(2,1)} %refs_2_.3, f32[4,8,512]{2,1,0:T(8,128)} %refs_3_.3), custom_call_target="tpu_custom_call" | custom-call | flops 33554432000 | tf_op jit(solution)/shard_map/top_states/pallas_call | solution.py:333
  2.2 0.0 copy-start
  2.2 0.0 copy-start.1
  2.3 0.0 copy-start.2
  2.3 0.0 copy-start.3
  2.3 0.0 copy-start.4
  2.3 4.0 %collective-permute-start.5 = (bf16[2,128,128]{2,1,0:T(8,128)(2,1)S(1)}, bf16[2,128,128]{2,1,0:T(8,128)(2,1)S(1)}, u32[]{:S(2)}, u32[]{:S(2)}) collective-permute-start(bf16[2,128,128]{2,1,0:T(8,128)(2,1)S(1)} %get-tuple-element.31.source), channel_id=1, source_target_pairs={{0,6},{2,4},{4,2},{6,0},{8,14},{10,12},{12,10},{14,8},{1,7},{3,5},... | collective-permute-start | bytes 196616 | tf_op jit(solution)/shard_map/ppermute | solution.py:29
  6.3 0.5 %collective-permute-start.3 = (bf16[2,128,128]{2,1,0:T(8,128)(2,1)S(1)}, bf16[2,128,128]{2,1,0:T(8,128)(2,1)S(1)}, u32[]{:S(2)}, u32[]{:S(2)}) collective-permute-start(bf16[2,128,128]{2,1,0:T(8,128)(2,1)S(1)} %x_part.1), channel_id=1, source_target_pairs={{0,2},{2,0},{4,6},{6,4},{8,10},{10,8},{12,14},{14,12},{1,3},{3,1},... | collective-permute-start | bytes 196616 | tf_op jit(solution)/shard_map/ppermute | solution.py:29
  6.9 0.1 collective-permute-start.4
  7.0 0.0 copy-done
  7.0 0.0 copy-done.1
  7.0 0.0 copy-done.2
  7.0 0.0 copy-done.3
  7.0 0.0 copy-done.4
  7.0 0.7 %low_states.1 = (bf16[4,128,512]{2,1,0:T(8,128)(2,1)S(1)}, bf16[4,128,512]{2,1,0:T(8,128)(2,1)S(1)}, bf16[4,128,128]{2,1,0:T(8,128)(2,1)S(1)}, bf16[4,128,128]{2,1,0:T(8,128)(2,1)S(1)}) custom-call(bf16[512,512]{1,0:T(8,128)(2,1)S(1)} %copy-done, bf16[512,512]{1,0:T(8,128)(2,1)S(1)} %copy-done.1, bf16[512,512]{1,0:T(8,128)(2,1)S(1)} %copy-done.2, ...), custom_call_target="tpu_custom_call" | custom-call | flops 33554432000 | tf_op jit(solution)/shard_map/low_states/pallas_call | solution.py:307
  7.7 1.9 %collective-permute-start = (bf16[4,128,128]{2,1,0:T(8,128)(2,1)S(1)}, bf16[4,128,128]{2,1,0:T(8,128)(2,1)S(1)}, u32[]{:S(2)}, u32[]{:S(2)}) collective-permute-start(bf16[4,128,128]{2,1,0:T(8,128)(2,1)S(1)} %first_level.1), channel_id=1, source_target_pairs={{0,2},{2,0},{4,6},{6,4},{8,10},{10,8},{12,14},{14,12},{1,3},{3,1},... | collective-permute-start | bytes 393224 | tf_op jit(solution)/shard_map/ppermute | solution.py:29
  9.6 1.6 %collective-permute-start.1 = (bf16[4,128,128]{2,1,0:T(8,128)(2,1)S(1)}, bf16[4,128,128]{2,1,0:T(8,128)(2,1)S(1)}, u32[]{:S(2)}, u32[]{:S(2)}) collective-permute-start(bf16[4,128,128]{2,1,0:T(8,128)(2,1)S(1)} %get-tuple-element.29), channel_id=1, source_target_pairs={{0,4},{2,6},{4,0},{6,2},{8,12},{10,14},{12,8},{14,10},{1,5},{3,7},... | collective-permute-start | bytes 393224 | tf_op jit(solution)/shard_map/ppermute | solution.py:29
  11.2 0.1 collective-permute-done.3.refs_1_
  11.3 0.1 collective-permute-done.4.refs_2_
  11.4 0.0 collective-permute-done.5.refs_3_
  11.4 2.6 %collective-permute-start.7 = (bf16[2,128,128]{2,1,0:T(8,128)(2,1)S(1)}, bf16[2,128,128]{2,1,0:T(8,128)(2,1)S(1)}, u32[]{:S(2)}, u32[]{:S(2)}) collective-permute-start(bf16[2,128,128]{2,1,0:T(8,128)(2,1)S(1)} %quad_sum.1), channel_id=1, source_target_pairs={{0,8},{2,10},{4,12},{6,14},{8,2},{10,0},{12,6},{14,4},{1,9},{3,11}... | collective-permute-start | bytes 196616 | tf_op jit(solution)/shard_map/ppermute | solution.py:37
  14.1 1.4 %collective-permute-start.6 = (bf16[2,128,128]{2,1,0:T(8,128)(2,1)S(1)}, bf16[2,128,128]{2,1,0:T(8,128)(2,1)S(1)}, u32[]{:S(2)}, u32[]{:S(2)}) collective-permute-start(bf16[2,128,128]{2,1,0:T(8,128)(2,1)S(1)} %quad_sum.1), channel_id=1, source_target_pairs={{0,10},{2,8},{4,14},{6,12},{8,0},{10,2},{12,4},{14,6},{1,11},{3,9}... | collective-permute-start | bytes 196616 | tf_op jit(solution)/shard_map/ppermute | solution.py:37
  15.4 0.0 collective-permute-done.1.refs_11_
  15.4 1.7 %collective-permute-start.2 = (bf16[4,128,128]{2,1,0:T(8,128)(2,1)S(1)}, bf16[4,128,128]{2,1,0:T(8,128)(2,1)S(1)}, u32[]{:S(2)}, u32[]{:S(2)}) collective-permute-start(bf16[4,128,128]{2,1,0:T(8,128)(2,1)S(1)} %collective-permute-done.1.refs_11_), channel_id=1, source_target_pairs={{0,2},{2,0},{4,6},{6,4},{8,10},{10,8},{12,14},{14,12},{1,3},{3,1},... | collective-permute-start | bytes 393224 | tf_op jit(solution)/shard_map/ppermute | solution.py:29
  17.2 2.7 %near.1 = (f32[4,128,512]{2,1,0:T(8,128)S(1)}, f32[4,8,512]{2,1,0:T(8,128)S(1)}, f32[4,512,128]{2,1,0:T(8,128)S(1)}, f32[4,512,128]{2,1,0:T(8,128)S(1)}, bf16[512,512]{1,0:T(8,128)(2,1)S(1)}) custom-call(bf16[512,512]{1,0:T(8,128)(2,1)S(1)} %copy-done, bf16[512,512]{1,0:T(8,128)(2,1)S(1)} %copy-done.1, bf16[512,512]{1,0:T(8,128)(2,1)S(1)} %copy-done.2, ...), custom_call_target="tpu_custom_call" | custom-call | flops 33554432000 | tf_op jit(solution)/shard_map/near/pallas_call | solution.py:307
  19.9 0.1 collective-permute-done.7.refs_14_
  20.0 0.2 collective-permute-done.6.refs_13_
  20.2 0.0 collective-permute-done.refs_10_
  20.2 0.4 %collective-permute-done.2.refs_12_ = bf16[4,128,128]{2,1,0:T(8,128)(2,1)S(1)} collective-permute-done((bf16[4,128,128]{2,1,0:T(8,128)(2,1)S(1)}, bf16[4,128,128]{2,1,0:T(8,128)(2,1)S(1)}, u32[]{:S(2)}, u32[]{:S(2)}) %collective-permute-start.2) | collective-permute-done | bytes 131104 | tf_op jit(solution)/shard_map/ppermute | solution.py:29
  20.6 1.4 %far.1 = (bf16[512,512]{1,0:T(8,128)(2,1)}, bf16[512,512]{1,0:T(8,128)(2,1)}, bf16[512,512]{1,0:T(8,128)(2,1)}, f32[4,8,512]{2,1,0:T(8,128)}, f32[4,128,512]{2,1,0:T(8,128)S(1)}) custom-call(bf16[512,512]{1,0:T(8,128)(2,1)S(1)} %copy-done.1, bf16[512,512]{1,0:T(8,128)(2,1)S(1)} %copy-done.2, ...), custom_call_target="tpu_custom_call", output_to_operand_aliasing={{4}: (5, {})} | custom-call | flops 33554432000 | tf_op jit(solution)/shard_map/far/pallas_call | solution.py:380
  (3 shorter events, 0.1 us)
Async XLA Ops:
  2.2 4.7 %copy-start = (bf16[512,512]{1,0:T(8,128)(2,1)S(1)}, bf16[512,512]{1,0:T(8,128)(2,1)}, u32[]{:S(2)}) copy-start(bf16[512,512]{1,0:T(8,128)(2,1)} %refs_0_.2) | copy-start | bytes 1572868
  2.2 4.7 %copy-start.1 = (bf16[512,512]{1,0:T(8,128)(2,1)S(1)}, bf16[512,512]{1,0:T(8,128)(2,1)}, u32[]{:S(2)}) copy-start(bf16[512,512]{1,0:T(8,128)(2,1)} %refs_0_.3) | copy-start | bytes 1572868
  2.3 4.7 %copy-start.2 = (bf16[512,512]{1,0:T(8,128)(2,1)S(1)}, bf16[512,512]{1,0:T(8,128)(2,1)}, u32[]{:S(2)}) copy-start(bf16[512,512]{1,0:T(8,128)(2,1)} %refs_1_.3) | copy-start | bytes 1572868
  2.3 4.7 %copy-start.3 = (bf16[512,512]{1,0:T(8,128)(2,1)S(1)}, bf16[512,512]{1,0:T(8,128)(2,1)}, u32[]{:S(2)}) copy-start(bf16[512,512]{1,0:T(8,128)(2,1)} %refs_2_.3) | copy-start | bytes 1572868
  2.3 4.7 %copy-start.4 = (f32[4,8,512]{2,1,0:T(8,128)S(1)}, f32[4,8,512]{2,1,0:T(8,128)}, u32[]{:S(2)}) copy-start(f32[4,8,512]{2,1,0:T(8,128)} %refs_3_.3) | copy-start | bytes 196612
  2.3 9.1 %collective-permute-start.5 = (bf16[2,128,128]{2,1,0:T(8,128)(2,1)S(1)}, bf16[2,128,128]{2,1,0:T(8,128)(2,1)S(1)}, u32[]{:S(2)}, u32[]{:S(2)}) collective-permute-start(bf16[2,128,128]{2,1,0:T(8,128)(2,1)S(1)} %get-tuple-element.31.source), channel_id=1, source_target_pairs={{0,6},{2,4},{4,2},{6,0},{8,14},{10,12},{12,10},{14,8},{1,7},{3,5},... | collective-permute-start | bytes 196616 | tf_op jit(solution)/shard_map/ppermute | solution.py:29
  6.3 5.0 %collective-permute-start.3 = (bf16[2,128,128]{2,1,0:T(8,128)(2,1)S(1)}, bf16[2,128,128]{2,1,0:T(8,128)(2,1)S(1)}, u32[]{:S(2)}, u32[]{:S(2)}) collective-permute-start(bf16[2,128,128]{2,1,0:T(8,128)(2,1)S(1)} %x_part.1), channel_id=1, source_target_pairs={{0,2},{2,0},{4,6},{6,4},{8,10},{10,8},{12,14},{14,12},{1,3},{3,1},... | collective-permute-start | bytes 196616 | tf_op jit(solution)/shard_map/ppermute | solution.py:29
  6.9 4.5 %collective-permute-start.4 = (bf16[2,128,128]{2,1,0:T(8,128)(2,1)S(1)}, bf16[2,128,128]{2,1,0:T(8,128)(2,1)S(1)}, u32[]{:S(2)}, u32[]{:S(2)}) collective-permute-start(bf16[2,128,128]{2,1,0:T(8,128)(2,1)S(1)} %get-tuple-element.30.refs_0_), channel_id=1, source_target_pairs={{0,4},{2,6},{4,0},{6,2},{8,12},{10,14},{12,8},{14,10},{1,5},{3,7},... | collective-permute-start | bytes 196616 | tf_op jit(solution)/shard_map/ppermute | solution.py:29
  7.7 12.4 %collective-permute-start = (bf16[4,128,128]{2,1,0:T(8,128)(2,1)S(1)}, bf16[4,128,128]{2,1,0:T(8,128)(2,1)S(1)}, u32[]{:S(2)}, u32[]{:S(2)}) collective-permute-start(bf16[4,128,128]{2,1,0:T(8,128)(2,1)S(1)} %first_level.1), channel_id=1, source_target_pairs={{0,2},{2,0},{4,6},{6,4},{8,10},{10,8},{12,14},{14,12},{1,3},{3,1},... | collective-permute-start | bytes 393224 | tf_op jit(solution)/shard_map/ppermute | solution.py:29
  9.6 5.8 %collective-permute-start.1 = (bf16[4,128,128]{2,1,0:T(8,128)(2,1)S(1)}, bf16[4,128,128]{2,1,0:T(8,128)(2,1)S(1)}, u32[]{:S(2)}, u32[]{:S(2)}) collective-permute-start(bf16[4,128,128]{2,1,0:T(8,128)(2,1)S(1)} %get-tuple-element.29), channel_id=1, source_target_pairs={{0,4},{2,6},{4,0},{6,2},{8,12},{10,14},{12,8},{14,10},{1,5},{3,7},... | collective-permute-start | bytes 393224 | tf_op jit(solution)/shard_map/ppermute | solution.py:29
  11.4 8.6 %collective-permute-start.7 = (bf16[2,128,128]{2,1,0:T(8,128)(2,1)S(1)}, bf16[2,128,128]{2,1,0:T(8,128)(2,1)S(1)}, u32[]{:S(2)}, u32[]{:S(2)}) collective-permute-start(bf16[2,128,128]{2,1,0:T(8,128)(2,1)S(1)} %quad_sum.1), channel_id=1, source_target_pairs={{0,8},{2,10},{4,12},{6,14},{8,2},{10,0},{12,6},{14,4},{1,9},{3,11}... | collective-permute-start | bytes 196616 | tf_op jit(solution)/shard_map/ppermute | solution.py:37
  14.1 6.1 %collective-permute-start.6 = (bf16[2,128,128]{2,1,0:T(8,128)(2,1)S(1)}, bf16[2,128,128]{2,1,0:T(8,128)(2,1)S(1)}, u32[]{:S(2)}, u32[]{:S(2)}) collective-permute-start(bf16[2,128,128]{2,1,0:T(8,128)(2,1)S(1)} %quad_sum.1), channel_id=1, source_target_pairs={{0,10},{2,8},{4,14},{6,12},{8,0},{10,2},{12,4},{14,6},{1,11},{3,9}... | collective-permute-start | bytes 196616 | tf_op jit(solution)/shard_map/ppermute | solution.py:37
  15.4 5.2 %collective-permute-start.2 = (bf16[4,128,128]{2,1,0:T(8,128)(2,1)S(1)}, bf16[4,128,128]{2,1,0:T(8,128)(2,1)S(1)}, u32[]{:S(2)}, u32[]{:S(2)}) collective-permute-start(bf16[4,128,128]{2,1,0:T(8,128)(2,1)S(1)} %collective-permute-done.1.refs_11_), channel_id=1, source_target_pairs={{0,2},{2,0},{4,6},{6,4},{8,10},{10,8},{12,14},{14,12},{1,3},{3,1},... | collective-permute-start | bytes 393224 | tf_op jit(solution)/shard_map/ppermute | solution.py:29

commit v11 on v10

--- a/solution.py
+++ b/solution.py
@@ -285,8 +285,8 @@
         value = v_ref[:, first * width : (first + GROUP) * width]
         key = k_ref[:, first * width : (first + GROUP) * width]
         gk_buf[first // GROUP] = (near_k + nt(value, low)).astype(LOW)
+        send(0, first, gk_buf, gk_hbm)
         gv_buf[first // GROUP] = (near_v + nn(key, low)).astype(LOW)
-        send(0, first, gk_buf, gk_hbm)
         send(1, first, gv_buf, gv_hbm)
     pltpu.make_async_copy(gq_buf, gq_hbm, gq_sem).wait()
     for copy in copies:

time: 22.1 us -> 22.1 us (level)
  no operation moved by 1% of the time
where the time goes in v11:
time: 22.1 us; the launch traced here: 22 us
  starting transfers between devices  13.9 us (63%)
  Pallas kernels  6.5 us (29%)
  waiting for transfers between devices  0.86 us (4%)
  between operations  0.72 us (3%)
    ppermute x6, starting transfers between devices, flip(): return lax.ppermute(block, AXES, [(i, i ^ mask) for i in range(size)])  9.85 us
    ppermute x2, starting transfers between devices, swap_halves(): return lax.ppermute(block, AXES, routes)  4.02 us
    pallas_call x5, Pallas kernels, call(): pl.pallas_call(kernel, out_shape=outs, in_specs=[IN_VMEM] * len(operands)...  3.51 us
    pallas_call x1, Pallas kernels, on_device(): pl.pallas_call(functools.partial(top_kernel, bits, scales), out_shape=[pl...  1.59 us
    pallas_call x1, Pallas kernels, on_device(): pl.pallas_call(functools.partial(far_kernel, bits, scales), out_shape=(ou...  1.4 us
    ppermute x6, waiting for transfers between devices, flip(): return lax.ppermute(block, AXES, [(i, i ^ mask) for i in range(size)])  0.57 us
  transfers between devices with their start and end apart: 8, of which 5 were waited for; matrix products, arithmetic and copies ran while one was open for 0% of the time, Pallas kernels for 16%

profile of v11, /device:TPU:0, one launch (start us, length us, event | category | flops | bytes accessed | tf_op | source)
XLA Modules:
  0.0 22.0 jit_solution(1492246559367325765)
XLA Ops:
  0.6 1.6 %top_states.1 = (bf16[4,128,512]{2,1,0:T(8,128)(2,1)S(1)}, bf16[2,128,128]{2,1,0:T(8,128)(2,1)S(1)}, bf16[2,128,128]{2,1,0:T(8,128)(2,1)S(1)}) custom-call(bf16[512,512]{1,0:T(8,128)(2,1)} %refs_0_.2, bf16[512,512]{1,0:T(8,128)(2,1)} %refs_0_.3, bf16[512,512]{1,0:T(8,128)(2,1)} %refs_1_.3, bf16[512,512]{1,0:T(8,128)(2,1)} %refs_2_.3, f32[4,8,512]{2,1,0:T(8,128)} %refs_3_.3), custom_call_target="tpu_custom_call" | custom-call | flops 33554432000 | tf_op jit(solution)/shard_map/top_states/pallas_call | solution.py:333
  2.2 0.0 copy-start
  2.2 0.0 copy-start.1
  2.3 0.0 copy-start.2
  2.3 0.0 copy-start.3
  2.3 0.0 copy-start.4
  2.3 4.0 %collective-permute-start.5 = (bf16[2,128,128]{2,1,0:T(8,128)(2,1)S(1)}, bf16[2,128,128]{2,1,0:T(8,128)(2,1)S(1)}, u32[]{:S(2)}, u32[]{:S(2)}) collective-permute-start(bf16[2,128,128]{2,1,0:T(8,128)(2,1)S(1)} %get-tuple-element.31.source), channel_id=1, source_target_pairs={{0,6},{2,4},{4,2},{6,0},{8,14},{10,12},{12,10},{14,8},{1,7},{3,5},... | collective-permute-start | bytes 196616 | tf_op jit(solution)/shard_map/ppermute | solution.py:29
  6.3 0.5 %collective-permute-start.3 = (bf16[2,128,128]{2,1,0:T(8,128)(2,1)S(1)}, bf16[2,128,128]{2,1,0:T(8,128)(2,1)S(1)}, u32[]{:S(2)}, u32[]{:S(2)}) collective-permute-start(bf16[2,128,128]{2,1,0:T(8,128)(2,1)S(1)} %x_part.1), channel_id=1, source_target_pairs={{0,2},{2,0},{4,6},{6,4},{8,10},{10,8},{12,14},{14,12},{1,3},{3,1},... | collective-permute-start | bytes 196616 | tf_op jit(solution)/shard_map/ppermute | solution.py:29
  6.9 0.1 collective-permute-start.4
  7.0 0.0 copy-done
  7.0 0.0 copy-done.1
  7.0 0.0 copy-done.2
  7.0 0.0 copy-done.3
  7.0 0.0 copy-done.4
  7.0 0.7 %low_states.1 = (bf16[4,128,512]{2,1,0:T(8,128)(2,1)S(1)}, bf16[4,128,512]{2,1,0:T(8,128)(2,1)S(1)}, bf16[4,128,128]{2,1,0:T(8,128)(2,1)S(1)}, bf16[4,128,128]{2,1,0:T(8,128)(2,1)S(1)}) custom-call(bf16[512,512]{1,0:T(8,128)(2,1)S(1)} %copy-done, bf16[512,512]{1,0:T(8,128)(2,1)S(1)} %copy-done.1, bf16[512,512]{1,0:T(8,128)(2,1)S(1)} %copy-done.2, ...), custom_call_target="tpu_custom_call" | custom-call | flops 33554432000 | tf_op jit(solution)/shard_map/low_states/pallas_call | solution.py:307
  7.7 1.9 %collective-permute-start = (bf16[4,128,128]{2,1,0:T(8,128)(2,1)S(1)}, bf16[4,128,128]{2,1,0:T(8,128)(2,1)S(1)}, u32[]{:S(2)}, u32[]{:S(2)}) collective-permute-start(bf16[4,128,128]{2,1,0:T(8,128)(2,1)S(1)} %first_level.1), channel_id=1, source_target_pairs={{0,2},{2,0},{4,6},{6,4},{8,10},{10,8},{12,14},{14,12},{1,3},{3,1},... | collective-permute-start | bytes 393224 | tf_op jit(solution)/shard_map/ppermute | solution.py:29
  9.6 1.6 %collective-permute-start.1 = (bf16[4,128,128]{2,1,0:T(8,128)(2,1)S(1)}, bf16[4,128,128]{2,1,0:T(8,128)(2,1)S(1)}, u32[]{:S(2)}, u32[]{:S(2)}) collective-permute-start(bf16[4,128,128]{2,1,0:T(8,128)(2,1)S(1)} %get-tuple-element.29), channel_id=1, source_target_pairs={{0,4},{2,6},{4,0},{6,2},{8,12},{10,14},{12,8},{14,10},{1,5},{3,7},... | collective-permute-start | bytes 393224 | tf_op jit(solution)/shard_map/ppermute | solution.py:29
  11.2 0.1 collective-permute-done.3.refs_1_
  11.3 0.1 collective-permute-done.4.refs_2_
  11.4 0.0 collective-permute-done.5.refs_3_
  11.4 2.6 %collective-permute-start.7 = (bf16[2,128,128]{2,1,0:T(8,128)(2,1)S(1)}, bf16[2,128,128]{2,1,0:T(8,128)(2,1)S(1)}, u32[]{:S(2)}, u32[]{:S(2)}) collective-permute-start(bf16[2,128,128]{2,1,0:T(8,128)(2,1)S(1)} %quad_sum.1), channel_id=1, source_target_pairs={{0,8},{2,10},{4,12},{6,14},{8,2},{10,0},{12,6},{14,4},{1,9},{3,11}... | collective-permute-start | bytes 196616 | tf_op jit(solution)/shard_map/ppermute | solution.py:37
  14.1 1.4 %collective-permute-start.6 = (bf16[2,128,128]{2,1,0:T(8,128)(2,1)S(1)}, bf16[2,128,128]{2,1,0:T(8,128)(2,1)S(1)}, u32[]{:S(2)}, u32[]{:S(2)}) collective-permute-start(bf16[2,128,128]{2,1,0:T(8,128)(2,1)S(1)} %quad_sum.1), channel_id=1, source_target_pairs={{0,10},{2,8},{4,14},{6,12},{8,0},{10,2},{12,4},{14,6},{1,11},{3,9}... | collective-permute-start | bytes 196616 | tf_op jit(solution)/shard_map/ppermute | solution.py:37
  15.4 0.0 collective-permute-done.1.refs_11_
  15.4 1.7 %collective-permute-start.2 = (bf16[4,128,128]{2,1,0:T(8,128)(2,1)S(1)}, bf16[4,128,128]{2,1,0:T(8,128)(2,1)S(1)}, u32[]{:S(2)}, u32[]{:S(2)}) collective-permute-start(bf16[4,128,128]{2,1,0:T(8,128)(2,1)S(1)} %collective-permute-done.1.refs_11_), channel_id=1, source_target_pairs={{0,2},{2,0},{4,6},{6,4},{8,10},{10,8},{12,14},{14,12},{1,3},{3,1},... | collective-permute-start | bytes 393224 | tf_op jit(solution)/shard_map/ppermute | solution.py:29
  17.2 2.7 %near.1 = (f32[4,128,512]{2,1,0:T(8,128)S(1)}, f32[4,8,512]{2,1,0:T(8,128)S(1)}, f32[4,512,128]{2,1,0:T(8,128)S(1)}, f32[4,512,128]{2,1,0:T(8,128)S(1)}, bf16[512,512]{1,0:T(8,128)(2,1)S(1)}) custom-call(bf16[512,512]{1,0:T(8,128)(2,1)S(1)} %copy-done, bf16[512,512]{1,0:T(8,128)(2,1)S(1)} %copy-done.1, bf16[512,512]{1,0:T(8,128)(2,1)S(1)} %copy-done.2, ...), custom_call_target="tpu_custom_call" | custom-call | flops 33554432000 | tf_op jit(solution)/shard_map/near/pallas_call | solution.py:307
  19.9 0.1 collective-permute-done.7.refs_14_
  20.0 0.2 collective-permute-done.6.refs_13_
  20.2 0.0 collective-permute-done.refs_10_
  20.2 0.4 %collective-permute-done.2.refs_12_ = bf16[4,128,128]{2,1,0:T(8,128)(2,1)S(1)} collective-permute-done((bf16[4,128,128]{2,1,0:T(8,128)(2,1)S(1)}, bf16[4,128,128]{2,1,0:T(8,128)(2,1)S(1)}, u32[]{:S(2)}, u32[]{:S(2)}) %collective-permute-start.2) | collective-permute-done | bytes 131104 | tf_op jit(solution)/shard_map/ppermute | solution.py:29
  20.6 1.4 %far.1 = (bf16[512,512]{1,0:T(8,128)(2,1)}, bf16[512,512]{1,0:T(8,128)(2,1)}, bf16[512,512]{1,0:T(8,128)(2,1)}, f32[4,8,512]{2,1,0:T(8,128)}, f32[4,128,512]{2,1,0:T(8,128)S(1)}) custom-call(bf16[512,512]{1,0:T(8,128)(2,1)S(1)} %copy-done.1, bf16[512,512]{1,0:T(8,128)(2,1)S(1)} %copy-done.2, ...), custom_call_target="tpu_custom_call", output_to_operand_aliasing={{4}: (5, {})} | custom-call | flops 33554432000 | tf_op jit(solution)/shard_map/far/pallas_call | solution.py:380
  (3 shorter events, 0.1 us)
Async XLA Ops:
  2.2 4.7 %copy-start = (bf16[512,512]{1,0:T(8,128)(2,1)S(1)}, bf16[512,512]{1,0:T(8,128)(2,1)}, u32[]{:S(2)}) copy-start(bf16[512,512]{1,0:T(8,128)(2,1)} %refs_0_.2) | copy-start | bytes 1572868
  2.2 4.7 %copy-start.1 = (bf16[512,512]{1,0:T(8,128)(2,1)S(1)}, bf16[512,512]{1,0:T(8,128)(2,1)}, u32[]{:S(2)}) copy-start(bf16[512,512]{1,0:T(8,128)(2,1)} %refs_0_.3) | copy-start | bytes 1572868
  2.3 4.7 %copy-start.2 = (bf16[512,512]{1,0:T(8,128)(2,1)S(1)}, bf16[512,512]{1,0:T(8,128)(2,1)}, u32[]{:S(2)}) copy-start(bf16[512,512]{1,0:T(8,128)(2,1)} %refs_1_.3) | copy-start | bytes 1572868
  2.3 4.7 %copy-start.3 = (bf16[512,512]{1,0:T(8,128)(2,1)S(1)}, bf16[512,512]{1,0:T(8,128)(2,1)}, u32[]{:S(2)}) copy-start(bf16[512,512]{1,0:T(8,128)(2,1)} %refs_2_.3) | copy-start | bytes 1572868
  2.3 4.7 %copy-start.4 = (f32[4,8,512]{2,1,0:T(8,128)S(1)}, f32[4,8,512]{2,1,0:T(8,128)}, u32[]{:S(2)}) copy-start(f32[4,8,512]{2,1,0:T(8,128)} %refs_3_.3) | copy-start | bytes 196612
  2.3 9.1 %collective-permute-start.5 = (bf16[2,128,128]{2,1,0:T(8,128)(2,1)S(1)}, bf16[2,128,128]{2,1,0:T(8,128)(2,1)S(1)}, u32[]{:S(2)}, u32[]{:S(2)}) collective-permute-start(bf16[2,128,128]{2,1,0:T(8,128)(2,1)S(1)} %get-tuple-element.31.source), channel_id=1, source_target_pairs={{0,6},{2,4},{4,2},{6,0},{8,14},{10,12},{12,10},{14,8},{1,7},{3,5},... | collective-permute-start | bytes 196616 | tf_op jit(solution)/shard_map/ppermute | solution.py:29
  6.3 5.0 %collective-permute-start.3 = (bf16[2,128,128]{2,1,0:T(8,128)(2,1)S(1)}, bf16[2,128,128]{2,1,0:T(8,128)(2,1)S(1)}, u32[]{:S(2)}, u32[]{:S(2)}) collective-permute-start(bf16[2,128,128]{2,1,0:T(8,128)(2,1)S(1)} %x_part.1), channel_id=1, source_target_pairs={{0,2},{2,0},{4,6},{6,4},{8,10},{10,8},{12,14},{14,12},{1,3},{3,1},... | collective-permute-start | bytes 196616 | tf_op jit(solution)/shard_map/ppermute | solution.py:29
  6.9 4.5 %collective-permute-start.4 = (bf16[2,128,128]{2,1,0:T(8,128)(2,1)S(1)}, bf16[2,128,128]{2,1,0:T(8,128)(2,1)S(1)}, u32[]{:S(2)}, u32[]{:S(2)}) collective-permute-start(bf16[2,128,128]{2,1,0:T(8,128)(2,1)S(1)} %get-tuple-element.30.refs_0_), channel_id=1, source_target_pairs={{0,4},{2,6},{4,0},{6,2},{8,12},{10,14},{12,8},{14,10},{1,5},{3,7},... | collective-permute-start | bytes 196616 | tf_op jit(solution)/shard_map/ppermute | solution.py:29
  7.7 12.4 %collective-permute-start = (bf16[4,128,128]{2,1,0:T(8,128)(2,1)S(1)}, bf16[4,128,128]{2,1,0:T(8,128)(2,1)S(1)}, u32[]{:S(2)}, u32[]{:S(2)}) collective-permute-start(bf16[4,128,128]{2,1,0:T(8,128)(2,1)S(1)} %first_level.1), channel_id=1, source_target_pairs={{0,2},{2,0},{4,6},{6,4},{8,10},{10,8},{12,14},{14,12},{1,3},{3,1},... | collective-permute-start | bytes 393224 | tf_op jit(solution)/shard_map/ppermute | solution.py:29
  9.6 5.8 %collective-permute-start.1 = (bf16[4,128,128]{2,1,0:T(8,128)(2,1)S(1)}, bf16[4,128,128]{2,1,0:T(8,128)(2,1)S(1)}, u32[]{:S(2)}, u32[]{:S(2)}) collective-permute-start(bf16[4,128,128]{2,1,0:T(8,128)(2,1)S(1)} %get-tuple-element.29), channel_id=1, source_target_pairs={{0,4},{2,6},{4,0},{6,2},{8,12},{10,14},{12,8},{14,10},{1,5},{3,7},... | collective-permute-start | bytes 393224 | tf_op jit(solution)/shard_map/ppermute | solution.py:29
  11.4 8.6 %collective-permute-start.7 = (bf16[2,128,128]{2,1,0:T(8,128)(2,1)S(1)}, bf16[2,128,128]{2,1,0:T(8,128)(2,1)S(1)}, u32[]{:S(2)}, u32[]{:S(2)}) collective-permute-start(bf16[2,128,128]{2,1,0:T(8,128)(2,1)S(1)} %quad_sum.1), channel_id=1, source_target_pairs={{0,8},{2,10},{4,12},{6,14},{8,2},{10,0},{12,6},{14,4},{1,9},{3,11}... | collective-permute-start | bytes 196616 | tf_op jit(solution)/shard_map/ppermute | solution.py:37
  14.1 6.1 %collective-permute-start.6 = (bf16[2,128,128]{2,1,0:T(8,128)(2,1)S(1)}, bf16[2,128,128]{2,1,0:T(8,128)(2,1)S(1)}, u32[]{:S(2)}, u32[]{:S(2)}) collective-permute-start(bf16[2,128,128]{2,1,0:T(8,128)(2,1)S(1)} %quad_sum.1), channel_id=1, source_target_pairs={{0,10},{2,8},{4,14},{6,12},{8,0},{10,2},{12,4},{14,6},{1,11},{3,9}... | collective-permute-start | bytes 196616 | tf_op jit(solution)/shard_map/ppermute | solution.py:37
  15.4 5.2 %collective-permute-start.2 = (bf16[4,128,128]{2,1,0:T(8,128)(2,1)S(1)}, bf16[4,128,128]{2,1,0:T(8,128)(2,1)S(1)}, u32[]{:S(2)}, u32[]{:S(2)}) collective-permute-start(bf16[4,128,128]{2,1,0:T(8,128)(2,1)S(1)} %collective-permute-done.1.refs_11_), channel_id=1, source_target_pairs={{0,2},{2,0},{4,6},{6,4},{8,10},{10,8},{12,14},{14,12},{1,3},{3,1},... | collective-permute-start | bytes 393224 | tf_op jit(solution)/shard_map/ppermute | solution.py:29

commit v12 on v11

--- a/solution.py
+++ b/solution.py
@@ -74,8 +74,9 @@
             copies.append(pltpu.make_async_copy(level_row, w_buf.at[index], sems.at[2, index]))
         for copy in copies:
             copy.start()
-        for copy in copies:
-            copy.wait()
+        copies[0].wait()
+        if upper:
+            copies[2].wait()
         held = []
         for first in range(0, heads, GROUP):
             lefts = []
@@ -86,6 +87,8 @@
                 if upper:
                     turned = (w_buf[index, h] * turned.astype(jnp.float32)).astype(LOW)
                 lefts.append(turned)
+            if first == 0:
+                copies[1].wait()
             columns = slice(first * width, (first + GROUP) * width)
             product = nn(jnp.concatenate(lefts, 0), right_buf[index, :, columns])
             for i in range(GROUP):

time: 22.1 us -> 22.1 us (level)
  no operation moved by 1% of the time
where the time goes in v12:
time: 22.1 us; the launch traced here: 21.9 us
  starting transfers between devices  13.9 us (63%)
  Pallas kernels  6.47 us (29%)
  waiting for transfers between devices  0.83 us (4%)
  between operations  0.72 us (3%)
    ppermute x6, starting transfers between devices, flip(): return lax.ppermute(block, AXES, [(i, i ^ mask) for i in range(size)])  9.87 us
    ppermute x2, starting transfers between devices, swap_halves(): return lax.ppermute(block, AXES, routes)  4.02 us
    pallas_call x5, Pallas kernels, call(): pl.pallas_call(kernel, out_shape=outs, in_specs=[IN_VMEM] * len(operands)...  3.51 us
    pallas_call x1, Pallas kernels, on_device(): pl.pallas_call(functools.partial(top_kernel, bits, scales), out_shape=[pl...  1.57 us
    pallas_call x1, Pallas kernels, on_device(): pl.pallas_call(functools.partial(far_kernel, bits, scales), out_shape=(ou...  1.39 us
    ppermute x6, waiting for transfers between devices, flip(): return lax.ppermute(block, AXES, [(i, i ^ mask) for i in range(size)])  0.56 us
  transfers between devices with their start and end apart: 8, of which 5 were waited for; matrix products, arithmetic and copies ran while one was open for 0% of the time, Pallas kernels for 16%

profile of v12, /device:TPU:0, one launch (start us, length us, event | category | flops | bytes accessed | tf_op | source)
XLA Modules:
  0.0 21.9 jit_solution(12066703603588015538)
XLA Ops:
  0.6 1.6 %top_states.1 = (bf16[4,128,512]{2,1,0:T(8,128)(2,1)S(1)}, bf16[2,128,128]{2,1,0:T(8,128)(2,1)S(1)}, bf16[2,128,128]{2,1,0:T(8,128)(2,1)S(1)}) custom-call(bf16[512,512]{1,0:T(8,128)(2,1)} %refs_0_.2, bf16[512,512]{1,0:T(8,128)(2,1)} %refs_0_.3, bf16[512,512]{1,0:T(8,128)(2,1)} %refs_1_.3, bf16[512,512]{1,0:T(8,128)(2,1)} %refs_2_.3, f32[4,8,512]{2,1,0:T(8,128)} %refs_3_.3), custom_call_target="tpu_custom_call" | custom-call | flops 33554432000 | tf_op jit(solution)/shard_map/top_states/pallas_call | solution.py:336
  2.2 0.0 copy-start
  2.2 0.0 copy-start.1
  2.2 0.0 copy-start.2
  2.2 0.0 copy-start.3
  2.3 0.0 copy-start.4
  2.3 4.0 %collective-permute-start.5 = (bf16[2,128,128]{2,1,0:T(8,128)(2,1)S(1)}, bf16[2,128,128]{2,1,0:T(8,128)(2,1)S(1)}, u32[]{:S(2)}, u32[]{:S(2)}) collective-permute-start(bf16[2,128,128]{2,1,0:T(8,128)(2,1)S(1)} %get-tuple-element.31.source), channel_id=1, source_target_pairs={{0,6},{2,4},{4,2},{6,0},{8,14},{10,12},{12,10},{14,8},{1,7},{3,5},... | collective-permute-start | bytes 196616 | tf_op jit(solution)/shard_map/ppermute | solution.py:29
  6.3 0.5 %collective-permute-start.3 = (bf16[2,128,128]{2,1,0:T(8,128)(2,1)S(1)}, bf16[2,128,128]{2,1,0:T(8,128)(2,1)S(1)}, u32[]{:S(2)}, u32[]{:S(2)}) collective-permute-start(bf16[2,128,128]{2,1,0:T(8,128)(2,1)S(1)} %x_part.1), channel_id=1, source_target_pairs={{0,2},{2,0},{4,6},{6,4},{8,10},{10,8},{12,14},{14,12},{1,3},{3,1},... | collective-permute-start | bytes 196616 | tf_op jit(solution)/shard_map/ppermute | solution.py:29
  6.8 0.1 collective-permute-start.4
  6.9 0.0 copy-done
  6.9 0.0 copy-done.1
  6.9 0.0 copy-done.2
  6.9 0.0 copy-done.3
  7.0 0.0 copy-done.4
  7.0 0.7 %low_states.1 = (bf16[4,128,512]{2,1,0:T(8,128)(2,1)S(1)}, bf16[4,128,512]{2,1,0:T(8,128)(2,1)S(1)}, bf16[4,128,128]{2,1,0:T(8,128)(2,1)S(1)}, bf16[4,128,128]{2,1,0:T(8,128)(2,1)S(1)}) custom-call(bf16[512,512]{1,0:T(8,128)(2,1)S(1)} %copy-done, bf16[512,512]{1,0:T(8,128)(2,1)S(1)} %copy-done.1, bf16[512,512]{1,0:T(8,128)(2,1)S(1)} %copy-done.2, ...), custom_call_target="tpu_custom_call" | custom-call | flops 33554432000 | tf_op jit(solution)/shard_map/low_states/pallas_call | solution.py:310
  7.7 1.9 %collective-permute-start = (bf16[4,128,128]{2,1,0:T(8,128)(2,1)S(1)}, bf16[4,128,128]{2,1,0:T(8,128)(2,1)S(1)}, u32[]{:S(2)}, u32[]{:S(2)}) collective-permute-start(bf16[4,128,128]{2,1,0:T(8,128)(2,1)S(1)} %first_level.1), channel_id=1, source_target_pairs={{0,2},{2,0},{4,6},{6,4},{8,10},{10,8},{12,14},{14,12},{1,3},{3,1},... | collective-permute-start | bytes 393224 | tf_op jit(solution)/shard_map/ppermute | solution.py:29
  9.6 1.6 %collective-permute-start.1 = (bf16[4,128,128]{2,1,0:T(8,128)(2,1)S(1)}, bf16[4,128,128]{2,1,0:T(8,128)(2,1)S(1)}, u32[]{:S(2)}, u32[]{:S(2)}) collective-permute-start(bf16[4,128,128]{2,1,0:T(8,128)(2,1)S(1)} %get-tuple-element.29), channel_id=1, source_target_pairs={{0,4},{2,6},{4,0},{6,2},{8,12},{10,14},{12,8},{14,10},{1,5},{3,7},... | collective-permute-start | bytes 393224 | tf_op jit(solution)/shard_map/ppermute | solution.py:29
  11.2 0.1 collective-permute-done.3.refs_1_
  11.3 0.1 collective-permute-done.4.refs_2_
  11.3 0.0 collective-permute-done.5.refs_3_
  11.4 2.7 %collective-permute-start.7 = (bf16[2,128,128]{2,1,0:T(8,128)(2,1)S(1)}, bf16[2,128,128]{2,1,0:T(8,128)(2,1)S(1)}, u32[]{:S(2)}, u32[]{:S(2)}) collective-permute-start(bf16[2,128,128]{2,1,0:T(8,128)(2,1)S(1)} %quad_sum.1), channel_id=1, source_target_pairs={{0,8},{2,10},{4,12},{6,14},{8,2},{10,0},{12,6},{14,4},{1,9},{3,11}... | collective-permute-start | bytes 196616 | tf_op jit(solution)/shard_map/ppermute | solution.py:37
  14.0 1.4 %collective-permute-start.6 = (bf16[2,128,128]{2,1,0:T(8,128)(2,1)S(1)}, bf16[2,128,128]{2,1,0:T(8,128)(2,1)S(1)}, u32[]{:S(2)}, u32[]{:S(2)}) collective-permute-start(bf16[2,128,128]{2,1,0:T(8,128)(2,1)S(1)} %quad_sum.1), channel_id=1, source_target_pairs={{0,10},{2,8},{4,14},{6,12},{8,0},{10,2},{12,4},{14,6},{1,11},{3,9}... | collective-permute-start | bytes 196616 | tf_op jit(solution)/shard_map/ppermute | solution.py:37
  15.4 0.0 collective-permute-done.1.refs_11_
  15.4 1.7 %collective-permute-start.2 = (bf16[4,128,128]{2,1,0:T(8,128)(2,1)S(1)}, bf16[4,128,128]{2,1,0:T(8,128)(2,1)S(1)}, u32[]{:S(2)}, u32[]{:S(2)}) collective-permute-start(bf16[4,128,128]{2,1,0:T(8,128)(2,1)S(1)} %collective-permute-done.1.refs_11_), channel_id=1, source_target_pairs={{0,2},{2,0},{4,6},{6,4},{8,10},{10,8},{12,14},{14,12},{1,3},{3,1},... | collective-permute-start | bytes 393224 | tf_op jit(solution)/shard_map/ppermute | solution.py:29
  17.1 2.7 %near.1 = (f32[4,128,512]{2,1,0:T(8,128)S(1)}, f32[4,8,512]{2,1,0:T(8,128)S(1)}, f32[4,512,128]{2,1,0:T(8,128)S(1)}, f32[4,512,128]{2,1,0:T(8,128)S(1)}, bf16[512,512]{1,0:T(8,128)(2,1)S(1)}) custom-call(bf16[512,512]{1,0:T(8,128)(2,1)S(1)} %copy-done, bf16[512,512]{1,0:T(8,128)(2,1)S(1)} %copy-done.1, bf16[512,512]{1,0:T(8,128)(2,1)S(1)} %copy-done.2, ...), custom_call_target="tpu_custom_call" | custom-call | flops 33554432000 | tf_op jit(solution)/shard_map/near/pallas_call | solution.py:310
  19.9 0.1 collective-permute-done.7.refs_14_
  20.0 0.2 collective-permute-done.6.refs_13_
  20.1 0.0 collective-permute-done.refs_10_
  20.1 0.4 %collective-permute-done.2.refs_12_ = bf16[4,128,128]{2,1,0:T(8,128)(2,1)S(1)} collective-permute-done((bf16[4,128,128]{2,1,0:T(8,128)(2,1)S(1)}, bf16[4,128,128]{2,1,0:T(8,128)(2,1)S(1)}, u32[]{:S(2)}, u32[]{:S(2)}) %collective-permute-start.2) | collective-permute-done | bytes 131104 | tf_op jit(solution)/shard_map/ppermute | solution.py:29
  20.6 1.4 %far.1 = (bf16[512,512]{1,0:T(8,128)(2,1)}, bf16[512,512]{1,0:T(8,128)(2,1)}, bf16[512,512]{1,0:T(8,128)(2,1)}, f32[4,8,512]{2,1,0:T(8,128)}, f32[4,128,512]{2,1,0:T(8,128)S(1)}) custom-call(bf16[512,512]{1,0:T(8,128)(2,1)S(1)} %copy-done.1, bf16[512,512]{1,0:T(8,128)(2,1)S(1)} %copy-done.2, ...), custom_call_target="tpu_custom_call", output_to_operand_aliasing={{4}: (5, {})} | custom-call | flops 33554432000 | tf_op jit(solution)/shard_map/far/pallas_call | solution.py:383
  (3 shorter events, 0.1 us)
Async XLA Ops:
  2.2 4.7 %copy-start = (bf16[512,512]{1,0:T(8,128)(2,1)S(1)}, bf16[512,512]{1,0:T(8,128)(2,1)}, u32[]{:S(2)}) copy-start(bf16[512,512]{1,0:T(8,128)(2,1)} %refs_0_.2) | copy-start | bytes 1572868
  2.2 4.7 %copy-start.1 = (bf16[512,512]{1,0:T(8,128)(2,1)S(1)}, bf16[512,512]{1,0:T(8,128)(2,1)}, u32[]{:S(2)}) copy-start(bf16[512,512]{1,0:T(8,128)(2,1)} %refs_0_.3) | copy-start | bytes 1572868
  2.2 4.7 %copy-start.2 = (bf16[512,512]{1,0:T(8,128)(2,1)S(1)}, bf16[512,512]{1,0:T(8,128)(2,1)}, u32[]{:S(2)}) copy-start(bf16[512,512]{1,0:T(8,128)(2,1)} %refs_1_.3) | copy-start | bytes 1572868
  2.2 4.7 %copy-start.3 = (bf16[512,512]{1,0:T(8,128)(2,1)S(1)}, bf16[512,512]{1,0:T(8,128)(2,1)}, u32[]{:S(2)}) copy-start(bf16[512,512]{1,0:T(8,128)(2,1)} %refs_2_.3) | copy-start | bytes 1572868
  2.3 4.7 %copy-start.4 = (f32[4,8,512]{2,1,0:T(8,128)S(1)}, f32[4,8,512]{2,1,0:T(8,128)}, u32[]{:S(2)}) copy-start(f32[4,8,512]{2,1,0:T(8,128)} %refs_3_.3) | copy-start | bytes 196612
  2.3 9.1 %collective-permute-start.5 = (bf16[2,128,128]{2,1,0:T(8,128)(2,1)S(1)}, bf16[2,128,128]{2,1,0:T(8,128)(2,1)S(1)}, u32[]{:S(2)}, u32[]{:S(2)}) collective-permute-start(bf16[2,128,128]{2,1,0:T(8,128)(2,1)S(1)} %get-tuple-element.31.source), channel_id=1, source_target_pairs={{0,6},{2,4},{4,2},{6,0},{8,14},{10,12},{12,10},{14,8},{1,7},{3,5},... | collective-permute-start | bytes 196616 | tf_op jit(solution)/shard_map/ppermute | solution.py:29
  6.3 5.0 %collective-permute-start.3 = (bf16[2,128,128]{2,1,0:T(8,128)(2,1)S(1)}, bf16[2,128,128]{2,1,0:T(8,128)(2,1)S(1)}, u32[]{:S(2)}, u32[]{:S(2)}) collective-permute-start(bf16[2,128,128]{2,1,0:T(8,128)(2,1)S(1)} %x_part.1), channel_id=1, source_target_pairs={{0,2},{2,0},{4,6},{6,4},{8,10},{10,8},{12,14},{14,12},{1,3},{3,1},... | collective-permute-start | bytes 196616 | tf_op jit(solution)/shard_map/ppermute | solution.py:29
  6.8 4.5 %collective-permute-start.4 = (bf16[2,128,128]{2,1,0:T(8,128)(2,1)S(1)}, bf16[2,128,128]{2,1,0:T(8,128)(2,1)S(1)}, u32[]{:S(2)}, u32[]{:S(2)}) collective-permute-start(bf16[2,128,128]{2,1,0:T(8,128)(2,1)S(1)} %get-tuple-element.30.refs_0_), channel_id=1, source_target_pairs={{0,4},{2,6},{4,0},{6,2},{8,12},{10,14},{12,8},{14,10},{1,5},{3,7},... | collective-permute-start | bytes 196616 | tf_op jit(solution)/shard_map/ppermute | solution.py:29
  7.7 12.4 %collective-permute-start = (bf16[4,128,128]{2,1,0:T(8,128)(2,1)S(1)}, bf16[4,128,128]{2,1,0:T(8,128)(2,1)S(1)}, u32[]{:S(2)}, u32[]{:S(2)}) collective-permute-start(bf16[4,128,128]{2,1,0:T(8,128)(2,1)S(1)} %first_level.1), channel_id=1, source_target_pairs={{0,2},{2,0},{4,6},{6,4},{8,10},{10,8},{12,14},{14,12},{1,3},{3,1},... | collective-permute-start | bytes 393224 | tf_op jit(solution)/shard_map/ppermute | solution.py:29
  9.6 5.8 %collective-permute-start.1 = (bf16[4,128,128]{2,1,0:T(8,128)(2,1)S(1)}, bf16[4,128,128]{2,1,0:T(8,128)(2,1)S(1)}, u32[]{:S(2)}, u32[]{:S(2)}) collective-permute-start(bf16[4,128,128]{2,1,0:T(8,128)(2,1)S(1)} %get-tuple-element.29), channel_id=1, source_target_pairs={{0,4},{2,6},{4,0},{6,2},{8,12},{10,14},{12,8},{14,10},{1,5},{3,7},... | collective-permute-start | bytes 393224 | tf_op jit(solution)/shard_map/ppermute | solution.py:29
  11.4 8.6 %collective-permute-start.7 = (bf16[2,128,128]{2,1,0:T(8,128)(2,1)S(1)}, bf16[2,128,128]{2,1,0:T(8,128)(2,1)S(1)}, u32[]{:S(2)}, u32[]{:S(2)}) collective-permute-start(bf16[2,128,128]{2,1,0:T(8,128)(2,1)S(1)} %quad_sum.1), channel_id=1, source_target_pairs={{0,8},{2,10},{4,12},{6,14},{8,2},{10,0},{12,6},{14,4},{1,9},{3,11}... | collective-permute-start | bytes 196616 | tf_op jit(solution)/shard_map/ppermute | solution.py:37
  14.0 6.1 %collective-permute-start.6 = (bf16[2,128,128]{2,1,0:T(8,128)(2,1)S(1)}, bf16[2,128,128]{2,1,0:T(8,128)(2,1)S(1)}, u32[]{:S(2)}, u32[]{:S(2)}) collective-permute-start(bf16[2,128,128]{2,1,0:T(8,128)(2,1)S(1)} %quad_sum.1), channel_id=1, source_target_pairs={{0,10},{2,8},{4,14},{6,12},{8,0},{10,2},{12,4},{14,6},{1,11},{3,9}... | collective-permute-start | bytes 196616 | tf_op jit(solution)/shard_map/ppermute | solution.py:37
  15.4 5.2 %collective-permute-start.2 = (bf16[4,128,128]{2,1,0:T(8,128)(2,1)S(1)}, bf16[4,128,128]{2,1,0:T(8,128)(2,1)S(1)}, u32[]{:S(2)}, u32[]{:S(2)}) collective-permute-start(bf16[4,128,128]{2,1,0:T(8,128)(2,1)S(1)} %collective-permute-done.1.refs_11_), channel_id=1, source_target_pairs={{0,2},{2,0},{4,6},{6,4},{8,10},{10,8},{12,14},{14,12},{1,3},{3,1},... | collective-permute-start | bytes 393224 | tf_op jit(solution)/shard_map/ppermute | solution.py:29
